TPU v7x, 512 devices: a whole 4x4x16 slice. The times are simulated.
512 devices in a mesh: seq: 128 (over y, z, core), head: 4 (over x).
Axes of the slice: x: 4, y: 4, z: 16, core: 2. Of those that a mesh axis runs over, the one named last changes fastest.
Arguments:
- queries: bfloat16 [16384, 4096], P('seq', 'head'), may hold values from -6 to 6
- key_states: bfloat16 [16384, 4096], P('seq', 'head'), may hold values from -6 to 6
- value_states: bfloat16 [16384, 4096], P('seq', 'head'), may hold values from -6 to 6
- cotangent: bfloat16 [16384, 4096], P(('seq', 'head')), may hold values from -6 to 6
Outputs:
- attended: bfloat16 [16384, 4096], P(('seq', 'head'))
- query_gradient: bfloat16 [16384, 4096], P('seq', 'head')
- key_gradient: bfloat16 [16384, 4096], P('seq', 'head')
- value_gradient: bfloat16 [16384, 4096], P('seq', 'head')
All inputs are finite; a program needn't handle non-finite values.
Results may differ from a plain program's by a relative error of at most 0.011.
Values may be sent and summed in bfloat16 or wider, within the bound.
No kernel may reach another device: no remote copies, remote signals or barrier semaphores. Data moves between devices by JAX's collectives and lax.ppermute only.
A program may use at most 64 MiB of HBM per device.

v0:
```python
import math

import jax
import jax.numpy as jnp
from jax import lax
from jax.sharding import PartitionSpec as P

HEAD_DIM = 128
LEVELS = 4


LOG_TWO = math.log(2.0)
MASKED = -1e30


def shifted(shard, axis, by):
    size = lax.axis_size(axis)
    pairs = [(i, i + by) for i in range(size) if 0 <= i + by < size]
    return lax.ppermute(shard, axis, pairs)


def pair_mean(values):
    row_count = values.shape[-2]
    grouped = values.astype(jnp.float32).reshape(
        values.shape[:-2] + (row_count // 2, 2, values.shape[-1])
    )
    return (0.5 * (grouped[..., 0, :] + grouped[..., 1, :])).astype(jnp.bfloat16)


def spread_rows(gradients):
    return jnp.repeat(0.5 * gradients, 2, axis=-2)


def span_bias(level_index, facing, block_index, blocks, block_rows):
    tier_rows = block_rows >> level_index
    distance = 2 ** (level_index - 1) + jnp.arange(block_rows // 2, dtype=jnp.int32) // tier_rows
    target = block_index + facing * distance
    valid = (target >= 0) & (target < blocks)
    return jnp.where(valid, level_index * LOG_TWO, MASKED).astype(jnp.float32)


def head_pass(query_part, key_part, value_part, key_bias, cotangent_part, score_scale):
    scores = (
        jnp.einsum("qe,ke->qk", query_part, key_part, preferred_element_type=jnp.float32)
        * score_scale
        + key_bias[None, :]
    )
    highest = jnp.max(scores, axis=1, keepdims=True)
    raised = jnp.exp(scores - highest)
    weights = raised / jnp.sum(raised, axis=1, keepdims=True)
    weights_low = weights.astype(jnp.bfloat16)
    attended = jnp.einsum(
        "qk,ke->qe", weights_low, value_part, preferred_element_type=jnp.float32
    ).astype(jnp.bfloat16)
    weight_grad = jnp.einsum(
        "qe,ke->qk", cotangent_part, value_part, preferred_element_type=jnp.float32
    )
    row_term = jnp.sum(weights * weight_grad, axis=1, keepdims=True)
    score_grad = (weights * (weight_grad - row_term) * score_scale).astype(jnp.bfloat16)
    query_grad = jnp.einsum(
        "qk,ke->qe", score_grad, key_part, preferred_element_type=jnp.float32
    ).astype(jnp.bfloat16)
    key_grad = jnp.einsum("qk,qe->ke", score_grad, query_part, preferred_element_type=jnp.float32)
    value_grad = jnp.einsum(
        "qk,qe->ke", weights_low, cotangent_part, preferred_element_type=jnp.float32
    )
    return (attended, query_grad, key_grad, value_grad)


def local(queries, key_states, value_states, cotangent):
    block_rows = queries.shape[0]
    feature_width = queries.shape[1]
    half_rows = block_rows // 2
    blocks = lax.axis_size("seq")
    block_index = lax.axis_index("seq")
    local_cotangent = lax.all_to_all(cotangent, "head", split_axis=1, concat_axis=0, tiled=True)
    stacked = jnp.stack([key_states, value_states])
    lower_spans = []
    upper_spans = []
    pyramid = [stacked]
    for level_index in range(1, LEVELS + 1):
        pyramid.append(pair_mean(pyramid[-1]))
    for level_index in range(1, LEVELS + 1):
        for facing in (-1, 1):
            pieces = []
            for distance in range(2 ** (level_index - 1), 2**level_index):
                pieces.append(shifted(pyramid[level_index], "seq", -facing * distance))
            target_list = lower_spans if facing < 0 else upper_spans
            target_list.append(jnp.concatenate(pieces, axis=1))
    key_set = jnp.concatenate([stacked] + lower_spans + upper_spans, axis=1)
    bias_parts = [jnp.zeros((block_rows,), jnp.float32)]
    for facing in (-1, 1):
        for level_index in range(1, LEVELS + 1):
            bias_parts.append(span_bias(level_index, facing, block_index, blocks, block_rows))
    key_bias = jnp.concatenate(bias_parts)
    score_scale = 1.0 / math.sqrt(HEAD_DIM)
    head_count = feature_width // HEAD_DIM
    out_columns = []
    query_columns = []
    key_columns = []
    value_columns = []
    for head_number in range(head_count):
        start_col = head_number * HEAD_DIM
        stop_col = start_col + HEAD_DIM
        results = head_pass(
            queries[:, start_col:stop_col],
            key_set[0, :, start_col:stop_col],
            key_set[1, :, start_col:stop_col],
            key_bias,
            local_cotangent[:, start_col:stop_col],
            score_scale,
        )
        out_columns.append(results[0])
        query_columns.append(results[1])
        key_columns.append(results[2])
        value_columns.append(results[3])
    local_attended = jnp.concatenate(out_columns, axis=1)
    query_gradient = jnp.concatenate(query_columns, axis=1)
    bounds = [0, block_rows] + [
        block_rows + half_rows * (number + 1) for number in range(2 * LEVELS)
    ]
    span_grads = []
    for span_number in range(2 * LEVELS + 1):
        low_row = bounds[span_number]
        high_row = bounds[span_number + 1]
        span_grads.append(
            jnp.stack(
                [
                    jnp.concatenate(
                        [grad_rows[low_row:high_row] for grad_rows in key_columns], axis=1
                    ),
                    jnp.concatenate(
                        [grad_rows[low_row:high_row] for grad_rows in value_columns], axis=1
                    ),
                ]
            )
        )
    own_grad = span_grads[0]
    lower_grads = span_grads[1 : LEVELS + 1]
    upper_grads = span_grads[LEVELS + 1 :]
    carried = None
    for level_index in range(LEVELS, 0, -1):
        tier_rows = block_rows >> level_index
        level_sum = jnp.zeros((2, tier_rows, feature_width), jnp.float32)
        for facing in (-1, 1):
            source = lower_grads if facing < 0 else upper_grads
            span_grad = source[level_index - 1]
            for distance in range(2 ** (level_index - 1), 2**level_index):
                first_row = (distance - 2 ** (level_index - 1)) * tier_rows
                part_grad = span_grad[:, first_row : first_row + tier_rows]
                level_sum = level_sum + shifted(
                    part_grad.astype(jnp.bfloat16), "seq", facing * distance
                ).astype(part_grad.dtype)
        carried = level_sum if carried is None else level_sum + spread_rows(carried)
    total_grad = own_grad + spread_rows(carried)
    attended = lax.all_to_all(local_attended, "head", split_axis=0, concat_axis=1, tiled=True)
    return (
        attended,
        query_gradient,
        total_grad[0].astype(jnp.bfloat16),
        total_grad[1].astype(jnp.bfloat16),
    )


def solution(mesh):
    placed = (P("seq", "head"), P("seq", "head"), P("seq", "head"), P(("seq", "head"), None))
    return jax.shard_map(
        local,
        mesh=mesh,
        in_specs=placed,
        out_specs=(P(("seq", "head"), None), P("seq", "head"), P("seq", "head"), P("seq", "head")),
        check_vma=False,
    )
```

profile of v0, /device:TPU:27, one launch (start us, length us, event | category | flops | bytes accessed | tf_op | source)
XLA Modules:
  0.0 552.1 jit_solution(11798761397661731781)
XLA Ops:
  4.4 15.7 %collective-permute-start.29 = (bf16[2,8,1024]{2,0,1:T(2,128)(2,1)}, bf16[2,8,1024]{2,0,1:T(2,128)(2,1)}, u32[]{:S(2)}, u32[]{:S(2)}) collective-permute-start(bf16[2,8,1024]{2,0,1:T(2,128)(2,1)} %fusion.81), channel_id=1, source_target_pairs={{60,0},{64,4},{68,8},{72,12},{76,16},{80,20},{84,24},{88,28},{92,3... | collective-permute-start | bytes 98312 | tf_op jit(solution)/shard_map/ppermute | solution.py:19
  22.1 11.1 %collective-permute-start.27 = (bf16[2,8,1024]{2,0,1:T(2,128)(2,1)}, bf16[2,8,1024]{2,0,1:T(2,128)(2,1)}, u32[]{:S(2)}, u32[]{:S(2)}) collective-permute-start(bf16[2,8,1024]{2,0,1:T(2,128)(2,1)} %fusion.81), channel_id=1, source_target_pairs={{52,0},{56,4},{60,8},{64,12},{68,16},{72,20},{76,24},{80,28},{84,3... | collective-permute-start | bytes 98312 | tf_op jit(solution)/shard_map/ppermute | solution.py:19
  33.9 4.3 all-to-all-start.1
  41.7 3.3 collective-permute-start
  48.6 7.3 %collective-permute-start.14 = (bf16[2,8,1024]{2,0,1:T(2,128)(2,1)}, bf16[2,8,1024]{2,0,1:T(2,128)(2,1)S(1)}, u32[]{:S(2)}, u32[]{:S(2)}) collective-permute-start(bf16[2,8,1024]{2,0,1:T(2,128)(2,1)} %fusion.81), channel_id=1, source_target_pairs={{0,60},{4,64},{8,68},{12,72},{16,76},{20,80},{24,84},{28,88},{32,9... | collective-permute-start | bytes 98312 | tf_op jit(solution)/shard_map/ppermute | solution.py:19
  58.8 7.2 %collective-permute-done.2 = bf16[2,32,1024]{2,0,1:T(2,128)(2,1)S(1)} collective-permute-done((bf16[2,32,1024]{2,0,1:T(2,128)(2,1)}, bf16[2,32,1024]{2,0,1:T(2,128)(2,1)S(1)}, u32[]{:S(2)}, u32[]{:S(2)}) %collective-permute-start.2) | collective-permute-done | bytes 131104 | tf_op jit(solution)/shard_map/ppermute | solution.py:19
  67.9 6.8 %collective-permute-done.3 = bf16[2,16,1024]{2,0,1:T(2,128)(2,1)S(1)} collective-permute-done((bf16[2,16,1024]{2,0,1:T(2,128)(2,1)S(1)}, bf16[2,16,1024]{2,0,1:T(2,128)(2,1)S(1)}, u32[]{:S(2)}, u32[]{:S(2)}) %collective-permute-start.3) | collective-permute-done | bytes 65568 | tf_op jit(solution)/shard_map/ppermute | solution.py:19
  74.7 2.4 collective-permute-start.4
  77.1 6.2 %collective-permute-done.4 = bf16[2,16,1024]{2,0,1:T(2,128)(2,1)S(1)} collective-permute-done((bf16[2,16,1024]{2,0,1:T(2,128)(2,1)S(1)}, bf16[2,16,1024]{2,0,1:T(2,128)(2,1)S(1)}, u32[]{:S(2)}, u32[]{:S(2)}) %collective-permute-start.4) | collective-permute-done | bytes 65568 | tf_op jit(solution)/shard_map/ppermute | solution.py:19
  83.3 3.0 collective-permute-start.5
  86.4 5.9 %collective-permute-done.5 = bf16[2,16,1024]{2,0,1:T(2,128)(2,1)S(1)} collective-permute-done((bf16[2,16,1024]{2,0,1:T(2,128)(2,1)S(1)}, bf16[2,16,1024]{2,0,1:T(2,128)(2,1)S(1)}, u32[]{:S(2)}, u32[]{:S(2)}) %collective-permute-start.5) | collective-permute-done | bytes 65568 | tf_op jit(solution)/shard_map/ppermute | solution.py:19
  92.3 7.6 %collective-permute-start.6 = (bf16[2,16,1024]{2,0,1:T(2,128)(2,1)S(1)}, bf16[2,16,1024]{2,0,1:T(2,128)(2,1)S(1)}, u32[]{:S(2)}, u32[]{:S(2)}) collective-permute-start(bf16[2,16,1024]{2,0,1:T(2,128)(2,1)S(1)} %fusion.189), channel_id=1, source_target_pairs={{0,28},{4,32},{8,36},{12,40},{16,44},{20,48},{24,52},{28,56},{32,6... | collective-permute-start | bytes 196616 | tf_op jit(solution)/shard_map/ppermute | solution.py:19
  100.0 5.6 %collective-permute-done.6 = bf16[2,16,1024]{2,0,1:T(2,128)(2,1)S(1)} collective-permute-done((bf16[2,16,1024]{2,0,1:T(2,128)(2,1)S(1)}, bf16[2,16,1024]{2,0,1:T(2,128)(2,1)S(1)}, u32[]{:S(2)}, u32[]{:S(2)}) %collective-permute-start.6) | collective-permute-done | bytes 65568 | tf_op jit(solution)/shard_map/ppermute | solution.py:19
  107.5 8.2 %collective-permute-done.7 = bf16[2,8,1024]{2,0,1:T(2,128)(2,1)S(1)} collective-permute-done((bf16[2,8,1024]{2,0,1:T(2,128)(2,1)}, bf16[2,8,1024]{2,0,1:T(2,128)(2,1)S(1)}, u32[]{:S(2)}, u32[]{:S(2)}) %collective-permute-start.7) | collective-permute-done | bytes 32800 | tf_op jit(solution)/shard_map/ppermute | solution.py:19
  115.6 3.3 collective-permute-start.8
  118.9 7.0 %collective-permute-done.8 = bf16[2,8,1024]{2,0,1:T(2,128)(2,1)S(1)} collective-permute-done((bf16[2,8,1024]{2,0,1:T(2,128)(2,1)}, bf16[2,8,1024]{2,0,1:T(2,128)(2,1)S(1)}, u32[]{:S(2)}, u32[]{:S(2)}) %collective-permute-start.8) | collective-permute-done | bytes 32800 | tf_op jit(solution)/shard_map/ppermute | solution.py:19
  125.9 3.7 collective-permute-start.9
  129.6 8.2 %collective-permute-done.9 = bf16[2,8,1024]{2,0,1:T(2,128)(2,1)S(1)} collective-permute-done((bf16[2,8,1024]{2,0,1:T(2,128)(2,1)}, bf16[2,8,1024]{2,0,1:T(2,128)(2,1)S(1)}, u32[]{:S(2)}, u32[]{:S(2)}) %collective-permute-start.9) | collective-permute-done | bytes 32800 | tf_op jit(solution)/shard_map/ppermute | solution.py:19
  137.8 4.2 collective-permute-start.10
  141.9 8.8 %collective-permute-done.10 = bf16[2,8,1024]{2,0,1:T(2,128)(2,1)S(1)} collective-permute-done((bf16[2,8,1024]{2,0,1:T(2,128)(2,1)}, bf16[2,8,1024]{2,0,1:T(2,128)(2,1)S(1)}, u32[]{:S(2)}, u32[]{:S(2)}) %collective-permute-start.10) | collective-permute-done | bytes 32800 | tf_op jit(solution)/shard_map/ppermute | solution.py:19
  150.7 2.5 collective-permute-start.11
  153.3 11.0 %collective-permute-done.11 = bf16[2,8,1024]{2,0,1:T(2,128)(2,1)S(1)} collective-permute-done((bf16[2,8,1024]{2,0,1:T(2,128)(2,1)}, bf16[2,8,1024]{2,0,1:T(2,128)(2,1)S(1)}, u32[]{:S(2)}, u32[]{:S(2)}) %collective-permute-start.11) | collective-permute-done | bytes 32800 | tf_op jit(solution)/shard_map/ppermute | solution.py:19
  164.3 3.5 collective-permute-start.12
  167.8 10.5 %collective-permute-done.12 = bf16[2,8,1024]{2,0,1:T(2,128)(2,1)S(1)} collective-permute-done((bf16[2,8,1024]{2,0,1:T(2,128)(2,1)}, bf16[2,8,1024]{2,0,1:T(2,128)(2,1)S(1)}, u32[]{:S(2)}, u32[]{:S(2)}) %collective-permute-start.12) | collective-permute-done | bytes 32800 | tf_op jit(solution)/shard_map/ppermute | solution.py:19
  178.3 2.7 collective-permute-start.13
  181.1 11.1 %collective-permute-done.13 = bf16[2,8,1024]{2,0,1:T(2,128)(2,1)S(1)} collective-permute-done((bf16[2,8,1024]{2,0,1:T(2,128)(2,1)}, bf16[2,8,1024]{2,0,1:T(2,128)(2,1)S(1)}, u32[]{:S(2)}, u32[]{:S(2)}) %collective-permute-start.13) | collective-permute-done | bytes 32800 | tf_op jit(solution)/shard_map/ppermute | solution.py:19
  192.1 9.9 %collective-permute-start.15 = (bf16[2,64,1024]{2,1,0:T(8,128)(2,1)}, bf16[2,64,1024]{2,1,0:T(8,128)(2,1)S(1)}, u32[]{:S(2)}, u32[]{:S(2)}) collective-permute-start(bf16[2,64,1024]{2,1,0:T(8,128)(2,1)} %fusion.191), channel_id=1, source_target_pairs={{4,0},{8,4},{12,8},{16,12},{20,16},{24,20},{28,24},{32,28},{36,32}... | collective-permute-start | bytes 786440 | tf_op jit(solution)/shard_map/ppermute | solution.py:19
  206.0 5.9 %collective-permute-done.16 = bf16[2,32,1024]{2,0,1:T(2,128)(2,1)S(1)} collective-permute-done((bf16[2,32,1024]{2,0,1:T(2,128)(2,1)}, bf16[2,32,1024]{2,0,1:T(2,128)(2,1)S(1)}, u32[]{:S(2)}, u32[]{:S(2)}) %collective-permute-start.16) | collective-permute-done | bytes 131104 | tf_op jit(solution)/shard_map/ppermute | solution.py:19
  211.9 6.6 %collective-permute-start.17 = (bf16[2,32,1024]{2,0,1:T(2,128)(2,1)}, bf16[2,32,1024]{2,0,1:T(2,128)(2,1)S(1)}, u32[]{:S(2)}, u32[]{:S(2)}) collective-permute-start(bf16[2,32,1024]{2,0,1:T(2,128)(2,1)} %fusion.190), channel_id=1, source_target_pairs={{12,0},{16,4},{20,8},{24,12},{28,16},{32,20},{36,24},{40,28},{44,3... | collective-permute-start | bytes 393224 | tf_op jit(solution)/shard_map/ppermute | solution.py:19
  218.6 3.3 collective-permute-done.17
  223.8 4.6 collective-permute-done.18
  228.5 2.6 collective-permute-start.19
  231.1 5.6 %collective-permute-done.19 = bf16[2,16,1024]{2,0,1:T(2,128)(2,1)S(1)} collective-permute-done((bf16[2,16,1024]{2,0,1:T(2,128)(2,1)S(1)}, bf16[2,16,1024]{2,0,1:T(2,128)(2,1)S(1)}, u32[]{:S(2)}, u32[]{:S(2)}) %collective-permute-start.19) | collective-permute-done | bytes 65568 | tf_op jit(solution)/shard_map/ppermute | solution.py:19
  236.7 7.8 %collective-permute-start.20 = (bf16[2,16,1024]{2,0,1:T(2,128)(2,1)S(1)}, bf16[2,16,1024]{2,0,1:T(2,128)(2,1)S(1)}, u32[]{:S(2)}, u32[]{:S(2)}) collective-permute-start(bf16[2,16,1024]{2,0,1:T(2,128)(2,1)S(1)} %fusion.189), channel_id=1, source_target_pairs={{24,0},{28,4},{32,8},{36,12},{40,16},{44,20},{48,24},{52,28},{56,3... | collective-permute-start | bytes 196616 | tf_op jit(solution)/shard_map/ppermute | solution.py:19
  246.1 8.0 %collective-permute-start.21 = (bf16[2,16,1024]{2,0,1:T(2,128)(2,1)S(1)}, bf16[2,16,1024]{2,0,1:T(2,128)(2,1)S(1)}, u32[]{:S(2)}, u32[]{:S(2)}) collective-permute-start(bf16[2,16,1024]{2,0,1:T(2,128)(2,1)S(1)} %fusion.189), channel_id=1, source_target_pairs={{28,0},{32,4},{36,8},{40,12},{44,16},{48,20},{52,24},{56,28},{60,3... | collective-permute-start | bytes 196616 | tf_op jit(solution)/shard_map/ppermute | solution.py:19
  256.0 10.4 %collective-permute-start.22 = (bf16[2,8,1024]{2,0,1:T(2,128)(2,1)}, bf16[2,8,1024]{2,0,1:T(2,128)(2,1)S(1)}, u32[]{:S(2)}, u32[]{:S(2)}) collective-permute-start(bf16[2,8,1024]{2,0,1:T(2,128)(2,1)} %fusion.81), channel_id=1, source_target_pairs={{32,0},{36,4},{40,8},{44,12},{48,16},{52,20},{56,24},{60,28},{64,3... | collective-permute-start | bytes 98312 | tf_op jit(solution)/shard_map/ppermute | solution.py:19
  267.7 11.0 %collective-permute-start.23 = (bf16[2,8,1024]{2,0,1:T(2,128)(2,1)}, bf16[2,8,1024]{2,0,1:T(2,128)(2,1)S(1)}, u32[]{:S(2)}, u32[]{:S(2)}) collective-permute-start(bf16[2,8,1024]{2,0,1:T(2,128)(2,1)} %fusion.81), channel_id=1, source_target_pairs={{36,0},{40,4},{44,8},{48,12},{52,16},{56,20},{60,24},{64,28},{68,3... | collective-permute-start | bytes 98312 | tf_op jit(solution)/shard_map/ppermute | solution.py:19
  279.9 11.5 %collective-permute-start.24 = (bf16[2,8,1024]{2,0,1:T(2,128)(2,1)}, bf16[2,8,1024]{2,0,1:T(2,128)(2,1)S(1)}, u32[]{:S(2)}, u32[]{:S(2)}) collective-permute-start(bf16[2,8,1024]{2,0,1:T(2,128)(2,1)} %fusion.81), channel_id=1, source_target_pairs={{40,0},{44,4},{48,8},{52,12},{56,16},{60,20},{64,24},{68,28},{72,3... | collective-permute-start | bytes 98312 | tf_op jit(solution)/shard_map/ppermute | solution.py:19
  292.8 7.1 %collective-permute-start.25 = (bf16[2,8,1024]{2,0,1:T(2,128)(2,1)}, bf16[2,8,1024]{2,0,1:T(2,128)(2,1)S(1)}, u32[]{:S(2)}, u32[]{:S(2)}) collective-permute-start(bf16[2,8,1024]{2,0,1:T(2,128)(2,1)} %fusion.81), channel_id=1, source_target_pairs={{44,0},{48,4},{52,8},{56,12},{60,16},{64,20},{68,24},{72,28},{76,3... | collective-permute-start | bytes 98312 | tf_op jit(solution)/shard_map/ppermute | solution.py:19
  300.0 4.0 collective-permute-done.25
  315.3 2.5 fusion.27
  359.3 4.2 all-to-all-start
  383.4 5.9 %collective-permute-start.52 = (bf16[2,8,1024]{2,1,0:T(8,128)(2,1)S(1)}, bf16[2,8,1024]{2,1,0:T(8,128)(2,1)S(1)}, u32[]{:S(2)}, u32[]{:S(2)}) collective-permute-start(bf16[2,8,1024]{2,1,0:T(8,128)(2,1)S(1)} %get-tuple-element.146), channel_id=1, source_target_pairs={{0,32},{4,36},{8,40},{12,44},{16,48},{20,52},{24,56},{28,60},{32,6... | collective-permute-start | bytes 98312 | tf_op jit(solution)/shard_map/ppermute | solution.py:19
  393.1 2.7 collective-permute-start.57
  408.2 6.8 %collective-permute-start.53 = (bf16[2,8,1024]{2,1,0:T(8,128)(2,1)S(1)}, bf16[2,8,1024]{2,1,0:T(8,128)(2,1)S(1)}, u32[]{:S(2)}, u32[]{:S(2)}) collective-permute-start(bf16[2,8,1024]{2,1,0:T(8,128)(2,1)S(1)} %get-tuple-element.153), channel_id=1, source_target_pairs={{0,36},{4,40},{8,44},{12,48},{16,52},{20,56},{24,60},{28,64},{32,6... | collective-permute-start | bytes 98312 | tf_op jit(solution)/shard_map/ppermute | solution.py:19
  415.1 8.2 %collective-permute-start.44 = (bf16[2,8,1024]{2,1,0:T(8,128)(2,1)S(1)}, bf16[2,8,1024]{2,1,0:T(8,128)(2,1)S(1)}, u32[]{:S(2)}, u32[]{:S(2)}) collective-permute-start(bf16[2,8,1024]{2,1,0:T(8,128)(2,1)S(1)} %get-tuple-element.138), channel_id=1, source_target_pairs={{32,0},{36,4},{40,8},{44,12},{48,16},{52,20},{56,24},{60,28},{64,3... | collective-permute-start | bytes 98312 | tf_op jit(solution)/shard_map/ppermute | solution.py:19
  423.4 8.0 %collective-permute-start.51 = (bf16[2,8,1024]{2,1,0:T(8,128)(2,1)S(1)}, bf16[2,8,1024]{2,1,0:T(8,128)(2,1)S(1)}, u32[]{:S(2)}, u32[]{:S(2)}) collective-permute-start(bf16[2,8,1024]{2,1,0:T(8,128)(2,1)S(1)} %get-tuple-element.139), channel_id=1, source_target_pairs={{60,0},{64,4},{68,8},{72,12},{76,16},{80,20},{84,24},{88,28},{92,3... | collective-permute-start | bytes 98312 | tf_op jit(solution)/shard_map/ppermute | solution.py:19
  431.4 12.1 %collective-permute-start.50 = (bf16[2,8,1024]{2,1,0:T(8,128)(2,1)S(1)}, bf16[2,8,1024]{2,1,0:T(8,128)(2,1)S(1)}, u32[]{:S(2)}, u32[]{:S(2)}) collective-permute-start(bf16[2,8,1024]{2,1,0:T(8,128)(2,1)S(1)} %get-tuple-element.140), channel_id=1, source_target_pairs={{56,0},{60,4},{64,8},{68,12},{72,16},{76,20},{80,24},{84,28},{88,3... | collective-permute-start | bytes 98312 | tf_op jit(solution)/shard_map/ppermute | solution.py:19
  443.5 11.5 %collective-permute-start.49 = (bf16[2,8,1024]{2,1,0:T(8,128)(2,1)S(1)}, bf16[2,8,1024]{2,1,0:T(8,128)(2,1)S(1)}, u32[]{:S(2)}, u32[]{:S(2)}) collective-permute-start(bf16[2,8,1024]{2,1,0:T(8,128)(2,1)S(1)} %get-tuple-element.141), channel_id=1, source_target_pairs={{52,0},{56,4},{60,8},{64,12},{68,16},{72,20},{76,24},{80,28},{84,3... | collective-permute-start | bytes 98312 | tf_op jit(solution)/shard_map/ppermute | solution.py:19
  455.0 9.1 %collective-permute-start.48 = (bf16[2,8,1024]{2,1,0:T(8,128)(2,1)S(1)}, bf16[2,8,1024]{2,1,0:T(8,128)(2,1)S(1)}, u32[]{:S(2)}, u32[]{:S(2)}) collective-permute-start(bf16[2,8,1024]{2,1,0:T(8,128)(2,1)S(1)} %get-tuple-element.142), channel_id=1, source_target_pairs={{48,0},{52,4},{56,8},{60,12},{64,16},{68,20},{72,24},{76,28},{80,3... | collective-permute-start | bytes 98312 | tf_op jit(solution)/shard_map/ppermute | solution.py:19
  464.1 9.6 %collective-permute-start.47 = (bf16[2,8,1024]{2,1,0:T(8,128)(2,1)S(1)}, bf16[2,8,1024]{2,1,0:T(8,128)(2,1)S(1)}, u32[]{:S(2)}, u32[]{:S(2)}) collective-permute-start(bf16[2,8,1024]{2,1,0:T(8,128)(2,1)S(1)} %get-tuple-element.143), channel_id=1, source_target_pairs={{44,0},{48,4},{52,8},{56,12},{60,16},{64,20},{68,24},{72,28},{76,3... | collective-permute-start | bytes 98312 | tf_op jit(solution)/shard_map/ppermute | solution.py:19
  473.7 9.4 %collective-permute-start.46 = (bf16[2,8,1024]{2,1,0:T(8,128)(2,1)S(1)}, bf16[2,8,1024]{2,1,0:T(8,128)(2,1)S(1)}, u32[]{:S(2)}, u32[]{:S(2)}) collective-permute-start(bf16[2,8,1024]{2,1,0:T(8,128)(2,1)S(1)} %get-tuple-element.144), channel_id=1, source_target_pairs={{40,0},{44,4},{48,8},{52,12},{56,16},{60,20},{64,24},{68,28},{72,3... | collective-permute-start | bytes 98312 | tf_op jit(solution)/shard_map/ppermute | solution.py:19
  483.2 4.0 collective-permute-start.45
  489.2 5.7 %collective-permute-start.43 = (bf16[2,16,1024]{2,1,0:T(8,128)(2,1)S(1)}, bf16[2,16,1024]{2,1,0:T(8,128)(2,1)S(1)}, u32[]{:S(2)}, u32[]{:S(2)}) collective-permute-start(bf16[2,16,1024]{2,1,0:T(8,128)(2,1)S(1)} %get-tuple-element.135), channel_id=1, source_target_pairs={{0,28},{4,32},{8,36},{12,40},{16,44},{20,48},{24,52},{28,56},{32,6... | collective-permute-start | bytes 196616 | tf_op jit(solution)/shard_map/ppermute | solution.py:19
  494.9 2.8 collective-permute-start.42
  500.9 6.4 %collective-permute-start.36 = (bf16[2,16,1024]{2,1,0:T(8,128)(2,1)S(1)}, bf16[2,16,1024]{2,1,0:T(8,128)(2,1)S(1)}, u32[]{:S(2)}, u32[]{:S(2)}) collective-permute-start(bf16[2,16,1024]{2,1,0:T(8,128)(2,1)S(1)} %get-tuple-element.130), channel_id=1, source_target_pairs={{16,0},{20,4},{24,8},{28,12},{32,16},{36,20},{40,24},{44,28},{48,3... | collective-permute-start | bytes 196616 | tf_op jit(solution)/shard_map/ppermute | solution.py:19
  507.3 5.7 %collective-permute-start.39 = (bf16[2,16,1024]{2,1,0:T(8,128)(2,1)S(1)}, bf16[2,16,1024]{2,1,0:T(8,128)(2,1)S(1)}, u32[]{:S(2)}, u32[]{:S(2)}) collective-permute-start(bf16[2,16,1024]{2,1,0:T(8,128)(2,1)S(1)} %get-tuple-element.131), channel_id=1, source_target_pairs={{28,0},{32,4},{36,8},{40,12},{44,16},{48,20},{52,24},{56,28},{60,3... | collective-permute-start | bytes 196616 | tf_op jit(solution)/shard_map/ppermute | solution.py:19
  513.0 3.8 collective-permute-start.38
  516.8 4.5 collective-permute-start.37
  521.4 3.6 collective-permute-start.34
  526.0 2.5 collective-permute-start.31
  530.4 3.1 collective-permute-start.35
  533.5 5.8 %collective-permute-start.32 = (bf16[2,32,1024]{2,1,0:T(8,128)(2,1)S(1)}, bf16[2,32,1024]{2,1,0:T(8,128)(2,1)S(1)}, u32[]{:S(2)}, u32[]{:S(2)}) collective-permute-start(bf16[2,32,1024]{2,1,0:T(8,128)(2,1)S(1)} %get-tuple-element.126), channel_id=1, source_target_pairs={{8,0},{12,4},{16,8},{20,12},{24,16},{28,20},{32,24},{36,28},{40,32... | collective-permute-start | bytes 393224 | tf_op jit(solution)/shard_map/ppermute | solution.py:19
  542.0 5.5 collective-permute-done.33
  (344 shorter events, 136.8 us)
Async XLA Ops:
  4.4 301.2 %collective-permute-start.29 = (bf16[2,8,1024]{2,0,1:T(2,128)(2,1)}, bf16[2,8,1024]{2,0,1:T(2,128)(2,1)}, u32[]{:S(2)}, u32[]{:S(2)}) collective-permute-start(bf16[2,8,1024]{2,0,1:T(2,128)(2,1)} %fusion.81), channel_id=1, source_target_pairs={{60,0},{64,4},{68,8},{72,12},{76,16},{80,20},{84,24},{88,28},{92,3... | collective-permute-start | bytes 98312 | tf_op jit(solution)/shard_map/ppermute | solution.py:19
  20.2 284.6 %collective-permute-start.28 = (bf16[2,8,1024]{2,0,1:T(2,128)(2,1)}, bf16[2,8,1024]{2,0,1:T(2,128)(2,1)}, u32[]{:S(2)}, u32[]{:S(2)}) collective-permute-start(bf16[2,8,1024]{2,0,1:T(2,128)(2,1)} %fusion.81), channel_id=1, source_target_pairs={{56,0},{60,4},{64,8},{68,12},{72,16},{76,20},{80,24},{84,28},{88,3... | collective-permute-start | bytes 98312 | tf_op jit(solution)/shard_map/ppermute | solution.py:19
  22.1 281.9 %collective-permute-start.27 = (bf16[2,8,1024]{2,0,1:T(2,128)(2,1)}, bf16[2,8,1024]{2,0,1:T(2,128)(2,1)}, u32[]{:S(2)}, u32[]{:S(2)}) collective-permute-start(bf16[2,8,1024]{2,0,1:T(2,128)(2,1)} %fusion.81), channel_id=1, source_target_pairs={{52,0},{56,4},{60,8},{64,12},{68,16},{72,20},{76,24},{80,28},{84,3... | collective-permute-start | bytes 98312 | tf_op jit(solution)/shard_map/ppermute | solution.py:19
  33.9 281.4 %all-to-all-start.1 = ((bf16[32,4,1024]{2,0,1:T(8,128)(2,1)}), bf16[32,4,1024]{2,0,1:T(8,128)(2,1)}, u32[]{:S(2)}, u32[]{:S(2)}) async-start(bf16[32,4,1024]{2,0,1:T(8,128)(2,1)} %bitcast.289), calls=%async_computation.1 | async-start | bytes 524288 | tf_op jit(solution)/shard_map/all_to_all | solution.py:76
  39.0 16.9 %collective-permute-start.1 = (bf16[2,32,1024]{2,0,1:T(2,128)(2,1)}, bf16[2,32,1024]{2,0,1:T(2,128)(2,1)}, u32[]{:S(2)}, u32[]{:S(2)}) collective-permute-start(bf16[2,32,1024]{2,0,1:T(2,128)(2,1)} %fusion.190), channel_id=1, source_target_pairs={{0,8},{4,12},{8,16},{12,20},{16,24},{20,28},{24,32},{28,36},{32,40... | collective-permute-start | bytes 393224 | tf_op jit(solution)/shard_map/ppermute | solution.py:19
  41.7 6.9 %collective-permute-start = (bf16[2,64,1024]{2,1,0:T(8,128)(2,1)}, bf16[2,64,1024]{2,1,0:T(8,128)(2,1)S(1)}, u32[]{:S(2)}, u32[]{:S(2)}) collective-permute-start(bf16[2,64,1024]{2,1,0:T(8,128)(2,1)} %fusion.191), channel_id=1, source_target_pairs={{0,4},{4,8},{8,12},{12,16},{16,20},{20,24},{24,28},{28,32},{32,36}... | collective-permute-start | bytes 786440 | tf_op jit(solution)/shard_map/ppermute | solution.py:19
  46.1 261.7 %copy-start.3 = (bf16[128,1024]{1,0:T(8,128)(2,1)S(1)}, bf16[128,1024]{1,0:T(8,128)(2,1)}, u32[]{:S(2)}) copy-start(bf16[128,1024]{1,0:T(8,128)(2,1)} %param.4) | copy-start | bytes 786436
  48.6 153.5 %collective-permute-start.14 = (bf16[2,8,1024]{2,0,1:T(2,128)(2,1)}, bf16[2,8,1024]{2,0,1:T(2,128)(2,1)S(1)}, u32[]{:S(2)}, u32[]{:S(2)}) collective-permute-start(bf16[2,8,1024]{2,0,1:T(2,128)(2,1)} %fusion.81), channel_id=1, source_target_pairs={{0,60},{4,64},{8,68},{12,72},{16,76},{20,80},{24,84},{28,88},{32,9... | collective-permute-start | bytes 98312 | tf_op jit(solution)/shard_map/ppermute | solution.py:19
  55.9 10.1 %collective-permute-start.2 = (bf16[2,32,1024]{2,0,1:T(2,128)(2,1)}, bf16[2,32,1024]{2,0,1:T(2,128)(2,1)S(1)}, u32[]{:S(2)}, u32[]{:S(2)}) collective-permute-start(bf16[2,32,1024]{2,0,1:T(2,128)(2,1)} %fusion.190), channel_id=1, source_target_pairs={{0,12},{4,16},{8,20},{12,24},{16,28},{20,32},{24,36},{28,40},{32,4... | collective-permute-start | bytes 393224 | tf_op jit(solution)/shard_map/ppermute | solution.py:19
  66.0 8.7 %collective-permute-start.3 = (bf16[2,16,1024]{2,0,1:T(2,128)(2,1)S(1)}, bf16[2,16,1024]{2,0,1:T(2,128)(2,1)S(1)}, u32[]{:S(2)}, u32[]{:S(2)}) collective-permute-start(bf16[2,16,1024]{2,0,1:T(2,128)(2,1)S(1)} %fusion.189), channel_id=1, source_target_pairs={{0,16},{4,20},{8,24},{12,28},{16,32},{20,36},{24,40},{28,44},{32,4... | collective-permute-start | bytes 196616 | tf_op jit(solution)/shard_map/ppermute | solution.py:19
  74.7 8.6 %collective-permute-start.4 = (bf16[2,16,1024]{2,0,1:T(2,128)(2,1)S(1)}, bf16[2,16,1024]{2,0,1:T(2,128)(2,1)S(1)}, u32[]{:S(2)}, u32[]{:S(2)}) collective-permute-start(bf16[2,16,1024]{2,0,1:T(2,128)(2,1)S(1)} %fusion.189), channel_id=1, source_target_pairs={{0,20},{4,24},{8,28},{12,32},{16,36},{20,40},{24,44},{28,48},{32,5... | collective-permute-start | bytes 196616 | tf_op jit(solution)/shard_map/ppermute | solution.py:19
  83.3 9.0 %collective-permute-start.5 = (bf16[2,16,1024]{2,0,1:T(2,128)(2,1)S(1)}, bf16[2,16,1024]{2,0,1:T(2,128)(2,1)S(1)}, u32[]{:S(2)}, u32[]{:S(2)}) collective-permute-start(bf16[2,16,1024]{2,0,1:T(2,128)(2,1)S(1)} %fusion.189), channel_id=1, source_target_pairs={{0,24},{4,28},{8,32},{12,36},{16,40},{20,44},{24,48},{28,52},{32,5... | collective-permute-start | bytes 196616 | tf_op jit(solution)/shard_map/ppermute | solution.py:19
  92.3 13.2 %collective-permute-start.6 = (bf16[2,16,1024]{2,0,1:T(2,128)(2,1)S(1)}, bf16[2,16,1024]{2,0,1:T(2,128)(2,1)S(1)}, u32[]{:S(2)}, u32[]{:S(2)}) collective-permute-start(bf16[2,16,1024]{2,0,1:T(2,128)(2,1)S(1)} %fusion.189), channel_id=1, source_target_pairs={{0,28},{4,32},{8,36},{12,40},{16,44},{20,48},{24,52},{28,56},{32,6... | collective-permute-start | bytes 196616 | tf_op jit(solution)/shard_map/ppermute | solution.py:19
  105.5 10.1 %collective-permute-start.7 = (bf16[2,8,1024]{2,0,1:T(2,128)(2,1)}, bf16[2,8,1024]{2,0,1:T(2,128)(2,1)S(1)}, u32[]{:S(2)}, u32[]{:S(2)}) collective-permute-start(bf16[2,8,1024]{2,0,1:T(2,128)(2,1)} %fusion.81), channel_id=1, source_target_pairs={{0,32},{4,36},{8,40},{12,44},{16,48},{20,52},{24,56},{28,60},{32,6... | collective-permute-start | bytes 98312 | tf_op jit(solution)/shard_map/ppermute | solution.py:19
  115.6 10.2 %collective-permute-start.8 = (bf16[2,8,1024]{2,0,1:T(2,128)(2,1)}, bf16[2,8,1024]{2,0,1:T(2,128)(2,1)S(1)}, u32[]{:S(2)}, u32[]{:S(2)}) collective-permute-start(bf16[2,8,1024]{2,0,1:T(2,128)(2,1)} %fusion.81), channel_id=1, source_target_pairs={{0,36},{4,40},{8,44},{12,48},{16,52},{20,56},{24,60},{28,64},{32,6... | collective-permute-start | bytes 98312 | tf_op jit(solution)/shard_map/ppermute | solution.py:19
  125.9 11.9 %collective-permute-start.9 = (bf16[2,8,1024]{2,0,1:T(2,128)(2,1)}, bf16[2,8,1024]{2,0,1:T(2,128)(2,1)S(1)}, u32[]{:S(2)}, u32[]{:S(2)}) collective-permute-start(bf16[2,8,1024]{2,0,1:T(2,128)(2,1)} %fusion.81), channel_id=1, source_target_pairs={{0,40},{4,44},{8,48},{12,52},{16,56},{20,60},{24,64},{28,68},{32,7... | collective-permute-start | bytes 98312 | tf_op jit(solution)/shard_map/ppermute | solution.py:19
  137.8 13.0 %collective-permute-start.10 = (bf16[2,8,1024]{2,0,1:T(2,128)(2,1)}, bf16[2,8,1024]{2,0,1:T(2,128)(2,1)S(1)}, u32[]{:S(2)}, u32[]{:S(2)}) collective-permute-start(bf16[2,8,1024]{2,0,1:T(2,128)(2,1)} %fusion.81), channel_id=1, source_target_pairs={{0,44},{4,48},{8,52},{12,56},{16,60},{20,64},{24,68},{28,72},{32,7... | collective-permute-start | bytes 98312 | tf_op jit(solution)/shard_map/ppermute | solution.py:19
  150.7 13.6 %collective-permute-start.11 = (bf16[2,8,1024]{2,0,1:T(2,128)(2,1)}, bf16[2,8,1024]{2,0,1:T(2,128)(2,1)S(1)}, u32[]{:S(2)}, u32[]{:S(2)}) collective-permute-start(bf16[2,8,1024]{2,0,1:T(2,128)(2,1)} %fusion.81), channel_id=1, source_target_pairs={{0,48},{4,52},{8,56},{12,60},{16,64},{20,68},{24,72},{28,76},{32,8... | collective-permute-start | bytes 98312 | tf_op jit(solution)/shard_map/ppermute | solution.py:19
  164.3 14.0 %collective-permute-start.12 = (bf16[2,8,1024]{2,0,1:T(2,128)(2,1)}, bf16[2,8,1024]{2,0,1:T(2,128)(2,1)S(1)}, u32[]{:S(2)}, u32[]{:S(2)}) collective-permute-start(bf16[2,8,1024]{2,0,1:T(2,128)(2,1)} %fusion.81), channel_id=1, source_target_pairs={{0,52},{4,56},{8,60},{12,64},{16,68},{20,72},{24,76},{28,80},{32,8... | collective-permute-start | bytes 98312 | tf_op jit(solution)/shard_map/ppermute | solution.py:19
  178.3 13.9 %collective-permute-start.13 = (bf16[2,8,1024]{2,0,1:T(2,128)(2,1)}, bf16[2,8,1024]{2,0,1:T(2,128)(2,1)S(1)}, u32[]{:S(2)}, u32[]{:S(2)}) collective-permute-start(bf16[2,8,1024]{2,0,1:T(2,128)(2,1)} %fusion.81), channel_id=1, source_target_pairs={{0,56},{4,60},{8,64},{12,68},{16,72},{20,76},{24,80},{28,84},{32,8... | collective-permute-start | bytes 98312 | tf_op jit(solution)/shard_map/ppermute | solution.py:19
  192.1 11.9 %collective-permute-start.15 = (bf16[2,64,1024]{2,1,0:T(8,128)(2,1)}, bf16[2,64,1024]{2,1,0:T(8,128)(2,1)S(1)}, u32[]{:S(2)}, u32[]{:S(2)}) collective-permute-start(bf16[2,64,1024]{2,1,0:T(8,128)(2,1)} %fusion.191), channel_id=1, source_target_pairs={{4,0},{8,4},{12,8},{16,12},{20,16},{24,20},{28,24},{32,28},{36,32}... | collective-permute-start | bytes 786440 | tf_op jit(solution)/shard_map/ppermute | solution.py:19
  202.1 9.9 %collective-permute-start.16 = (bf16[2,32,1024]{2,0,1:T(2,128)(2,1)}, bf16[2,32,1024]{2,0,1:T(2,128)(2,1)S(1)}, u32[]{:S(2)}, u32[]{:S(2)}) collective-permute-start(bf16[2,32,1024]{2,0,1:T(2,128)(2,1)} %fusion.190), channel_id=1, source_target_pairs={{8,0},{12,4},{16,8},{20,12},{24,16},{28,20},{32,24},{36,28},{40,32... | collective-permute-start | bytes 393224 | tf_op jit(solution)/shard_map/ppermute | solution.py:19
  204.0 100.0 %collective-permute-start.26 = (bf16[2,8,1024]{2,0,1:T(2,128)(2,1)}, bf16[2,8,1024]{2,0,1:T(2,128)(2,1)S(1)}, u32[]{:S(2)}, u32[]{:S(2)}) collective-permute-start(bf16[2,8,1024]{2,0,1:T(2,128)(2,1)} %fusion.81), channel_id=1, source_target_pairs={{48,0},{52,4},{56,8},{60,12},{64,16},{68,20},{72,24},{76,28},{80,3... | collective-permute-start | bytes 98312 | tf_op jit(solution)/shard_map/ppermute | solution.py:19
  211.9 10.0 %collective-permute-start.17 = (bf16[2,32,1024]{2,0,1:T(2,128)(2,1)}, bf16[2,32,1024]{2,0,1:T(2,128)(2,1)S(1)}, u32[]{:S(2)}, u32[]{:S(2)}) collective-permute-start(bf16[2,32,1024]{2,0,1:T(2,128)(2,1)} %fusion.190), channel_id=1, source_target_pairs={{12,0},{16,4},{20,8},{24,12},{28,16},{32,20},{36,24},{40,28},{44,3... | collective-permute-start | bytes 393224 | tf_op jit(solution)/shard_map/ppermute | solution.py:19
  221.9 6.6 %collective-permute-start.18 = (bf16[2,16,1024]{2,0,1:T(2,128)(2,1)S(1)}, bf16[2,16,1024]{2,0,1:T(2,128)(2,1)S(1)}, u32[]{:S(2)}, u32[]{:S(2)}) collective-permute-start(bf16[2,16,1024]{2,0,1:T(2,128)(2,1)S(1)} %fusion.189), channel_id=1, source_target_pairs={{16,0},{20,4},{24,8},{28,12},{32,16},{36,20},{40,24},{44,28},{48,3... | collective-permute-start | bytes 196616 | tf_op jit(solution)/shard_map/ppermute | solution.py:19
  228.5 8.2 %collective-permute-start.19 = (bf16[2,16,1024]{2,0,1:T(2,128)(2,1)S(1)}, bf16[2,16,1024]{2,0,1:T(2,128)(2,1)S(1)}, u32[]{:S(2)}, u32[]{:S(2)}) collective-permute-start(bf16[2,16,1024]{2,0,1:T(2,128)(2,1)S(1)} %fusion.189), channel_id=1, source_target_pairs={{20,0},{24,4},{28,8},{32,12},{36,16},{40,20},{44,24},{48,28},{52,3... | collective-permute-start | bytes 196616 | tf_op jit(solution)/shard_map/ppermute | solution.py:19
  236.7 9.4 %collective-permute-start.20 = (bf16[2,16,1024]{2,0,1:T(2,128)(2,1)S(1)}, bf16[2,16,1024]{2,0,1:T(2,128)(2,1)S(1)}, u32[]{:S(2)}, u32[]{:S(2)}) collective-permute-start(bf16[2,16,1024]{2,0,1:T(2,128)(2,1)S(1)} %fusion.189), channel_id=1, source_target_pairs={{24,0},{28,4},{32,8},{36,12},{40,16},{44,20},{48,24},{52,28},{56,3... | collective-permute-start | bytes 196616 | tf_op jit(solution)/shard_map/ppermute | solution.py:19
  246.1 9.9 %collective-permute-start.21 = (bf16[2,16,1024]{2,0,1:T(2,128)(2,1)S(1)}, bf16[2,16,1024]{2,0,1:T(2,128)(2,1)S(1)}, u32[]{:S(2)}, u32[]{:S(2)}) collective-permute-start(bf16[2,16,1024]{2,0,1:T(2,128)(2,1)S(1)} %fusion.189), channel_id=1, source_target_pairs={{28,0},{32,4},{36,8},{40,12},{44,16},{48,20},{52,24},{56,28},{60,3... | collective-permute-start | bytes 196616 | tf_op jit(solution)/shard_map/ppermute | solution.py:19
  256.0 11.7 %collective-permute-start.22 = (bf16[2,8,1024]{2,0,1:T(2,128)(2,1)}, bf16[2,8,1024]{2,0,1:T(2,128)(2,1)S(1)}, u32[]{:S(2)}, u32[]{:S(2)}) collective-permute-start(bf16[2,8,1024]{2,0,1:T(2,128)(2,1)} %fusion.81), channel_id=1, source_target_pairs={{32,0},{36,4},{40,8},{44,12},{48,16},{52,20},{56,24},{60,28},{64,3... | collective-permute-start | bytes 98312 | tf_op jit(solution)/shard_map/ppermute | solution.py:19
  267.7 12.3 %collective-permute-start.23 = (bf16[2,8,1024]{2,0,1:T(2,128)(2,1)}, bf16[2,8,1024]{2,0,1:T(2,128)(2,1)S(1)}, u32[]{:S(2)}, u32[]{:S(2)}) collective-permute-start(bf16[2,8,1024]{2,0,1:T(2,128)(2,1)} %fusion.81), channel_id=1, source_target_pairs={{36,0},{40,4},{44,8},{48,12},{52,16},{56,20},{60,24},{64,28},{68,3... | collective-permute-start | bytes 98312 | tf_op jit(solution)/shard_map/ppermute | solution.py:19
  279.9 12.9 %collective-permute-start.24 = (bf16[2,8,1024]{2,0,1:T(2,128)(2,1)}, bf16[2,8,1024]{2,0,1:T(2,128)(2,1)S(1)}, u32[]{:S(2)}, u32[]{:S(2)}) collective-permute-start(bf16[2,8,1024]{2,0,1:T(2,128)(2,1)} %fusion.81), channel_id=1, source_target_pairs={{40,0},{44,4},{48,8},{52,12},{56,16},{60,20},{64,24},{68,28},{72,3... | collective-permute-start | bytes 98312 | tf_op jit(solution)/shard_map/ppermute | solution.py:19
  292.8 11.2 %collective-permute-start.25 = (bf16[2,8,1024]{2,0,1:T(2,128)(2,1)}, bf16[2,8,1024]{2,0,1:T(2,128)(2,1)S(1)}, u32[]{:S(2)}, u32[]{:S(2)}) collective-permute-start(bf16[2,8,1024]{2,0,1:T(2,128)(2,1)} %fusion.81), channel_id=1, source_target_pairs={{44,0},{48,4},{52,8},{56,12},{60,16},{64,20},{68,24},{72,28},{76,3... | collective-permute-start | bytes 98312 | tf_op jit(solution)/shard_map/ppermute | solution.py:19
  359.3 188.8 %all-to-all-start = ((bf16[4,32,1024]{2,1,0:T(8,128)(2,1)}), bf16[4,32,1024]{2,1,0:T(8,128)(2,1)S(1)}, u32[]{:S(2)}, u32[]{:S(2)}) async-start(bf16[4,32,1024]{2,1,0:T(8,128)(2,1)} %bitcast.35), calls=%async_computation | async-start | bytes 524288 | tf_op jit(solution)/shard_map/all_to_all | solution.py:156
  383.4 20.1 %collective-permute-start.52 = (bf16[2,8,1024]{2,1,0:T(8,128)(2,1)S(1)}, bf16[2,8,1024]{2,1,0:T(8,128)(2,1)S(1)}, u32[]{:S(2)}, u32[]{:S(2)}) collective-permute-start(bf16[2,8,1024]{2,1,0:T(8,128)(2,1)S(1)} %get-tuple-element.146), channel_id=1, source_target_pairs={{0,32},{4,36},{8,40},{12,44},{16,48},{20,52},{24,56},{28,60},{32,6... | collective-permute-start | bytes 98312 | tf_op jit(solution)/shard_map/ppermute | solution.py:19
  389.3 16.1 %collective-permute-start.59 = (bf16[2,8,1024]{2,1,0:T(8,128)(2,1)S(1)}, bf16[2,8,1024]{2,1,0:T(8,128)(2,1)S(1)}, u32[]{:S(2)}, u32[]{:S(2)}) collective-permute-start(bf16[2,8,1024]{2,1,0:T(8,128)(2,1)S(1)} %get-tuple-element.147), channel_id=1, source_target_pairs={{0,60},{4,64},{8,68},{12,72},{16,76},{20,80},{24,84},{28,88},{32,9... | collective-permute-start | bytes 98312 | tf_op jit(solution)/shard_map/ppermute | solution.py:19
  391.2 16.9 %collective-permute-start.58 = (bf16[2,8,1024]{2,1,0:T(8,128)(2,1)S(1)}, bf16[2,8,1024]{2,1,0:T(8,128)(2,1)S(1)}, u32[]{:S(2)}, u32[]{:S(2)}) collective-permute-start(bf16[2,8,1024]{2,1,0:T(8,128)(2,1)S(1)} %get-tuple-element.148), channel_id=1, source_target_pairs={{0,56},{4,60},{8,64},{12,68},{16,72},{20,76},{24,80},{28,84},{32,8... | collective-permute-start | bytes 98312 | tf_op jit(solution)/shard_map/ppermute | solution.py:19
  393.1 21.9 %collective-permute-start.57 = (bf16[2,8,1024]{2,1,0:T(8,128)(2,1)S(1)}, bf16[2,8,1024]{2,1,0:T(8,128)(2,1)S(1)}, u32[]{:S(2)}, u32[]{:S(2)}) collective-permute-start(bf16[2,8,1024]{2,1,0:T(8,128)(2,1)S(1)} %get-tuple-element.149), channel_id=1, source_target_pairs={{0,52},{4,56},{8,60},{12,64},{16,68},{20,72},{24,76},{28,80},{32,8... | collective-permute-start | bytes 98312 | tf_op jit(solution)/shard_map/ppermute | solution.py:19
  395.9 27.5 %collective-permute-start.56 = (bf16[2,8,1024]{2,1,0:T(8,128)(2,1)S(1)}, bf16[2,8,1024]{2,1,0:T(8,128)(2,1)S(1)}, u32[]{:S(2)}, u32[]{:S(2)}) collective-permute-start(bf16[2,8,1024]{2,1,0:T(8,128)(2,1)S(1)} %get-tuple-element.150), channel_id=1, source_target_pairs={{0,48},{4,52},{8,56},{12,60},{16,64},{20,68},{24,72},{28,76},{32,8... | collective-permute-start | bytes 98312 | tf_op jit(solution)/shard_map/ppermute | solution.py:19
  397.9 102.2 %copy-start.14 = (bf16[128,1024]{0,1:T(8,128)(2,1)S(1)}, bf16[128,1024]{0,1:T(8,128)(2,1)}, u32[]{:S(2)}) copy-start(bf16[128,1024]{0,1:T(8,128)(2,1)} %fusion.8) | copy-start | bytes 786436
  403.4 28.0 %collective-permute-start.55 = (bf16[2,8,1024]{2,1,0:T(8,128)(2,1)S(1)}, bf16[2,8,1024]{2,1,0:T(8,128)(2,1)S(1)}, u32[]{:S(2)}, u32[]{:S(2)}) collective-permute-start(bf16[2,8,1024]{2,1,0:T(8,128)(2,1)S(1)} %get-tuple-element.151), channel_id=1, source_target_pairs={{0,44},{4,48},{8,52},{12,56},{16,60},{20,64},{24,68},{28,72},{32,7... | collective-permute-start | bytes 98312 | tf_op jit(solution)/shard_map/ppermute | solution.py:19
  405.4 38.1 %collective-permute-start.54 = (bf16[2,8,1024]{2,1,0:T(8,128)(2,1)S(1)}, bf16[2,8,1024]{2,1,0:T(8,128)(2,1)S(1)}, u32[]{:S(2)}, u32[]{:S(2)}) collective-permute-start(bf16[2,8,1024]{2,1,0:T(8,128)(2,1)S(1)} %get-tuple-element.152), channel_id=1, source_target_pairs={{0,40},{4,44},{8,48},{12,52},{16,56},{20,60},{24,64},{28,68},{32,7... | collective-permute-start | bytes 98312 | tf_op jit(solution)/shard_map/ppermute | solution.py:19
  408.2 46.8 %collective-permute-start.53 = (bf16[2,8,1024]{2,1,0:T(8,128)(2,1)S(1)}, bf16[2,8,1024]{2,1,0:T(8,128)(2,1)S(1)}, u32[]{:S(2)}, u32[]{:S(2)}) collective-permute-start(bf16[2,8,1024]{2,1,0:T(8,128)(2,1)S(1)} %get-tuple-element.153), channel_id=1, source_target_pairs={{0,36},{4,40},{8,44},{12,48},{16,52},{20,56},{24,60},{28,64},{32,6... | collective-permute-start | bytes 98312 | tf_op jit(solution)/shard_map/ppermute | solution.py:19
  415.1 49.0 %collective-permute-start.44 = (bf16[2,8,1024]{2,1,0:T(8,128)(2,1)S(1)}, bf16[2,8,1024]{2,1,0:T(8,128)(2,1)S(1)}, u32[]{:S(2)}, u32[]{:S(2)}) collective-permute-start(bf16[2,8,1024]{2,1,0:T(8,128)(2,1)S(1)} %get-tuple-element.138), channel_id=1, source_target_pairs={{32,0},{36,4},{40,8},{44,12},{48,16},{52,20},{56,24},{60,28},{64,3... | collective-permute-start | bytes 98312 | tf_op jit(solution)/shard_map/ppermute | solution.py:19
  423.4 50.4 %collective-permute-start.51 = (bf16[2,8,1024]{2,1,0:T(8,128)(2,1)S(1)}, bf16[2,8,1024]{2,1,0:T(8,128)(2,1)S(1)}, u32[]{:S(2)}, u32[]{:S(2)}) collective-permute-start(bf16[2,8,1024]{2,1,0:T(8,128)(2,1)S(1)} %get-tuple-element.139), channel_id=1, source_target_pairs={{60,0},{64,4},{68,8},{72,12},{76,16},{80,20},{84,24},{88,28},{92,3... | collective-permute-start | bytes 98312 | tf_op jit(solution)/shard_map/ppermute | solution.py:19
  431.4 51.7 %collective-permute-start.50 = (bf16[2,8,1024]{2,1,0:T(8,128)(2,1)S(1)}, bf16[2,8,1024]{2,1,0:T(8,128)(2,1)S(1)}, u32[]{:S(2)}, u32[]{:S(2)}) collective-permute-start(bf16[2,8,1024]{2,1,0:T(8,128)(2,1)S(1)} %get-tuple-element.140), channel_id=1, source_target_pairs={{56,0},{60,4},{64,8},{68,12},{72,16},{76,20},{80,24},{84,28},{88,3... | collective-permute-start | bytes 98312 | tf_op jit(solution)/shard_map/ppermute | solution.py:19
  443.5 43.7 %collective-permute-start.49 = (bf16[2,8,1024]{2,1,0:T(8,128)(2,1)S(1)}, bf16[2,8,1024]{2,1,0:T(8,128)(2,1)S(1)}, u32[]{:S(2)}, u32[]{:S(2)}) collective-permute-start(bf16[2,8,1024]{2,1,0:T(8,128)(2,1)S(1)} %get-tuple-element.141), channel_id=1, source_target_pairs={{52,0},{56,4},{60,8},{64,12},{68,16},{72,20},{76,24},{80,28},{84,3... | collective-permute-start | bytes 98312 | tf_op jit(solution)/shard_map/ppermute | solution.py:19
  455.0 34.2 %collective-permute-start.48 = (bf16[2,8,1024]{2,1,0:T(8,128)(2,1)S(1)}, bf16[2,8,1024]{2,1,0:T(8,128)(2,1)S(1)}, u32[]{:S(2)}, u32[]{:S(2)}) collective-permute-start(bf16[2,8,1024]{2,1,0:T(8,128)(2,1)S(1)} %get-tuple-element.142), channel_id=1, source_target_pairs={{48,0},{52,4},{56,8},{60,12},{64,16},{68,20},{72,24},{76,28},{80,3... | collective-permute-start | bytes 98312 | tf_op jit(solution)/shard_map/ppermute | solution.py:19
  464.1 30.8 %collective-permute-start.47 = (bf16[2,8,1024]{2,1,0:T(8,128)(2,1)S(1)}, bf16[2,8,1024]{2,1,0:T(8,128)(2,1)S(1)}, u32[]{:S(2)}, u32[]{:S(2)}) collective-permute-start(bf16[2,8,1024]{2,1,0:T(8,128)(2,1)S(1)} %get-tuple-element.143), channel_id=1, source_target_pairs={{44,0},{48,4},{52,8},{56,12},{60,16},{64,20},{68,24},{72,28},{76,3... | collective-permute-start | bytes 98312 | tf_op jit(solution)/shard_map/ppermute | solution.py:19
  473.7 24.0 %collective-permute-start.46 = (bf16[2,8,1024]{2,1,0:T(8,128)(2,1)S(1)}, bf16[2,8,1024]{2,1,0:T(8,128)(2,1)S(1)}, u32[]{:S(2)}, u32[]{:S(2)}) collective-permute-start(bf16[2,8,1024]{2,1,0:T(8,128)(2,1)S(1)} %get-tuple-element.144), channel_id=1, source_target_pairs={{40,0},{44,4},{48,8},{52,12},{56,16},{60,20},{64,24},{68,28},{72,3... | collective-permute-start | bytes 98312 | tf_op jit(solution)/shard_map/ppermute | solution.py:19
  483.2 17.7 %collective-permute-start.45 = (bf16[2,8,1024]{2,1,0:T(8,128)(2,1)S(1)}, bf16[2,8,1024]{2,1,0:T(8,128)(2,1)}, u32[]{:S(2)}, u32[]{:S(2)}) collective-permute-start(bf16[2,8,1024]{2,1,0:T(8,128)(2,1)S(1)} %get-tuple-element.145), channel_id=1, source_target_pairs={{36,0},{40,4},{44,8},{48,12},{52,16},{56,20},{60,24},{64,28},{68,3... | collective-permute-start | bytes 98312 | tf_op jit(solution)/shard_map/ppermute | solution.py:19
  487.2 20.0 %collective-permute-start.40 = (bf16[2,16,1024]{2,1,0:T(8,128)(2,1)S(1)}, bf16[2,16,1024]{2,1,0:T(8,128)(2,1)S(1)}, u32[]{:S(2)}, u32[]{:S(2)}) collective-permute-start(bf16[2,16,1024]{2,1,0:T(8,128)(2,1)S(1)} %get-tuple-element.134), channel_id=1, source_target_pairs={{0,16},{4,20},{8,24},{12,28},{16,32},{20,36},{24,40},{28,44},{32,4... | collective-permute-start | bytes 196616 | tf_op jit(solution)/shard_map/ppermute | solution.py:19
  489.2 23.8 %collective-permute-start.43 = (bf16[2,16,1024]{2,1,0:T(8,128)(2,1)S(1)}, bf16[2,16,1024]{2,1,0:T(8,128)(2,1)S(1)}, u32[]{:S(2)}, u32[]{:S(2)}) collective-permute-start(bf16[2,16,1024]{2,1,0:T(8,128)(2,1)S(1)} %get-tuple-element.135), channel_id=1, source_target_pairs={{0,28},{4,32},{8,36},{12,40},{16,44},{20,48},{24,52},{28,56},{32,6... | collective-permute-start | bytes 196616 | tf_op jit(solution)/shard_map/ppermute | solution.py:19
  494.9 21.9 %collective-permute-start.42 = (bf16[2,16,1024]{2,1,0:T(8,128)(2,1)S(1)}, bf16[2,16,1024]{2,1,0:T(8,128)(2,1)S(1)}, u32[]{:S(2)}, u32[]{:S(2)}) collective-permute-start(bf16[2,16,1024]{2,1,0:T(8,128)(2,1)S(1)} %get-tuple-element.136), channel_id=1, source_target_pairs={{0,24},{4,28},{8,32},{12,36},{16,40},{20,44},{24,48},{28,52},{32,5... | collective-permute-start | bytes 196616 | tf_op jit(solution)/shard_map/ppermute | solution.py:19
  497.8 23.6 %collective-permute-start.41 = (bf16[2,16,1024]{2,1,0:T(8,128)(2,1)S(1)}, bf16[2,16,1024]{2,1,0:T(8,128)(2,1)S(1)}, u32[]{:S(2)}, u32[]{:S(2)}) collective-permute-start(bf16[2,16,1024]{2,1,0:T(8,128)(2,1)S(1)} %get-tuple-element.137), channel_id=1, source_target_pairs={{0,20},{4,24},{8,28},{12,32},{16,36},{20,40},{24,44},{28,48},{32,5... | collective-permute-start | bytes 196616 | tf_op jit(solution)/shard_map/ppermute | solution.py:19
  500.9 25.1 %collective-permute-start.36 = (bf16[2,16,1024]{2,1,0:T(8,128)(2,1)S(1)}, bf16[2,16,1024]{2,1,0:T(8,128)(2,1)S(1)}, u32[]{:S(2)}, u32[]{:S(2)}) collective-permute-start(bf16[2,16,1024]{2,1,0:T(8,128)(2,1)S(1)} %get-tuple-element.130), channel_id=1, source_target_pairs={{16,0},{20,4},{24,8},{28,12},{32,16},{36,20},{40,24},{44,28},{48,3... | collective-permute-start | bytes 196616 | tf_op jit(solution)/shard_map/ppermute | solution.py:19
  507.3 21.2 %collective-permute-start.39 = (bf16[2,16,1024]{2,1,0:T(8,128)(2,1)S(1)}, bf16[2,16,1024]{2,1,0:T(8,128)(2,1)S(1)}, u32[]{:S(2)}, u32[]{:S(2)}) collective-permute-start(bf16[2,16,1024]{2,1,0:T(8,128)(2,1)S(1)} %get-tuple-element.131), channel_id=1, source_target_pairs={{28,0},{32,4},{36,8},{40,12},{44,16},{48,20},{52,24},{56,28},{60,3... | collective-permute-start | bytes 196616 | tf_op jit(solution)/shard_map/ppermute | solution.py:19
  513.0 17.4 %collective-permute-start.38 = (bf16[2,16,1024]{2,1,0:T(8,128)(2,1)S(1)}, bf16[2,16,1024]{2,1,0:T(8,128)(2,1)S(1)}, u32[]{:S(2)}, u32[]{:S(2)}) collective-permute-start(bf16[2,16,1024]{2,1,0:T(8,128)(2,1)S(1)} %get-tuple-element.132), channel_id=1, source_target_pairs={{24,0},{28,4},{32,8},{36,12},{40,16},{44,20},{48,24},{52,28},{56,3... | collective-permute-start | bytes 196616 | tf_op jit(solution)/shard_map/ppermute | solution.py:19
  516.8 16.7 %collective-permute-start.37 = (bf16[2,16,1024]{2,1,0:T(8,128)(2,1)S(1)}, bf16[2,16,1024]{2,1,0:T(8,128)(2,1)S(1)}, u32[]{:S(2)}, u32[]{:S(2)}) collective-permute-start(bf16[2,16,1024]{2,1,0:T(8,128)(2,1)S(1)} %get-tuple-element.133), channel_id=1, source_target_pairs={{20,0},{24,4},{28,8},{32,12},{36,16},{40,20},{44,24},{48,28},{52,3... | collective-permute-start | bytes 196616 | tf_op jit(solution)/shard_map/ppermute | solution.py:19
  521.4 17.9 %collective-permute-start.34 = (bf16[2,32,1024]{2,1,0:T(8,128)(2,1)S(1)}, bf16[2,32,1024]{2,1,0:T(8,128)(2,1)S(1)}, u32[]{:S(2)}, u32[]{:S(2)}) collective-permute-start(bf16[2,32,1024]{2,1,0:T(8,128)(2,1)S(1)} %get-tuple-element.128), channel_id=1, source_target_pairs={{0,8},{4,12},{8,16},{12,20},{16,24},{20,28},{24,32},{28,36},{32,40... | collective-permute-start | bytes 393224 | tf_op jit(solution)/shard_map/ppermute | solution.py:19
  526.0 22.9 %collective-permute-start.31 = (bf16[2,64,1024]{2,1,0:T(8,128)(2,1)S(1)}, bf16[2,64,1024]{2,1,0:T(8,128)(2,1)S(1)}, u32[]{:S(2)}, u32[]{:S(2)}) collective-permute-start(bf16[2,64,1024]{2,1,0:T(8,128)(2,1)S(1)} %pad_maximum_fusion.1), channel_id=1, source_target_pairs={{0,4},{4,8},{8,12},{12,16},{16,20},{20,24},{24,28},{28,32},{32,36}... | collective-permute-start | bytes 786440 | tf_op jit(solution)/shard_map/ppermute | solution.py:19
  528.5 20.4 %collective-permute-start.30 = (bf16[2,64,1024]{2,1,0:T(8,128)(2,1)S(1)}, bf16[2,64,1024]{2,1,0:T(8,128)(2,1)}, u32[]{:S(2)}, u32[]{:S(2)}) collective-permute-start(bf16[2,64,1024]{2,1,0:T(8,128)(2,1)S(1)} %pad_maximum_fusion), channel_id=1, source_target_pairs={{4,0},{8,4},{12,8},{16,12},{20,16},{24,20},{28,24},{32,28},{36,32}... | collective-permute-start | bytes 786440 | tf_op jit(solution)/shard_map/ppermute | solution.py:19
  530.4 11.2 %collective-permute-start.35 = (bf16[2,32,1024]{2,1,0:T(8,128)(2,1)S(1)}, bf16[2,32,1024]{2,1,0:T(8,128)(2,1)S(1)}, u32[]{:S(2)}, u32[]{:S(2)}) collective-permute-start(bf16[2,32,1024]{2,1,0:T(8,128)(2,1)S(1)} %get-tuple-element.129), channel_id=1, source_target_pairs={{0,12},{4,16},{8,20},{12,24},{16,28},{20,32},{24,36},{28,40},{32,4... | collective-permute-start | bytes 393224 | tf_op jit(solution)/shard_map/ppermute | solution.py:19
  533.5 8.5 %collective-permute-start.32 = (bf16[2,32,1024]{2,1,0:T(8,128)(2,1)S(1)}, bf16[2,32,1024]{2,1,0:T(8,128)(2,1)S(1)}, u32[]{:S(2)}, u32[]{:S(2)}) collective-permute-start(bf16[2,32,1024]{2,1,0:T(8,128)(2,1)S(1)} %get-tuple-element.126), channel_id=1, source_target_pairs={{8,0},{12,4},{16,8},{20,12},{24,16},{28,20},{32,24},{36,28},{40,32... | collective-permute-start | bytes 393224 | tf_op jit(solution)/shard_map/ppermute | solution.py:19
  539.3 8.2 %collective-permute-start.33 = (bf16[2,32,1024]{2,1,0:T(8,128)(2,1)S(1)}, bf16[2,32,1024]{2,1,0:T(8,128)(2,1)S(1)}, u32[]{:S(2)}, u32[]{:S(2)}) collective-permute-start(bf16[2,32,1024]{2,1,0:T(8,128)(2,1)S(1)} %get-tuple-element.127), channel_id=1, source_target_pairs={{12,0},{16,4},{20,8},{24,12},{28,16},{32,20},{36,24},{40,28},{44,3... | collective-permute-start | bytes 393224 | tf_op jit(solution)/shard_map/ppermute | solution.py:19
  (42 other events, 343.3 us)
where the time goes:
time: 556 us; the launch traced here: 552 us
  starting transfers between devices  318 us (57%)
  waiting for transfers between devices  136 us (24%)
  matrix products  62 us (11%)
  local copies, waits for them, and re-layouts  22.5 us (4%)
  other arithmetic  10.7 us (2%)
    ppermute x60, starting transfers between devices, shifted(): return lax.ppermute(shard, axis, pairs)  309 us
    ppermute x60, waiting for transfers between devices, shifted(): return lax.ppermute(shard, axis, pairs)  136 us
    dot_general x8, matrix products, head_pass(): jnp.einsum('qe,ke->qk', cotangent_part, value_part, preferred_element_typ...  17.1 us
    dot_general x8, matrix products, head_pass(): jnp.einsum('qk,qe->ke', weights_low, cotangent_part, preferred_element_ty...  13.9 us
    dot_general x8, matrix products, head_pass(): jnp.einsum('qk,ke->qe', score_grad, key_part, preferred_element_type=jnp....  13.8 us
    unnamed x160, local copies, waits for them, and re-layouts  12.2 us
  transfers between devices with their start and end apart: 62, of which 27 were waited for; matrix products, arithmetic and copies ran while one was open for 8% of the time, Pallas kernels for 0%

commit v1 on v0

v1 whole, which is shorter than its diff:
```python
import math

import jax
import jax.numpy as jnp
import numpy as np
from jax import lax
from jax.experimental import pallas as pl
from jax.experimental.pallas import tpu as pltpu
from jax.sharding import PartitionSpec as P

HEAD_DIM = 128
BLOCK = 128
BLOCKS = 128
LOG_TWO = math.log(2.0)
MASKED = -1e30
SCALE = 1.0 / math.sqrt(HEAD_DIM)
VMEM = 56 * 1024 * 1024

SIDE_LEVELS = [1] + [2] * 2 + [3] * 4 + [4] * 8


def _place(matrix, row, col, rows, factor):
    for r in range(rows):
        matrix[row + r, col + r * factor : col + (r + 1) * factor] = 1.0 / factor


def _own_matrix():
    m = np.zeros((240, 256), np.float32)
    row = 0
    for level in range(1, 5):
        for block in range(2):
            rows = BLOCK >> level
            _place(m, row, block * BLOCK, rows, 1 << level)
            row += rows
    return m


def _derive_matrix():
    m = np.zeros((192, 256), np.float32)
    _place(m, 0, 0, 32, 2)
    _place(m, 32, 64, 32, 1)
    _place(m, 64, 96, 16, 2)
    _place(m, 80, 128, 48, 1)
    _place(m, 128, 176, 8, 2)
    _place(m, 136, 192, 56, 1)
    return m


def _second_matrix(right):
    m = np.zeros((96, 224), np.float32)
    ahead, behind = (96, 0) if right else (0, 96)
    near, far = (208, 192) if right else (192, 208)
    _place(m, 0, ahead + 64, 32, 1)
    _place(m, 32, ahead, 16, 4)
    _place(m, 48, near, 16, 1)
    _place(m, 64, far, 16, 1)
    _place(m, 80, behind, 16, 4)
    return m


def _third_matrix(right):
    m = np.zeros((64, 208), np.float32)
    _place(m, 0, 192 if right else 200, 8, 1)
    _place(m, 8, 0, 8, 8)
    _place(m, 16, 64, 8, 4)
    _place(m, 24, 96, 8, 4)
    for i in range(4):
        _place(m, 32 + 8 * i, 128 + 16 * i, 8, 2)
    return m


def _final_matrix():
    own = _own_matrix()
    a1, b1, a2, b2 = own[0:64], own[64:128], own[128:160], own[160:192]
    a3, b3, a4, b4 = own[192:208], own[208:224], own[224:232], own[232:240]
    m = np.zeros((512, 256), np.float32)
    m[0:64], m[64:96] = b1, a2
    m[96:160], m[160:192] = a1, b2
    m[192 + 48 : 192 + 64], m[192 + 64 : 192 + 80] = b3, a3
    m[288 + 48 : 288 + 64], m[288 + 64 : 288 + 80] = a3, b3
    m[384:392] = a4
    m[448:456] = b4
    return m.T.copy()


def _bias_tables():
    side = [(k + 1, lv) for k, lv in enumerate(SIDE_LEVELS) for _ in range(BLOCK >> lv)]
    derived = [(k, lv) for k, lv in zip(range(1, 15), SIDE_LEVELS[1:], strict=True) for _ in range(BLOCK >> lv)]
    a = [(0, 0)] * 128 + [(1, 1)] * 64 + [(1 + k, lv) for k, lv in derived] + [(-k, lv) for k, lv in side]
    b = [(1, 0)] * 128 + [(0, 1)] * 64 + [(-k, lv) for k, lv in derived] + [(1 + k, lv) for k, lv in side]
    table = np.array([a, b], np.int32)
    return table[..., 0], table[..., 1].astype(np.float32) * LOG_TWO


def _bf(m):
    return jnp.asarray(m, jnp.bfloat16)


def _dot(a, b):
    return jnp.dot(a, b, preferred_element_type=jnp.float32)


def _pull(a, b):
    return lax.dot_general(a, b, (((0,), (0,)), ((), ())), preferred_element_type=jnp.float32)


def _outer(a, b):
    return lax.dot_general(a, b, (((1,), (1,)), ((), ())), preferred_element_type=jnp.float32)


def pack_first(core_ref, k_ref, v_ref, own_ref, right_ref, left_ref, one_ref, coarse_ref):
    for part, ref in enumerate((k_ref, v_ref)):
        rows = jnp.concatenate([ref[0], ref[1]], axis=0)
        levels = _dot(own_ref[...], rows).astype(jnp.bfloat16)
        one_ref[part] = levels[0:128]
        right_ref[part] = jnp.concatenate([levels[64:128], levels[128:160]], axis=0)
        left_ref[part] = jnp.concatenate([levels[0:64], levels[160:192]], axis=0)
        coarse_ref[part] = levels[192:240]


def pack_second(l1_ref, r1_ref, coarse_ref, wr_ref, wl_ref, right_ref, left_ref):
    for part in range(2):
        rows = jnp.concatenate([l1_ref[part], r1_ref[part], coarse_ref[part, 0:32]], axis=0)
        right_ref[part] = _dot(wr_ref[...], rows).astype(jnp.bfloat16)
        left_ref[part] = _dot(wl_ref[...], rows).astype(jnp.bfloat16)


def pack_third(l1_ref, r1_ref, l2_ref, r2_ref, coarse_ref, wr_ref, wl_ref, right_ref, left_ref):
    for part in range(2):
        own = coarse_ref[part, 32:48]
        rows = jnp.concatenate([l1_ref[part], l2_ref[part], own], axis=0)
        right_ref[part] = _dot(wr_ref[...], rows).astype(jnp.bfloat16)
        rows = jnp.concatenate([r1_ref[part], r2_ref[part], own], axis=0)
        left_ref[part] = _dot(wl_ref[...], rows).astype(jnp.bfloat16)


def attend(
    core_ref, q_ref, k_ref, v_ref, do_ref, one_ref, l1_ref, l2_ref, l3_ref, r1_ref, r2_ref, r3_ref,
    derive_ref, derive_t_ref, spread_ref, bias_ref,
    o_ref, dq_ref, own_ref, gl_ref, gr_ref, gl3_ref, gr3_ref,
):
    left, right, set_a, set_b = [], [], [], []
    for part, ref in enumerate((k_ref, v_ref)):
        lt = jnp.concatenate([l1_ref[part], l2_ref[part], l3_ref[part]], axis=0)
        rt = jnp.concatenate([r1_ref[part], r2_ref[part], r3_ref[part]], axis=0)
        lt_derived = _dot(derive_ref[...], lt).astype(jnp.bfloat16)
        rt_derived = _dot(derive_ref[...], rt).astype(jnp.bfloat16)
        set_a.append(jnp.concatenate([ref[0], one_ref[part, 64:128], rt_derived, lt], axis=0))
        set_b.append(jnp.concatenate([ref[1], one_ref[part, 0:64], lt_derived, rt], axis=0))
    grads = []
    for block, (keys, values) in enumerate((set_a, set_b)):
        q = q_ref[block]
        do = do_ref[block * BLOCK : (block + 1) * BLOCK]
        scores = _outer(q, keys) * SCALE + bias_ref[block : block + 1]
        highest = jnp.max(scores, axis=1, keepdims=True)
        raised = jnp.exp(scores - highest)
        weights = raised * (1.0 / jnp.sum(raised, axis=1, keepdims=True))
        low = weights.astype(jnp.bfloat16)
        o_ref[block * BLOCK : (block + 1) * BLOCK] = _dot(low, values).astype(jnp.bfloat16)
        weight_grad = _outer(do, values)
        row_term = jnp.sum(weights * weight_grad, axis=1, keepdims=True)
        score_grad = (weights * ((weight_grad - row_term) * SCALE)).astype(jnp.bfloat16)
        dq_ref[block * BLOCK : (block + 1) * BLOCK] = _dot(score_grad, keys).astype(jnp.bfloat16)
        grads.append((_pull(score_grad, q), _pull(low, do)))
    for part in range(2):
        ga, gb = grads[0][part], grads[1][part]
        g_left = ga[384:640] + _dot(derive_t_ref[...], gb[192:384].astype(jnp.bfloat16))
        g_right = gb[384:640] + _dot(derive_t_ref[...], ga[192:384].astype(jnp.bfloat16))
        gl_ref[part] = g_left[0:192]
        gr_ref[part] = g_right[0:192]
        gl3_ref[part] = g_left[192:256].astype(jnp.bfloat16)
        gr3_ref[part] = g_right[192:256].astype(jnp.bfloat16)
        ones = jnp.concatenate([gb[128:192], ga[128:192]], axis=0).astype(jnp.bfloat16)
        own_ref[part] = jnp.concatenate([ga[0:128], gb[0:128]], axis=0) + _dot(spread_ref[...], ones)


def fold_third(gl_ref, gr_ref, fr_ref, fl_ref, w_ref, gl1_ref, gr1_ref, gl2_ref, gr2_ref):
    for part in range(2):
        g = gl_ref[part] + _dot(w_ref[...], fr_ref[part])
        gl1_ref[part] = g[0:96]
        gl2_ref[part] = g[96:192].astype(jnp.bfloat16)
        g = gr_ref[part] + _dot(w_ref[...], fl_ref[part])
        gr1_ref[part] = g[0:96]
        gr2_ref[part] = g[96:192].astype(jnp.bfloat16)


def fold_second(gl1_ref, gr1_ref, fr_ref, fl_ref, w_ref, gl_ref, gr_ref):
    for part in range(2):
        g = _dot(w_ref[...], jnp.concatenate([fr_ref[part], fl_ref[part]], axis=0))
        gl_ref[part] = (gl1_ref[part] + g[0:96]).astype(jnp.bfloat16)
        gr_ref[part] = (gr1_ref[part] + g[96:192]).astype(jnp.bfloat16)


def fold_own(own_ref, f1r, f1l, f2r, f2l, f3r, f3l, w_ref, out_ref):
    for part in range(2):
        rows = jnp.concatenate([f[part] for f in (f1r, f1l, f2r, f2l, f3r, f3l)], axis=0)
        out_ref[part] = (own_ref[part] + _dot(w_ref[...], rows)).astype(jnp.bfloat16)


def _whole(body, outs, *args):
    return pl.pallas_call(
        body,
        out_shape=[jax.ShapeDtypeStruct(s, d) for s, d in outs],
        compiler_params=pltpu.CompilerParams(vmem_limit_bytes=VMEM),
    )(*args)


def local(queries, key_states, value_states, cotangent):
    bf16, f32 = jnp.bfloat16, jnp.float32
    size = lax.axis_size("seq")
    seq = lax.axis_index("seq")
    core = lax.rem(seq, 2)
    half = queries.shape[1] // 2
    heads = half // HEAD_DIM
    n_head = lax.axis_size("head")
    chip_cores = [[2 * i, 2 * i + 1] for i in range(size // 2)]
    chip_groups = [[g * 2 * n_head + m for m in range(2 * n_head)] for g in range(size // 2)]

    def hop(x, chips):
        return lax.ppermute(x, "seq", [(i, (i + 2 * chips) % size) for i in range(size)])

    def both_cores(x):
        return lax.all_gather(x, "seq", axis=0, axis_index_groups=chip_cores)

    split = cotangent.reshape(-1, n_head, 2, half).transpose(2, 1, 0, 3).reshape(2 * n_head, -1, half)
    do = lax.all_to_all(split, ("seq", "head"), 0, 0, axis_index_groups=chip_groups, tiled=True)
    do = do.reshape(2 * BLOCK, half)

    keys, values, quest = both_cores(key_states), both_cores(value_states), both_cores(queries)
    core_arg = core.reshape(1).astype(jnp.int32)

    def rows_out(n, dtype=bf16):
        return ((2, n, half), dtype)

    pick = pl.BlockSpec((2, BLOCK, half), lambda i, c: (0, 0, c[0]))
    whole = lambda n: pl.BlockSpec((2, n, half), lambda i, c: (0, 0, 0))
    p1r, p1l, ones, coarse = pl.pallas_call(
        pack_first,
        out_shape=[jax.ShapeDtypeStruct(*rows_out(n)) for n in (96, 96, 128, 48)],
        grid_spec=pltpu.PrefetchScalarGridSpec(
            num_scalar_prefetch=1,
            grid=(1,),
            in_specs=[pick, pick, pl.BlockSpec((240, 256), lambda i, c: (0, 0))],
            out_specs=[whole(n) for n in (96, 96, 128, 48)],
        ),
        compiler_params=pltpu.CompilerParams(vmem_limit_bytes=VMEM),
    )(core_arg, keys, values, _bf(_own_matrix()))

    l1, r1 = hop(p1r, 1), hop(p1l, -1)
    w2r, w2l = _second_matrix(True), _second_matrix(False)
    p2r, p2l = _whole(pack_second, [rows_out(96)] * 2, l1, r1, coarse, _bf(w2r), _bf(w2l))
    l2, r2 = hop(p2r, 3), hop(p2l, -3)
    w3r, w3l = _third_matrix(True), _third_matrix(False)
    p3r, p3l = _whole(pack_third, [rows_out(64)] * 2, l1, r1, l2, r2, coarse, _bf(w3r), _bf(w3l))
    l3, r3 = hop(p3r, 4), hop(p3l, -4)

    offsets, raise_by = _bias_tables()
    target = seq - core + jnp.asarray(offsets)
    bias = jnp.where((target >= 0) & (target < size), jnp.asarray(raise_by, f32), MASKED).astype(f32)

    def cut(n):
        return pl.BlockSpec((2, n, HEAD_DIM), lambda h, c: (0, 0, h))

    mine = pl.BlockSpec((2, BLOCK, HEAD_DIM), lambda h, c: (0, 0, c[0] * heads + h))
    flat = pl.BlockSpec((2 * BLOCK, HEAD_DIM), lambda h, c: (0, h))
    const = lambda *s: pl.BlockSpec(s, lambda h, c: (0,) * len(s))
    derive = _derive_matrix()
    spread = _own_matrix()[0:128].T.copy()
    attended, dq, own, gl, gr, gl3, gr3 = pl.pallas_call(
        attend,
        out_shape=[jax.ShapeDtypeStruct((2 * BLOCK, half), bf16)] * 2
        + [jax.ShapeDtypeStruct(*rows_out(n, d)) for n, d in ((256, f32), (192, f32), (192, f32), (64, bf16), (64, bf16))],
        grid_spec=pltpu.PrefetchScalarGridSpec(
            num_scalar_prefetch=1,
            grid=(heads,),
            in_specs=[mine, mine, mine, flat, cut(128)]
            + [cut(96), cut(96), cut(64)] * 2
            + [const(192, 256), const(256, 192), const(256, 128), const(2, 640)],
            out_specs=[flat, flat, cut(256), cut(192), cut(192), cut(64), cut(64)],
        ),
        compiler_params=pltpu.CompilerParams(vmem_limit_bytes=VMEM),
    )(
        core_arg, quest, keys, values, do, ones, l1, l2, l3, r1, r2, r3,
        _bf(derive), _bf(derive.T.copy()), _bf(spread), bias,
    )

    f3l, f3r = hop(gr3, 4), hop(gl3, -4)
    w3t = w3r[:, 0:192].T.copy()
    gl1, gr1, gl2, gr2 = _whole(
        fold_third, [rows_out(96, f32)] * 2 + [rows_out(96)] * 2, gl, gr, f3r, f3l, _bf(w3t)
    )
    f2l, f2r = hop(gr2, 3), hop(gl2, -3)
    w2t = np.concatenate([w2r[:, 0:192], w2l[:, 0:192]], axis=0).T.copy()
    s1l, s1r = _whole(fold_second, [rows_out(96)] * 2, gl1, gr1, f2r, f2l, _bf(w2t))
    f1l, f1r = hop(s1r, 1), hop(s1l, -1)
    (own,) = _whole(fold_own, [rows_out(256)], own, f1r, f1l, f2r, f2l, f3r, f3l, _bf(_final_matrix()))

    out = lax.all_to_all(
        attended.reshape(2 * n_head, -1, half), ("seq", "head"), 0, 0, axis_index_groups=chip_groups, tiled=True
    )
    out = out.reshape(2, n_head, -1, half).transpose(2, 1, 0, 3).reshape(-1, n_head * 2 * half)

    grads = jnp.concatenate([own, dq[None]], axis=0).reshape(3, 2, BLOCK, half)
    keep = lax.dynamic_index_in_dim(grads, core, 1, keepdims=False)
    give = lax.dynamic_index_in_dim(grads, 1 - core, 1, keepdims=False)
    take = lax.ppermute(give, "seq", [(i, i ^ 1) for i in range(size)])
    low = jnp.where(core == 0, keep, take)
    high = jnp.where(core == 0, take, keep)
    full = jnp.concatenate([low, high], axis=2)
    return (out, full[2], full[0], full[1])


def solution(mesh):
    placed = (P("seq", "head"), P("seq", "head"), P("seq", "head"), P(("seq", "head"), None))
    return jax.shard_map(
        local,
        mesh=mesh,
        in_specs=placed,
        out_specs=(P(("seq", "head"), None), P("seq", "head"), P("seq", "head"), P("seq", "head")),
        check_vma=False,
    )
```

time: 556 us -> 181 us (0.33)
  the two profiles are of different devices: /device:TPU:27 before, /device:TPU:1 now
where the time goes in v1:
time: 181 us; the launch traced here: 180 us
  starting transfers between devices  80.9 us (45%)
  waiting for transfers between devices  44.8 us (25%)
  Pallas kernels  25.6 us (14%)
  blocking collectives  18.9 us (10%)
  local copies, waits for them, and re-layouts  6.32 us (3%)
  other arithmetic  2.55 us (1%)
    ppermute x12, starting transfers between devices, hop(): lax.ppermute(x, 'seq', [(i, (i + 2 * chips) % size) for i in range(size)])  67.4 us
    ppermute x12, waiting for transfers between devices, hop(): lax.ppermute(x, 'seq', [(i, (i + 2 * chips) % size) for i in range(size)])  38.2 us
    all_gather x3, blocking collectives, both_cores(): return lax.all_gather(x, 'seq', axis=0, axis_index_groups=chip_cores)  18.9 us
    pallas_call x5, Pallas kernels, _whole(): pl.pallas_call(body, out_shape=[jax.ShapeDtypeStruct(s, d) for s, d in ou...  12.2 us
    pallas_call x1, Pallas kernels, local(): pl.pallas_call(attend, out_shape=[jax.ShapeDtypeStruct((2 * BLOCK, half),...  11.2 us
    all_to_all x1, waiting for transfers between devices, local(): lax.all_to_all(attended.reshape(2 * n_head, -1, half), ('seq', 'head'), 0...  6.56 us
    ppermute x1, starting transfers between devices, local(): take = lax.ppermute(give, 'seq', [(i, i ^ 1) for i in range(size)])  5.12 us
    all_to_all x1, starting transfers between devices, local(): lax.all_to_all(split, ('seq', 'head'), 0, 0, axis_index_groups=chip_group...  4.73 us
  transfers between devices with their start and end apart: 15, of which 9 were waited for; matrix products, arithmetic and copies ran while one was open for 2% of the time, Pallas kernels for 2%

profile of v1, /device:TPU:1, one launch (start us, length us, event | category | flops | bytes accessed | tf_op | source)
XLA Modules:
  0.0 179.9 jit_solution(288222959391303463)
XLA Ops:
  0.6 0.0 copy-start.11
  0.6 10.7 %all-gather.1 = bf16[256,1024]{1,0:T(8,128)(2,1)} all-gather(bf16[128,1024]{1,0:T(8,128)(2,1)} %param.18), channel_id=3, replica_groups={{0,4},{8,12},{16,20},{24,28},{32,36},{40,44},{48,52},{56,60},{64,68},{7..., dimensions={0}, use_global_device_ids=true | all-gather | bytes 786432 | tf_op jit(solution)/shard_map/all_gather | solution.py:223
  11.3 0.0 copy-done.11
  11.4 2.3 %all-gather.2 = bf16[256,1024]{1,0:T(8,128)(2,1)} all-gather(bf16[128,1024]{1,0:T(8,128)(2,1)S(1)} %copy-done.11), channel_id=4, replica_groups={{0,4},{8,12},{16,20},{24,28},{32,36},{40,44},{48,52},{56,60},{64,68},{7..., dimensions={0}, use_global_device_ids=true | all-gather | bytes 786432 | tf_op jit(solution)/shard_map/all_gather | solution.py:223
  13.7 2.2 %shard_map.192 = (bf16[2,96,512]{2,1,0:T(8,128)(2,1)}, bf16[2,96,512]{2,1,0:T(8,128)(2,1)}, bf16[2,128,512]{2,1,0:T(8,128)(2,1)}, bf16[2,48,512]{2,1,0:T(8,128)(2,1)}) custom-call(s32[1]{0:T(128)} %bitcast.core_ref, bf16[2,128,1024]{2,1,0:T(8,128)(2,1)} %bitcast.30, bf16[2,128,1024]{2,1,0:T(8,128)(2,1)} %bitcast.32, bf16[240,256]{1,0:T(8,128)(2,1)} %constant.53.clone.own_ref), custom_call_target="tpu_custom_call" | custom-call | tf_op jit(solution)/shard_map/pallas_call | solution.py:237
  15.9 1.9 %collective-permute-start = (bf16[2,96,512]{2,1,0:T(8,128)(2,1)}, bf16[2,96,512]{2,1,0:T(8,128)(2,1)S(1)}, u32[]{:S(2)}, u32[]{:S(2)}) collective-permute-start(bf16[2,96,512]{2,1,0:T(8,128)(2,1)} %get-tuple-element.26), channel_id=1, source_target_pairs={{0,8},{4,12},{8,16},{12,20},{16,24},{20,28},{24,32},{28,36},{32,40... | collective-permute-start | bytes 589832 | tf_op jit(solution)/shard_map/ppermute | solution.py:220
  17.8 8.2 %collective-permute-start.1 = (bf16[2,96,512]{2,1,0:T(8,128)(2,1)}, bf16[2,96,512]{2,1,0:T(8,128)(2,1)S(1)}, u32[]{:S(2)}, u32[]{:S(2)}) collective-permute-start(bf16[2,96,512]{2,1,0:T(8,128)(2,1)} %get-tuple-element.27), channel_id=1, source_target_pairs={{0,504},{4,508},{8,0},{12,4},{16,8},{20,12},{24,16},{28,20},{32,24... | collective-permute-start | bytes 589832 | tf_op jit(solution)/shard_map/ppermute | solution.py:220
  26.0 0.0 copy-done.13
  26.0 0.2 reshape.34
  26.2 0.8 copy.21
  27.0 4.7 %all-to-all-start = ((bf16[8,32,512]{2,1,0:T(8,128)(2,1)}), bf16[8,32,512]{2,1,0:T(8,128)(2,1)S(1)}, u32[]{:S(2)}, u32[]{:S(2)}) async-start(bf16[8,32,512]{2,1,0:T(8,128)(2,1)} %bitcast.5), calls=%async_computation | async-start | bytes 524288 | tf_op jit(solution)/shard_map/all_to_all | solution.py:226
  31.7 0.0 collective-permute-done.l1_ref
  31.7 0.0 collective-permute-done.1.r1_ref
  31.7 0.0 copy-start.2
  31.7 0.7 copy-done.1
  32.4 0.1 copy-done.2
  32.5 2.1 %shard_map.193 = (bf16[2,96,512]{2,1,0:T(8,128)(2,1)}, bf16[2,96,512]{2,1,0:T(8,128)(2,1)}) custom-call(bf16[2,96,512]{2,1,0:T(8,128)(2,1)} %copy-done.1, bf16[2,96,512]{2,1,0:T(8,128)(2,1)} %copy-done.2, bf16[2,48,512]{2,1,0:T(8,128)(2,1)} %get-tuple-element.28.coarse_ref, bf16[96,224]{1,0:T(8,128)(2,1)} %constant.54.clone.wr_ref, ...), custom_call_target="tpu_custom_call" | custom-call | tf_op jit(solution)/shard_map/pallas_call | solution.py:201
  34.6 1.9 %collective-permute-start.2 = (bf16[2,96,512]{2,1,0:T(8,128)(2,1)}, bf16[2,96,512]{2,1,0:T(8,128)(2,1)S(1)}, u32[]{:S(2)}, u32[]{:S(2)}) collective-permute-start(bf16[2,96,512]{2,1,0:T(8,128)(2,1)} %get-tuple-element.29), channel_id=1, source_target_pairs={{0,24},{4,28},{8,32},{12,36},{16,40},{20,44},{24,48},{28,52},{32,5... | collective-permute-start | bytes 589832 | tf_op jit(solution)/shard_map/ppermute | solution.py:220
  36.5 8.5 %collective-permute-start.3 = (bf16[2,96,512]{2,1,0:T(8,128)(2,1)}, bf16[2,96,512]{2,1,0:T(8,128)(2,1)S(1)}, u32[]{:S(2)}, u32[]{:S(2)}) collective-permute-start(bf16[2,96,512]{2,1,0:T(8,128)(2,1)} %get-tuple-element.30), channel_id=1, source_target_pairs={{0,488},{4,492},{8,496},{12,500},{16,504},{20,508},{24,0},{28,4},{... | collective-permute-start | bytes 589832 | tf_op jit(solution)/shard_map/ppermute | solution.py:220
  45.0 0.0 copy-done.18
  45.0 0.6 and_select_fusion.bias_ref
  45.6 6.6 %collective-permute-done.2.l2_ref = bf16[2,96,512]{2,1,0:T(8,128)(2,1)S(1)} collective-permute-done((bf16[2,96,512]{2,1,0:T(8,128)(2,1)}, bf16[2,96,512]{2,1,0:T(8,128)(2,1)S(1)}, u32[]{:S(2)}, u32[]{:S(2)}) %collective-permute-start.2) | collective-permute-done | bytes 196640 | tf_op jit(solution)/shard_map/ppermute | solution.py:220
  52.2 0.9 collective-permute-done.3.r2_ref
  53.0 0.7 copy-done.8
  53.7 2.2 %shard_map.194 = (bf16[2,64,512]{2,1,0:T(8,128)(2,1)}, bf16[2,64,512]{2,1,0:T(8,128)(2,1)}) custom-call(bf16[2,96,512]{2,1,0:T(8,128)(2,1)} %copy-done.1, bf16[2,96,512]{2,1,0:T(8,128)(2,1)} %copy-done.2, bf16[2,96,512]{2,1,0:T(8,128)(2,1)} %copy-done.7, bf16[2,96,512]{2,1,0:T(8,128)(2,1)} %copy-done.8, bf16[2,48,512]{2,1,0:T(8,128)(2,1)} %get-tuple-element.28.coarse_ref, ...), custom_call_target="tpu_custom_call" | custom-call | tf_op jit(solution)/shard_map/pallas_call | solution.py:201
  55.9 6.4 %collective-permute-start.4 = (bf16[2,64,512]{2,1,0:T(8,128)(2,1)}, bf16[2,64,512]{2,1,0:T(8,128)(2,1)S(1)}, u32[]{:S(2)}, u32[]{:S(2)}) collective-permute-start(bf16[2,64,512]{2,1,0:T(8,128)(2,1)} %get-tuple-element.31), channel_id=1, source_target_pairs={{0,32},{4,36},{8,40},{12,44},{16,48},{20,52},{24,56},{28,60},{32,6... | collective-permute-start | bytes 393224 | tf_op jit(solution)/shard_map/ppermute | solution.py:220
  62.3 4.9 %collective-permute-start.5 = (bf16[2,64,512]{2,1,0:T(8,128)(2,1)}, bf16[2,64,512]{2,1,0:T(8,128)(2,1)S(1)}, u32[]{:S(2)}, u32[]{:S(2)}) collective-permute-start(bf16[2,64,512]{2,1,0:T(8,128)(2,1)} %get-tuple-element.32), channel_id=1, source_target_pairs={{0,480},{4,484},{8,488},{12,492},{16,496},{20,500},{24,504},{28,50... | collective-permute-start | bytes 393224 | tf_op jit(solution)/shard_map/ppermute | solution.py:220
  67.2 5.9 %all-gather = bf16[256,1024]{1,0:T(8,128)(2,1)} all-gather(bf16[128,1024]{1,0:T(8,128)(2,1)S(1)} %copy-done.12), channel_id=2, replica_groups={{0,4},{8,12},{16,20},{24,28},{32,36},{40,44},{48,52},{56,60},{64,68},{7..., dimensions={0}, use_global_device_ids=true | all-gather | bytes 786432 | tf_op jit(solution)/shard_map/all_gather | solution.py:223
  73.1 0.0 all-to-all-done
  73.1 0.0 collective-permute-done.4.l3_ref
  73.2 0.0 collective-permute-done.5.r3_ref
  73.2 0.7 copy-done.4
  73.9 0.1 copy-done.16
  73.9 0.0 copy-done.17
  73.9 11.2 %shard_map.195 = (bf16[256,512]{1,0:T(8,128)(2,1)}, bf16[256,512]{1,0:T(8,128)(2,1)}, f32[2,256,512]{2,1,0:T(8,128)}, f32[2,192,512]{2,1,0:T(8,128)}, f32[2,192,...) custom-call(s32[1]{0:T(128)} %bitcast.core_ref, bf16[2,128,1024]{2,1,0:T(8,128)(2,1)} %bitcast.34, ...), custom_call_target="tpu_custom_call" | custom-call | tf_op jit(solution)/shard_map/pallas_call | solution.py:269
  85.1 8.9 %collective-permute-start.6 = (bf16[2,64,512]{2,1,0:T(8,128)(2,1)}, bf16[2,64,512]{2,1,0:T(8,128)(2,1)S(1)}, u32[]{:S(2)}, u32[]{:S(2)}) collective-permute-start(bf16[2,64,512]{2,1,0:T(8,128)(2,1)} %get-tuple-element.37), channel_id=1, source_target_pairs={{0,480},{4,484},{8,488},{12,492},{16,496},{20,500},{24,504},{28,50... | collective-permute-start | bytes 393224 | tf_op jit(solution)/shard_map/ppermute | solution.py:220
  94.1 1.9 %collective-permute-start.7 = (bf16[2,64,512]{2,1,0:T(8,128)(2,1)}, bf16[2,64,512]{2,1,0:T(8,128)(2,1)S(1)}, u32[]{:S(2)}, u32[]{:S(2)}) collective-permute-start(bf16[2,64,512]{2,1,0:T(8,128)(2,1)} %get-tuple-element.38), channel_id=1, source_target_pairs={{0,32},{4,36},{8,40},{12,44},{16,48},{20,52},{24,56},{28,60},{32,6... | collective-permute-start | bytes 393224 | tf_op jit(solution)/shard_map/ppermute | solution.py:220
  96.0 0.3 collective-permute-done.6.fr_ref.f3r
  96.3 11.1 %collective-permute-done.7.fl_ref.f3l = bf16[2,64,512]{2,1,0:T(8,128)(2,1)S(1)} collective-permute-done((bf16[2,64,512]{2,1,0:T(8,128)(2,1)}, bf16[2,64,512]{2,1,0:T(8,128)(2,1)S(1)}, u32[]{:S(2)}, u32[]{:S(2)}) %collective-permute-start.7) | collective-permute-done | bytes 131104 | tf_op jit(solution)/shard_map/ppermute | solution.py:220
  107.4 0.6 copy-done.10
  108.1 2.7 %shard_map.196 = (f32[2,96,512]{2,1,0:T(8,128)}, f32[2,96,512]{2,1,0:T(8,128)}, bf16[2,96,512]{2,1,0:T(8,128)(2,1)}, bf16[2,96,512]{2,1,0:T(8,128)(2,1)}) custom-call(f32[2,192,512]{2,1,0:T(8,128)} %get-tuple-element.35.gl_ref, f32[2,192,512]{2,1,0:T(8,128)} %get-tuple-element.36.gr_ref, bf16[2,64,512]{2,1,0:T(8,128)(2,1)} %copy-done.9, ...), custom_call_target="tpu_custom_call" | custom-call | tf_op jit(solution)/shard_map/pallas_call | solution.py:201
  110.7 12.1 %collective-permute-start.8 = (bf16[2,96,512]{2,1,0:T(8,128)(2,1)}, bf16[2,96,512]{2,1,0:T(8,128)(2,1)S(1)}, u32[]{:S(2)}, u32[]{:S(2)}) collective-permute-start(bf16[2,96,512]{2,1,0:T(8,128)(2,1)} %get-tuple-element.41), channel_id=1, source_target_pairs={{0,488},{4,492},{8,496},{12,500},{16,504},{20,508},{24,0},{28,4},{... | collective-permute-start | bytes 589832 | tf_op jit(solution)/shard_map/ppermute | solution.py:220
  122.8 4.1 %collective-permute-start.9 = (bf16[2,96,512]{2,1,0:T(8,128)(2,1)}, bf16[2,96,512]{2,1,0:T(8,128)(2,1)S(1)}, u32[]{:S(2)}, u32[]{:S(2)}) collective-permute-start(bf16[2,96,512]{2,1,0:T(8,128)(2,1)} %get-tuple-element.42), channel_id=1, source_target_pairs={{0,24},{4,28},{8,32},{12,36},{16,40},{20,44},{24,48},{28,52},{32,5... | collective-permute-start | bytes 589832 | tf_op jit(solution)/shard_map/ppermute | solution.py:220
  126.9 11.7 %collective-permute-done.8.fr_ref.f2r = bf16[2,96,512]{2,1,0:T(8,128)(2,1)S(1)} collective-permute-done((bf16[2,96,512]{2,1,0:T(8,128)(2,1)}, bf16[2,96,512]{2,1,0:T(8,128)(2,1)S(1)}, u32[]{:S(2)}, u32[]{:S(2)}) %collective-permute-start.8) | collective-permute-done | bytes 196640 | tf_op jit(solution)/shard_map/ppermute | solution.py:220
  138.5 0.1 collective-permute-done.9.fl_ref.f2l
  138.6 0.6 copy-done.5
  139.2 0.1 copy-done.6
  139.3 2.2 %shard_map.197 = (bf16[2,96,512]{2,1,0:T(8,128)(2,1)}, bf16[2,96,512]{2,1,0:T(8,128)(2,1)}) custom-call(f32[2,96,512]{2,1,0:T(8,128)} %get-tuple-element.39.gl1_ref, f32[2,96,512]{2,1,0:T(8,128)} %get-tuple-element.40.gr1_ref, bf16[2,96,512]{2,1,0:T(8,128)(2,1)} %copy-done.5, bf16[2,96,512]{2,1,0:T(8,128)(2,1)} %copy-done.6, ...), custom_call_target="tpu_custom_call" | custom-call | tf_op jit(solution)/shard_map/pallas_call | solution.py:201
  141.5 6.3 %collective-permute-start.10 = (bf16[2,96,512]{2,1,0:T(8,128)(2,1)}, bf16[2,96,512]{2,1,0:T(8,128)(2,1)S(1)}, u32[]{:S(2)}, u32[]{:S(2)}) collective-permute-start(bf16[2,96,512]{2,1,0:T(8,128)(2,1)} %get-tuple-element.43), channel_id=1, source_target_pairs={{0,504},{4,508},{8,0},{12,4},{16,8},{20,12},{24,16},{28,20},{32,24... | collective-permute-start | bytes 589832 | tf_op jit(solution)/shard_map/ppermute | solution.py:220
  147.9 2.3 %collective-permute-start.11 = (bf16[2,96,512]{2,1,0:T(8,128)(2,1)}, bf16[2,96,512]{2,1,0:T(8,128)(2,1)S(1)}, u32[]{:S(2)}, u32[]{:S(2)}) collective-permute-start(bf16[2,96,512]{2,1,0:T(8,128)(2,1)} %get-tuple-element.44), channel_id=1, source_target_pairs={{0,8},{4,12},{8,16},{12,20},{16,24},{20,28},{24,32},{28,36},{32,40... | collective-permute-start | bytes 589832 | tf_op jit(solution)/shard_map/ppermute | solution.py:220
  150.2 2.5 %collective-permute-done.10.f1r = bf16[2,96,512]{2,1,0:T(8,128)(2,1)S(1)} collective-permute-done((bf16[2,96,512]{2,1,0:T(8,128)(2,1)}, bf16[2,96,512]{2,1,0:T(8,128)(2,1)S(1)}, u32[]{:S(2)}, u32[]{:S(2)}) %collective-permute-start.10) | collective-permute-done | bytes 196640 | tf_op jit(solution)/shard_map/ppermute | solution.py:220
  152.7 5.1 %collective-permute-done.11.f1l = bf16[2,96,512]{2,1,0:T(8,128)(2,1)S(1)} collective-permute-done((bf16[2,96,512]{2,1,0:T(8,128)(2,1)}, bf16[2,96,512]{2,1,0:T(8,128)(2,1)S(1)}, u32[]{:S(2)}, u32[]{:S(2)}) %collective-permute-start.11) | collective-permute-done | bytes 196640 | tf_op jit(solution)/shard_map/ppermute | solution.py:220
  157.8 0.7 copy-done.15
  158.5 3.0 %shard_map.198 = bf16[2,256,512]{2,1,0:T(8,128)(2,1)} custom-call(f32[2,256,512]{2,1,0:T(8,128)} %get-tuple-element.34.own_ref, bf16[2,96,512]{2,1,0:T(8,128)(2,1)} %copy-done.14, bf16[2,96,512]{2,1,0:T(8,128)(2,1)} %copy-done.15, bf16[2,96,512]{2,1,0:T(8,128)(2,1)} %copy-done.5, bf16[2,96,512]{2,1,0:T(8,128)(2,1)} %copy-done.6, ...), custom_call_target="tpu_custom_call" | custom-call | tf_op jit(solution)/shard_map/pallas_call | solution.py:201
  161.5 1.0 fusion.1
  162.5 5.1 %collective-permute-start.12 = (bf16[3,128,512]{2,1,0:T(8,128)(2,1)S(1)}, bf16[3,128,512]{2,1,0:T(8,128)(2,1)S(1)}, u32[]{:S(2)}, u32[]{:S(2)}) collective-permute-start(bf16[3,128,512]{2,1,0:T(8,128)(2,1)S(1)} %fusion.1), channel_id=1, source_target_pairs={{0,4},{4,0},{8,12},{12,8},{16,20},{20,16},{24,28},{28,24},{32,36},... | collective-permute-start | bytes 1179656 | tf_op jit(solution)/shard_map/ppermute | solution.py:306
  167.6 3.6 %all-to-all-start.1 = ((bf16[8,32,512]{2,1,0:T(8,128)(2,1)}), bf16[8,32,512]{2,1,0:T(8,128)(2,1)S(1)}, u32[]{:S(2)}, u32[]{:S(2)}) async-start(bf16[8,32,512]{2,1,0:T(8,128)(2,1)} %bitcast.7), calls=%async_computation.1 | async-start | bytes 524288 | tf_op jit(solution)/shard_map/all_to_all | solution.py:298
  171.2 6.6 %all-to-all-done.1 = bf16[8,32,512]{2,1,0:T(8,128)(2,1)S(1)} async-done(((bf16[8,32,512]{2,1,0:T(8,128)(2,1)}), bf16[8,32,512]{2,1,0:T(8,128)(2,1)S(1)}, u32[]{:S(2)}, u32[]{:S(2)}) %all-to-all-start.1) | async-done | bytes 262176 | tf_op jit(solution)/shard_map/all_to_all | solution.py:298
  177.8 0.3 copy.24
  178.1 0.9 reshape.39
  178.9 0.0 collective-permute-done.12
  179.0 0.0 copy-done
  179.0 0.1 broadcast_select_fusion
  179.0 0.9 fusion.8
  (24 shorter events, 0.0 us)
Async XLA Ops:
  0.6 10.7 %copy-start.11 = (bf16[128,1024]{1,0:T(8,128)(2,1)S(1)}, bf16[128,1024]{1,0:T(8,128)(2,1)}, u32[]{:S(2)}) copy-start(bf16[128,1024]{1,0:T(8,128)(2,1)} %param.19) | copy-start | bytes 786436
  13.7 12.4 %copy-start.13 = (bf16[32,4096]{1,0:T(8,128)(2,1)S(1)}, bf16[32,4096]{1,0:T(8,128)(2,1)}, u32[]{:S(2)}) copy-start(bf16[32,4096]{1,0:T(8,128)(2,1)} %param.20) | copy-start | bytes 786436
  15.9 15.8 %collective-permute-start = (bf16[2,96,512]{2,1,0:T(8,128)(2,1)}, bf16[2,96,512]{2,1,0:T(8,128)(2,1)S(1)}, u32[]{:S(2)}, u32[]{:S(2)}) collective-permute-start(bf16[2,96,512]{2,1,0:T(8,128)(2,1)} %get-tuple-element.26), channel_id=1, source_target_pairs={{0,8},{4,12},{8,16},{12,20},{16,24},{20,28},{24,32},{28,36},{32,40... | collective-permute-start | bytes 589832 | tf_op jit(solution)/shard_map/ppermute | solution.py:220
  17.8 13.9 %collective-permute-start.1 = (bf16[2,96,512]{2,1,0:T(8,128)(2,1)}, bf16[2,96,512]{2,1,0:T(8,128)(2,1)S(1)}, u32[]{:S(2)}, u32[]{:S(2)}) collective-permute-start(bf16[2,96,512]{2,1,0:T(8,128)(2,1)} %get-tuple-element.27), channel_id=1, source_target_pairs={{0,504},{4,508},{8,0},{12,4},{16,8},{20,12},{24,16},{28,20},{32,24... | collective-permute-start | bytes 589832 | tf_op jit(solution)/shard_map/ppermute | solution.py:220
  27.0 46.2 %all-to-all-start = ((bf16[8,32,512]{2,1,0:T(8,128)(2,1)}), bf16[8,32,512]{2,1,0:T(8,128)(2,1)S(1)}, u32[]{:S(2)}, u32[]{:S(2)}) async-start(bf16[8,32,512]{2,1,0:T(8,128)(2,1)} %bitcast.5), calls=%async_computation | async-start | bytes 524288 | tf_op jit(solution)/shard_map/all_to_all | solution.py:226
  31.7 0.7 copy-start.1
  31.7 0.7 copy-start.2
  32.5 12.5 %copy-start.18 = (s32[2,640]{1,0:T(2,128)S(1)}, s32[2,640]{1,0:T(2,128)}, u32[]{:S(2)}) copy-start(s32[2,640]{1,0:T(2,128)} %constant.58.clone) | copy-start | bytes 15364
  32.5 12.5 %copy-start.19 = (f32[2,640]{1,0:T(2,128)S(1)}, f32[2,640]{1,0:T(2,128)}, u32[]{:S(2)}) copy-start(f32[2,640]{1,0:T(2,128)} %constant.59.clone) | copy-start | bytes 15364
  34.6 17.6 %collective-permute-start.2 = (bf16[2,96,512]{2,1,0:T(8,128)(2,1)}, bf16[2,96,512]{2,1,0:T(8,128)(2,1)S(1)}, u32[]{:S(2)}, u32[]{:S(2)}) collective-permute-start(bf16[2,96,512]{2,1,0:T(8,128)(2,1)} %get-tuple-element.29), channel_id=1, source_target_pairs={{0,24},{4,28},{8,32},{12,36},{16,40},{20,44},{24,48},{28,52},{32,5... | collective-permute-start | bytes 589832 | tf_op jit(solution)/shard_map/ppermute | solution.py:220
  36.5 16.5 %collective-permute-start.3 = (bf16[2,96,512]{2,1,0:T(8,128)(2,1)}, bf16[2,96,512]{2,1,0:T(8,128)(2,1)S(1)}, u32[]{:S(2)}, u32[]{:S(2)}) collective-permute-start(bf16[2,96,512]{2,1,0:T(8,128)(2,1)} %get-tuple-element.30), channel_id=1, source_target_pairs={{0,488},{4,492},{8,496},{12,500},{16,504},{20,508},{24,0},{28,4},{... | collective-permute-start | bytes 589832 | tf_op jit(solution)/shard_map/ppermute | solution.py:220
  45.6 21.6 %copy-start.12 = (bf16[128,1024]{1,0:T(8,128)(2,1)S(1)}, bf16[128,1024]{1,0:T(8,128)(2,1)}, u32[]{:S(2)}) copy-start(bf16[128,1024]{1,0:T(8,128)(2,1)} %param.17) | copy-start | bytes 786436
  52.2 0.9 copy-start.7
  53.0 0.7 copy-start.8
  55.9 17.2 %collective-permute-start.4 = (bf16[2,64,512]{2,1,0:T(8,128)(2,1)}, bf16[2,64,512]{2,1,0:T(8,128)(2,1)S(1)}, u32[]{:S(2)}, u32[]{:S(2)}) collective-permute-start(bf16[2,64,512]{2,1,0:T(8,128)(2,1)} %get-tuple-element.31), channel_id=1, source_target_pairs={{0,32},{4,36},{8,40},{12,44},{16,48},{20,52},{24,56},{28,60},{32,6... | collective-permute-start | bytes 393224 | tf_op jit(solution)/shard_map/ppermute | solution.py:220
  62.3 10.9 %collective-permute-start.5 = (bf16[2,64,512]{2,1,0:T(8,128)(2,1)}, bf16[2,64,512]{2,1,0:T(8,128)(2,1)S(1)}, u32[]{:S(2)}, u32[]{:S(2)}) collective-permute-start(bf16[2,64,512]{2,1,0:T(8,128)(2,1)} %get-tuple-element.32), channel_id=1, source_target_pairs={{0,480},{4,484},{8,488},{12,492},{16,496},{20,500},{24,504},{28,50... | collective-permute-start | bytes 393224 | tf_op jit(solution)/shard_map/ppermute | solution.py:220
  73.1 0.7 copy-start.4
  73.2 0.7 copy-start.16
  73.2 0.8 copy-start.17
  85.1 11.2 %collective-permute-start.6 = (bf16[2,64,512]{2,1,0:T(8,128)(2,1)}, bf16[2,64,512]{2,1,0:T(8,128)(2,1)S(1)}, u32[]{:S(2)}, u32[]{:S(2)}) collective-permute-start(bf16[2,64,512]{2,1,0:T(8,128)(2,1)} %get-tuple-element.37), channel_id=1, source_target_pairs={{0,480},{4,484},{8,488},{12,492},{16,496},{20,500},{24,504},{28,50... | collective-permute-start | bytes 393224 | tf_op jit(solution)/shard_map/ppermute | solution.py:220
  94.1 13.3 %collective-permute-start.7 = (bf16[2,64,512]{2,1,0:T(8,128)(2,1)}, bf16[2,64,512]{2,1,0:T(8,128)(2,1)S(1)}, u32[]{:S(2)}, u32[]{:S(2)}) collective-permute-start(bf16[2,64,512]{2,1,0:T(8,128)(2,1)} %get-tuple-element.38), channel_id=1, source_target_pairs={{0,32},{4,36},{8,40},{12,44},{16,48},{20,52},{24,56},{28,60},{32,6... | collective-permute-start | bytes 393224 | tf_op jit(solution)/shard_map/ppermute | solution.py:220
  96.3 11.1 %copy-start.9 = (bf16[2,64,512]{2,1,0:T(8,128)(2,1)}, bf16[2,64,512]{2,1,0:T(8,128)(2,1)S(1)}, u32[]{:S(2)}) copy-start(bf16[2,64,512]{2,1,0:T(8,128)(2,1)S(1)} %collective-permute-done.6.fr_ref.f3r) | copy-start | bytes 393220
  107.4 0.6 copy-start.10
  110.7 27.8 %collective-permute-start.8 = (bf16[2,96,512]{2,1,0:T(8,128)(2,1)}, bf16[2,96,512]{2,1,0:T(8,128)(2,1)S(1)}, u32[]{:S(2)}, u32[]{:S(2)}) collective-permute-start(bf16[2,96,512]{2,1,0:T(8,128)(2,1)} %get-tuple-element.41), channel_id=1, source_target_pairs={{0,488},{4,492},{8,496},{12,500},{16,504},{20,508},{24,0},{28,4},{... | collective-permute-start | bytes 589832 | tf_op jit(solution)/shard_map/ppermute | solution.py:220
  122.8 15.8 %collective-permute-start.9 = (bf16[2,96,512]{2,1,0:T(8,128)(2,1)}, bf16[2,96,512]{2,1,0:T(8,128)(2,1)S(1)}, u32[]{:S(2)}, u32[]{:S(2)}) collective-permute-start(bf16[2,96,512]{2,1,0:T(8,128)(2,1)} %get-tuple-element.42), channel_id=1, source_target_pairs={{0,24},{4,28},{8,32},{12,36},{16,40},{20,44},{24,48},{28,52},{32,5... | collective-permute-start | bytes 589832 | tf_op jit(solution)/shard_map/ppermute | solution.py:220
  138.5 0.7 copy-start.5
  138.6 0.7 copy-start.6
  141.5 11.2 %collective-permute-start.10 = (bf16[2,96,512]{2,1,0:T(8,128)(2,1)}, bf16[2,96,512]{2,1,0:T(8,128)(2,1)S(1)}, u32[]{:S(2)}, u32[]{:S(2)}) collective-permute-start(bf16[2,96,512]{2,1,0:T(8,128)(2,1)} %get-tuple-element.43), channel_id=1, source_target_pairs={{0,504},{4,508},{8,0},{12,4},{16,8},{20,12},{24,16},{28,20},{32,24... | collective-permute-start | bytes 589832 | tf_op jit(solution)/shard_map/ppermute | solution.py:220
  147.9 9.9 %collective-permute-start.11 = (bf16[2,96,512]{2,1,0:T(8,128)(2,1)}, bf16[2,96,512]{2,1,0:T(8,128)(2,1)S(1)}, u32[]{:S(2)}, u32[]{:S(2)}) collective-permute-start(bf16[2,96,512]{2,1,0:T(8,128)(2,1)} %get-tuple-element.44), channel_id=1, source_target_pairs={{0,8},{4,12},{8,16},{12,20},{16,24},{20,28},{24,32},{28,36},{32,40... | collective-permute-start | bytes 589832 | tf_op jit(solution)/shard_map/ppermute | solution.py:220
  152.7 5.1 %copy-start.14 = (bf16[2,96,512]{2,1,0:T(8,128)(2,1)}, bf16[2,96,512]{2,1,0:T(8,128)(2,1)S(1)}, u32[]{:S(2)}) copy-start(bf16[2,96,512]{2,1,0:T(8,128)(2,1)S(1)} %collective-permute-done.10.f1r) | copy-start | bytes 589828
  157.8 0.7 copy-start.15
  158.5 3.0 %copy-start.3 = (bf16[256,512]{1,0:T(8,128)(2,1)S(1)}, bf16[256,512]{1,0:T(8,128)(2,1)}, u32[]{:S(2)}) copy-start(bf16[256,512]{1,0:T(8,128)(2,1)} %get-tuple-element.45) | copy-start | bytes 786436
  162.5 16.5 %collective-permute-start.12 = (bf16[3,128,512]{2,1,0:T(8,128)(2,1)S(1)}, bf16[3,128,512]{2,1,0:T(8,128)(2,1)S(1)}, u32[]{:S(2)}, u32[]{:S(2)}) collective-permute-start(bf16[3,128,512]{2,1,0:T(8,128)(2,1)S(1)} %fusion.1), channel_id=1, source_target_pairs={{0,4},{4,0},{8,12},{12,8},{16,20},{20,16},{24,28},{28,24},{32,36},... | collective-permute-start | bytes 1179656 | tf_op jit(solution)/shard_map/ppermute | solution.py:306
  167.6 10.2 %all-to-all-start.1 = ((bf16[8,32,512]{2,1,0:T(8,128)(2,1)}), bf16[8,32,512]{2,1,0:T(8,128)(2,1)S(1)}, u32[]{:S(2)}, u32[]{:S(2)}) async-start(bf16[8,32,512]{2,1,0:T(8,128)(2,1)} %bitcast.7), calls=%async_computation.1 | async-start | bytes 524288 | tf_op jit(solution)/shard_map/all_to_all | solution.py:298
  177.8 1.2 copy-start

commit v2 on v1

v2 whole, which is shorter than its diff:
```python
import math

import jax
import jax.numpy as jnp
import numpy as np
from jax import lax
from jax.experimental import pallas as pl
from jax.experimental.pallas import tpu as pltpu
from jax.sharding import PartitionSpec as P

HEAD_DIM = 128
BLOCK = 128
BLOCKS = 128
LOG_TWO = math.log(2.0)
MASKED = -1e30
SCALE = 1.0 / math.sqrt(HEAD_DIM)
VMEM = 10 * 1024 * 1024
HALF = 512

SIDE_LEVELS = [0] + [1] + [2] * 2 + [3] * 4 + [4] * 8
VIEW = {1: [1, 2, 7, 8, 13, 14], 2: [3, 4, 9, 10, 15], 3: [5, 6], 6: [11, 12]}
VIEW_BLOCKS = VIEW[1] + VIEW[2] + VIEW[3] + VIEW[6]
FAR_BLOCKS = VIEW[3] + VIEW[6]
LEVEL_ORDER = [(level, block) for level in (1, 2, 3, 4) for block in "PO"]


def _rows(level):
    return BLOCK >> level


def _starts(blocks, level_of):
    starts, row = {}, 0
    for k in blocks:
        starts[k] = row
        row += _rows(level_of(k))
    return starts, row


def _finest(k):
    return SIDE_LEVELS[k]


def _pool(matrix, row, col, rows, factor):
    for r in range(rows):
        matrix[row + r, col + r * factor : col + (r + 1) * factor] = 1.0 / factor


def _own_matrix():
    m = np.zeros((240, 256), np.float32)
    row = 0
    for level, block in LEVEL_ORDER:
        _pool(m, row, 0 if block == "P" else BLOCK, _rows(level), 1 << level)
        row += _rows(level)
    return m


def _own_rows(level, block):
    row = 0
    for entry in LEVEL_ORDER:
        if entry == (level, block):
            return row, row + _rows(level)
        row += _rows(entry[0])
    raise KeyError


def _own_sent(distance):
    return [(_finest(2 * distance - 1), "O"), (_finest(2 * distance), "P")]


def _pass_matrix():
    cols, width = _starts(FAR_BLOCKS, _finest)
    sent = [(k, 1) for k in VIEW[1][2:]] + [(k, 2) for k in VIEW[2][2:]]
    m = np.zeros((sum(_rows(_finest(k)) for k, _ in sent), width), np.float32)
    row = 0
    for k, distance in sent:
        held = k - 2 * distance
        _pool(m, row, cols[held], _rows(_finest(k)), 1 << (_finest(k) - _finest(held)))
        row += _rows(_finest(k))
    return m


def _derive_matrix():
    cols, width = _starts(VIEW_BLOCKS, _finest)
    blocks = [k for k in VIEW_BLOCKS if k < 15]
    rows, height = _starts(blocks, lambda k: SIDE_LEVELS[k + 1])
    m = np.zeros((height, width), np.float32)
    for k in blocks:
        level = SIDE_LEVELS[k + 1]
        _pool(m, rows[k], cols[k], _rows(level), 1 << (level - _finest(k)))
    return m


def _final_matrix():
    own = _own_matrix()
    m = np.zeros((256, 256), np.float32)
    row = 0
    for distance, blocks in VIEW.items():
        start = row
        for level, block in _own_sent(distance):
            first, last = _own_rows(level, block)
            m[start : start + last - first] = own[first:last]
            start += last - first
        row += sum(_rows(_finest(k)) for k in blocks)
    return m.T.copy()


def _bias_tables():
    derived = [(k, SIDE_LEVELS[k + 1]) for k in VIEW_BLOCKS if k < 15]
    direct = [(k, _finest(k)) for k in VIEW_BLOCKS]
    p = [(0, 0, 128), (-1, 1, 64)] + [(k, lv, _rows(lv)) for k, lv in direct] + [(-1 - k, lv, _rows(lv)) for k, lv in derived]
    o = [(-1, 0, 128), (0, 1, 64)] + [(-1 - k, lv, _rows(lv)) for k, lv in direct] + [(k, lv, _rows(lv)) for k, lv in derived]
    table = np.array([[(off, lv) for off, lv, n in part for _ in range(n)] for part in (p, o)], np.int32)
    return table[..., 0], table[..., 1].astype(np.float32) * LOG_TWO


def _bf(m):
    return jnp.asarray(m, jnp.bfloat16)


def _dot(a, b):
    return jnp.dot(a, b, preferred_element_type=jnp.float32)


def _pull(a, b):
    return lax.dot_general(a, b, (((0,), (0,)), ((), ())), preferred_element_type=jnp.float32)


def _outer(a, b):
    return lax.dot_general(a, b, (((1,), (1,)), ((), ())), preferred_element_type=jnp.float32)


def _wide(*parts):
    return jnp.concatenate([p.astype(jnp.float32) for p in parts], axis=0)


def _half(core):
    return pl.ds(pl.multiple_of(core * HALF, HALF), HALF)


def pack_own(core_ref, k_ref, v_ref, own_ref, three_ref, six_ref, one_own_ref, two_own_ref, ones_ref):
    core = core_ref[0]
    for part, ref in enumerate((k_ref, v_ref)):
        levels = _dot(own_ref[...], jnp.concatenate([ref[core], ref[1 - core]], axis=0))
        for out, distance in ((three_ref, 3), (six_ref, 6), (one_own_ref, 1), (two_own_ref, 2)):
            spans = [_own_rows(level, block) for level, block in _own_sent(distance)]
            out[part] = jnp.concatenate([levels[a:b] for a, b in spans], axis=0).astype(jnp.bfloat16)
        one_own = jnp.concatenate([ref[core, :, _half(core)], ref[1 - core, :, _half(core)]], axis=0)
        ones_ref[part] = _dot(own_ref[0:128], one_own).astype(jnp.bfloat16)


def pack_on(three_ref, six_ref, one_own_ref, two_own_ref, w_ref, one_ref, two_ref):
    for part in range(2):
        on = _dot(w_ref[...], jnp.concatenate([three_ref[part], six_ref[part]], axis=0))
        one_ref[part] = _wide(one_own_ref[part], on[0:40]).astype(jnp.bfloat16)
        two_ref[part] = _wide(two_own_ref[part], on[40:64]).astype(jnp.bfloat16)


def join_view(core_ref, one_ref, two_ref, three_ref, six_ref, mine_ref, give_ref):
    core = core_ref[0]
    for out, lanes in ((mine_ref, _half(core)), (give_ref, _half(1 - core))):
        for part in range(2):
            near = _wide(one_ref[part, :, lanes], two_ref[part, :, lanes]).astype(jnp.bfloat16)
            out[part, 0:208] = near
            out[part, 208:240] = three_ref[part, :, lanes]
            out[part, 240:256] = six_ref[part, :, lanes]


def attend(
    core_ref, q_ref, k_ref, v_ref, do_ref, ones_ref, x_ref, y_ref, derive_ref, derive_t_ref, spread_ref, bias_ref,
    o_ref, dqp_ref, dqo_ref, gp_ref, go_ref, gx_ref, gy_ref,
):
    core = core_ref[0]
    lanes = pl.ds(pl.multiple_of(pl.program_id(0) * HEAD_DIM, HEAD_DIM), HEAD_DIM)
    sets_p, sets_o = [], []
    for part, ref in enumerate((k_ref, v_ref)):
        x, y = x_ref[part, :, lanes], y_ref[part, :, lanes]
        x_derived = _dot(derive_ref[...], x).astype(jnp.bfloat16)
        y_derived = _dot(derive_ref[...], y).astype(jnp.bfloat16)
        sets_p.append(jnp.concatenate([ref[core], ones_ref[part, 64:128, lanes], x, y_derived], axis=0))
        sets_o.append(jnp.concatenate([ref[1 - core], ones_ref[part, 0:64, lanes], y, x_derived], axis=0))
    grads = []
    for block, (keys, values) in enumerate((sets_p, sets_o)):
        place = core if block == 0 else 1 - core
        here = pl.ds(pl.multiple_of(place * BLOCK, BLOCK), BLOCK)
        q = q_ref[place]
        do = do_ref[here, lanes]
        scores = _outer(q, keys) * SCALE + bias_ref[block : block + 1]
        highest = jnp.max(scores, axis=1, keepdims=True)
        raised = jnp.exp(scores - highest)
        weights = raised * (1.0 / jnp.sum(raised, axis=1, keepdims=True))
        low = weights.astype(jnp.bfloat16)
        o_ref[here, lanes] = _dot(low, values).astype(jnp.bfloat16)
        weight_grad = _outer(do, values)
        row_term = jnp.sum(weights * weight_grad, axis=1, keepdims=True)
        score_grad = (weights * ((weight_grad - row_term) * SCALE)).astype(jnp.bfloat16)
        dq_ref = dqp_ref if block == 0 else dqo_ref
        dq_ref[:, lanes] = _dot(score_grad, keys).astype(jnp.bfloat16)
        grads.append((_pull(score_grad, q), _pull(low, do)))
    for part in range(2):
        gp, go = grads[0][part], grads[1][part]
        gx = gp[192:448] + _dot(derive_t_ref[...], go[448:640].astype(jnp.bfloat16))
        gy = go[192:448] + _dot(derive_t_ref[...], gp[448:640].astype(jnp.bfloat16))
        gx_ref[part, :, lanes] = gx.astype(jnp.bfloat16)
        gy_ref[part, :, lanes] = gy.astype(jnp.bfloat16)
        gp_ref[part, :, lanes] = gp[0:128] + _dot(spread_ref[...], go[128:192].astype(jnp.bfloat16))
        go_ref[part, :, lanes] = go[0:128] + _dot(spread_ref[...], gp[128:192].astype(jnp.bfloat16))


def split_view(core_ref, mine_ref, take_ref, one_ref, two_ref, far_ref):
    core = core_ref[0]
    for src, lanes in ((mine_ref, _half(core)), (take_ref, _half(1 - core))):
        for part in range(2):
            near = src[part, 0:208].astype(jnp.float32)
            one_ref[part, :, lanes] = near[0:136].astype(jnp.bfloat16)
            two_ref[part, :, lanes] = near[136:208].astype(jnp.bfloat16)
            far_ref[part, :, lanes] = src[part, 208:256]


def fold_on(far_ref, one_ref, two_ref, w_ref, three_ref, six_ref):
    for part in range(2):
        back = _wide(one_ref[part], two_ref[part])
        on = jnp.concatenate([back[96:136], back[184:208]], axis=0).astype(jnp.bfloat16)
        far = far_ref[part].astype(jnp.float32) + _dot(w_ref[...], on)
        three_ref[part] = far[0:32].astype(jnp.bfloat16)
        six_ref[part] = far[32:48].astype(jnp.bfloat16)


def fold_own(core_ref, one_ref, two_ref, three_ref, six_ref, gp_ref, go_ref, w_ref, keep_ref, give_ref):
    lanes = _half(core_ref[0])
    for part in range(2):
        near = _wide(one_ref[part], two_ref[part]).astype(jnp.bfloat16)
        total = _dot(w_ref[...], jnp.concatenate([near, three_ref[part], six_ref[part]], axis=0))
        keep_ref[part] = total[0:BLOCK]
        keep_ref[part, :, lanes] += gp_ref[part]
        give_ref[part] = total[BLOCK:].astype(jnp.bfloat16)
        give_ref[part, :, lanes] = (give_ref[part, :, lanes].astype(jnp.float32) + go_ref[part]).astype(jnp.bfloat16)


def finish(keep_ref, take_ref, k_ref, v_ref):
    for part, ref in enumerate((k_ref, v_ref)):
        ref[...] = (keep_ref[part] + take_ref[part].astype(jnp.float32)).astype(jnp.bfloat16)


VMEM_SPEC = pl.BlockSpec(memory_space=pltpu.VMEM)
SMEM_SPEC = pl.BlockSpec(memory_space=pltpu.SMEM)


def _whole(body, outs, *args, scalars=0):
    return pl.pallas_call(
        body,
        out_shape=[jax.ShapeDtypeStruct(s, d) for s, d in outs],
        in_specs=[SMEM_SPEC] * scalars + [VMEM_SPEC] * (len(args) - scalars),
        out_specs=[VMEM_SPEC] * len(outs),
        compiler_params=pltpu.CompilerParams(vmem_limit_bytes=VMEM),
    )(*args)


def local(queries, key_states, value_states, cotangent):
    bf16, f32 = jnp.bfloat16, jnp.float32
    tie = lax.optimization_barrier
    size = lax.axis_size("seq")
    seq = lax.axis_index("seq")
    core = lax.rem(seq, 2)
    width = queries.shape[1]
    half = width // 2
    heads = half // HEAD_DIM
    n_head = lax.axis_size("head")
    chip_cores = [[2 * i, 2 * i + 1] for i in range(size // 2)]
    chip_groups = [[g * 2 * n_head + m for m in range(2 * n_head)] for g in range(size // 2)]

    def hop(x, chips):
        return lax.ppermute(x, "seq", [(i, (i + (2 - 4 * (i % 2)) * chips) % size) for i in range(size)])

    def swap(x):
        return lax.ppermute(x, "seq", [(i, i ^ 1) for i in range(size)])

    def both_cores(x):
        return lax.all_gather(x, "seq", axis=0, axis_index_groups=chip_cores)

    def full(n, dtype=bf16):
        return ((2, n, width), dtype)

    def part(n, dtype=bf16):
        return ((2, n, half), dtype)

    keys, values = both_cores(key_states), both_cores(value_states)
    core_arg = core.reshape(1).astype(jnp.int32)

    t3, t6, own1, own2, ones = _whole(
        pack_own, [full(32), full(16), full(96), full(48), part(128)],
        core_arg, keys, values, _bf(_own_matrix()), scalars=1,
    )
    t3, t6, late_queries = tie((t3, t6, queries))
    r3, r6 = hop(t3, 3), hop(t6, 6)
    quest = both_cores(late_queries)
    r3, r6, quest, late_cotangent = tie((r3, r6, quest, cotangent))

    t1, t2 = _whole(pack_on, [full(136), full(72)], r3, r6, own1, own2, _bf(_pass_matrix()))
    t1, t2, late_cotangent = tie((t1, t2, late_cotangent))
    r2, r1 = hop(t2, 2), hop(t1, 1)
    split = late_cotangent.reshape(-1, n_head, 2, half).transpose(2, 1, 0, 3).reshape(2 * n_head, -1, half)
    do = lax.all_to_all(split, ("seq", "head"), 0, 0, axis_index_groups=chip_groups, tiled=True)
    do = do.reshape(2 * BLOCK, half)
    r1, r2, do = tie((r1, r2, do))
    mine, give = _whole(join_view, [part(256)] * 2, core_arg, r1, r2, r3, r6, scalars=1)
    other = swap(give)

    offsets, raise_by = _bias_tables()
    target = seq + (2 * core - 1) * jnp.asarray(offsets)
    bias = jnp.where((target >= 0) & (target < size), jnp.asarray(raise_by, f32), MASKED).astype(f32)

    pick = pl.BlockSpec((2, BLOCK, HEAD_DIM), lambda h, c: (0, 0, c[0] * heads + h))
    derive = _derive_matrix()
    spread = _own_matrix()[0:64, 0:BLOCK].T.copy()
    outs = [((2 * BLOCK, half), bf16)] + [((BLOCK, half), bf16)] * 2 + [part(BLOCK, f32)] * 2 + [part(256)] * 2
    attended, dq_mine, dq_give, gp, go, gx, gy = pl.pallas_call(
        attend,
        out_shape=[jax.ShapeDtypeStruct(s, d) for s, d in outs],
        grid_spec=pltpu.PrefetchScalarGridSpec(
            num_scalar_prefetch=1,
            grid=(heads,),
            in_specs=[pick] * 3 + [VMEM_SPEC] * 8,
            out_specs=[VMEM_SPEC] * len(outs),
        ),
        compiler_params=pltpu.CompilerParams(vmem_limit_bytes=VMEM),
    )(core_arg, quest, keys, values, do, ones, mine, other, _bf(derive), _bf(derive.T.copy()), _bf(spread), bias)

    u1, u2, far = _whole(split_view, [full(136), full(72), full(48)], core_arg, gx, swap(gy), scalars=1)
    u1, u2, attended, dq_give = tie((u1, u2, attended, dq_give))
    v2, v1 = hop(u2, -2), hop(u1, -1)

    out = lax.all_to_all(
        attended.reshape(2 * n_head, -1, half), ("seq", "head"), 0, 0, axis_index_groups=chip_groups, tiled=True
    )
    v1, v2, out, dq_give = tie((v1, v2, out, dq_give))

    u3, u6 = _whole(fold_on, [full(32), full(16)], far, v1, v2, _bf(_pass_matrix().T.copy()))
    u3, u6, out, dq_give = tie((u3, u6, out, dq_give))
    v3, v6 = hop(u3, -3), hop(u6, -6)
    out = out.reshape(2, n_head, -1, half).transpose(2, 1, 0, 3).reshape(-1, n_head * width)
    dq_take = swap(dq_give)
    query_gradient = jnp.concatenate(
        [jnp.where(core == 0, dq_mine, dq_take), jnp.where(core == 0, dq_take, dq_mine)], axis=1
    )
    v3, v6, out, query_gradient = tie((v3, v6, out, query_gradient))
    keep, back = _whole(
        fold_own, [full(BLOCK, f32), full(BLOCK)], core_arg, v1, v2, v3, v6, gp, go, _bf(_final_matrix()), scalars=1
    )
    key_gradient, value_gradient = pl.pallas_call(
        finish,
        out_shape=[jax.ShapeDtypeStruct((BLOCK, width), bf16)] * 2,
        in_specs=[VMEM_SPEC] * 2,
        compiler_params=pltpu.CompilerParams(vmem_limit_bytes=VMEM),
    )(keep, swap(back))
    return (out, query_gradient, key_gradient, value_gradient)


def solution(mesh):
    placed = (P("seq", "head"), P("seq", "head"), P("seq", "head"), P(("seq", "head"), None))
    return jax.shard_map(
        local,
        mesh=mesh,
        in_specs=placed,
        out_specs=(P(("seq", "head"), None), P("seq", "head"), P("seq", "head"), P("seq", "head")),
        check_vma=False,
    )
```

time: 181 us -> 127 us (0.70)
  the two profiles are of different devices: /device:TPU:1 before, /device:TPU:33 now
where the time goes in v2:
time: 127 us; the launch traced here: 126 us
  starting transfers between devices  50.4 us (40%)
  blocking collectives  32.2 us (25%)
  waiting for transfers between devices  20.6 us (16%)
  Pallas kernels  13.5 us (11%)
  local copies, waits for them, and re-layouts  7.76 us (6%)
    ppermute x8, starting transfers between devices, hop(): lax.ppermute(x, 'seq', [(i, (i + (2 - 4 * (i % 2)) * chips) % size) for i...  40.4 us
    ppermute x8, waiting for transfers between devices, hop(): lax.ppermute(x, 'seq', [(i, (i + (2 - 4 * (i % 2)) * chips) % size) for i...  15.9 us
    all_to_all x1, blocking collectives, local(): lax.all_to_all(attended.reshape(2 * n_head, -1, half), ('seq', 'head'), 0...  14.1 us
    all_to_all x1, blocking collectives, local(): lax.all_to_all(split, ('seq', 'head'), 0, 0, axis_index_groups=chip_group...  10.8 us
    ppermute x4, starting transfers between devices, swap(): return lax.ppermute(x, 'seq', [(i, i ^ 1) for i in range(size)])  10 us
    pallas_call x1, Pallas kernels, local(): pl.pallas_call(attend, out_shape=[jax.ShapeDtypeStruct(s, d) for s, d in...  9.55 us
    all_gather x3, blocking collectives, both_cores(): return lax.all_gather(x, 'seq', axis=0, axis_index_groups=chip_cores)  7.31 us
    unnamed x30, local copies, waits for them, and re-layouts  5.37 us
  transfers between devices with their start and end apart: 12, of which 6 were waited for; matrix products, arithmetic and copies ran while one was open for 3% of the time, Pallas kernels for 0%

profile of v2, /device:TPU:33, one launch (start us, length us, event | category | flops | bytes accessed | tf_op | source)
XLA Modules:
  0.0 126.1 jit_solution(12518469122905237616)
XLA Ops:
  0.6 0.0 copy-start.11
  0.6 2.8 %all-gather = bf16[256,1024]{1,0:T(8,128)(2,1)S(1)} all-gather(bf16[128,1024]{1,0:T(8,128)(2,1)} %param.14), channel_id=2, replica_groups={{0,4},{8,12},{16,20},{24,28},{32,36},{40,44},{48,52},{56,60},{64,68},{7..., dimensions={0}, use_global_device_ids=true | all-gather | bytes 786432 | tf_op jit(solution)/shard_map/all_gather | solution.py:278
  3.5 0.0 copy-done.11
  3.5 0.0 copy-start.6
  3.5 2.3 %all-gather.1 = bf16[256,1024]{1,0:T(8,128)(2,1)S(1)} all-gather(bf16[128,1024]{1,0:T(8,128)(2,1)S(1)} %copy-done.11), channel_id=3, replica_groups={{0,4},{8,12},{16,20},{24,28},{32,36},{40,44},{48,52},{56,60},{64,68},{7..., dimensions={0}, use_global_device_ids=true | all-gather | bytes 786432 | tf_op jit(solution)/shard_map/all_gather | solution.py:278
  5.8 0.0 copy-done.6
  5.8 0.0 copy-start.12
  5.8 0.5 shard_map.156
  6.3 0.0 copy-start.2
  6.3 13.6 %collective-permute-start = (bf16[2,32,1024]{2,1,0:T(8,128)(2,1)S(1)}, bf16[2,32,1024]{2,1,0:T(8,128)(2,1)S(1)}, u32[]{:S(2)}, u32[]{:S(2)}) collective-permute-start(bf16[2,32,1024]{2,1,0:T(8,128)(2,1)S(1)} %get-tuple-element.60), channel_id=1, source_target_pairs={{0,24},{4,492},{8,32},{12,500},{16,40},{20,508},{24,48},{28,4},{32... | collective-permute-start | bytes 393224 | tf_op jit(solution)/shard_map/ppermute | solution.py:272
  19.9 6.1 %collective-permute-start.1 = (bf16[2,16,1024]{2,1,0:T(8,128)(2,1)S(1)}, bf16[2,16,1024]{2,1,0:T(8,128)(2,1)S(1)}, u32[]{:S(2)}, u32[]{:S(2)}) collective-permute-start(bf16[2,16,1024]{2,1,0:T(8,128)(2,1)S(1)} %get-tuple-element.61), channel_id=1, source_target_pairs={{0,48},{4,468},{8,56},{12,476},{16,64},{20,484},{24,72},{28,492},{... | collective-permute-start | bytes 196616 | tf_op jit(solution)/shard_map/ppermute | solution.py:272
  25.9 0.0 copy-done.12
  26.0 0.0 copy-start.9
  26.0 2.2 %all-gather.2 = bf16[256,1024]{1,0:T(8,128)(2,1)S(1)} all-gather(bf16[128,1024]{1,0:T(8,128)(2,1)S(1)} %copy-done.12), channel_id=4, replica_groups={{0,4},{8,12},{16,20},{24,28},{32,36},{40,44},{48,52},{56,60},{64,68},{7..., dimensions={0}, use_global_device_ids=true | all-gather | bytes 786432 | tf_op jit(solution)/shard_map/all_gather | solution.py:278
  28.1 0.0 copy-done.2
  28.2 2.7 %collective-permute-done.1.six_ref = bf16[2,16,1024]{2,1,0:T(8,128)(2,1)S(1)} collective-permute-done((bf16[2,16,1024]{2,1,0:T(8,128)(2,1)S(1)}, bf16[2,16,1024]{2,1,0:T(8,128)(2,1)S(1)}, u32[]{:S(2)}, u32[]{:S(2)}) %collective-permute-start.1) | collective-permute-done | bytes 65568 | tf_op jit(solution)/shard_map/ppermute | solution.py:272
  30.9 0.0 collective-permute-done.three_ref
  30.9 0.0 copy-done.9
  30.9 0.9 shard_map.157
  31.8 3.4 %collective-permute-start.2 = (bf16[2,136,1024]{2,1,0:T(8,128)(2,1)S(1)}, bf16[2,136,1024]{2,1,0:T(8,128)(2,1)S(1)}, u32[]{:S(2)}, u32[]{:S(2)}) collective-permute-start(bf16[2,136,1024]{2,1,0:T(8,128)(2,1)S(1)} %get-tuple-element.71), channel_id=1, source_target_pairs={{0,8},{4,508},{8,16},{12,4},{16,24},{20,12},{24,32},{28,20},{32,40... | collective-permute-start | bytes 1671176 | tf_op jit(solution)/shard_map/ppermute | solution.py:272
  35.2 8.6 %collective-permute-start.3 = (bf16[2,72,1024]{2,1,0:T(8,128)(2,1)}, bf16[2,72,1024]{2,1,0:T(8,128)(2,1)S(1)}, u32[]{:S(2)}, u32[]{:S(2)}) collective-permute-start(bf16[2,72,1024]{2,1,0:T(8,128)(2,1)} %get-tuple-element.72), channel_id=1, source_target_pairs={{0,16},{4,500},{8,24},{12,508},{16,32},{20,4},{24,40},{28,12},{32,... | collective-permute-start | bytes 884744 | tf_op jit(solution)/shard_map/ppermute | solution.py:272
  43.8 1.1 reshape.30
  44.9 0.1 copy.17
  45.0 10.8 %all_to_all.10 = bf16[8,32,512]{2,1,0:T(8,128)(2,1)S(1)} all-to-all(bf16[8,32,512]{2,1,0:T(8,128)(2,1)S(1)} %bitcast.20), channel_id=1, replica_groups={{0,1,2,3,4,5,6,7},{8,9,10,11,12,13,14,15},{16,17,18,19,20,21,22,23},{24..., dimensions={0} | all-to-all | bytes 524288 | tf_op jit(solution)/shard_map/all_to_all | solution.py:302
  55.8 0.0 collective-permute-done.3.two_ref
  55.8 0.0 collective-permute-done.2.one_ref
  55.8 0.9 shard_map.158
  56.7 2.4 %collective-permute-start.4 = (bf16[2,256,512]{2,1,0:T(8,128)(2,1)}, bf16[2,256,512]{2,1,0:T(8,128)(2,1)S(1)}, u32[]{:S(2)}, u32[]{:S(2)}) collective-permute-start(bf16[2,256,512]{2,1,0:T(8,128)(2,1)} %get-tuple-element.79), channel_id=1, source_target_pairs={{0,4},{4,0},{8,12},{12,8},{16,20},{20,16},{24,28},{28,24},{32,36},... | collective-permute-start | bytes 1572872 | tf_op jit(solution)/shard_map/ppermute | solution.py:275
  59.1 0.0 copy-done.14
  59.1 0.0 copy-done.13
  59.1 1.7 %collective-permute-done.4.y_ref = bf16[2,256,512]{2,1,0:T(8,128)(2,1)S(1)} collective-permute-done((bf16[2,256,512]{2,1,0:T(8,128)(2,1)}, bf16[2,256,512]{2,1,0:T(8,128)(2,1)S(1)}, u32[]{:S(2)}, u32[]{:S(2)}) %collective-permute-start.4) | collective-permute-done | bytes 524320 | tf_op jit(solution)/shard_map/ppermute | solution.py:275
  60.8 0.8 copy-done
  61.6 1.0 copy-done.1
  62.6 0.9 copy-done.3
  63.6 0.9 copy-done.5
  64.5 0.9 copy-done.7
  65.4 0.8 copy-done.8
  66.1 9.5 %shard_map.159 = (bf16[256,512]{1,0:T(8,128)(2,1)S(1)}, bf16[128,512]{1,0:T(8,128)(2,1)S(1)}, bf16[128,512]{1,0:T(8,128)(2,1)}, f32[2,128,512]{2,1,0:T(8,128)S(1...) custom-call(s32[1]{0:T(128)} %bitcast.core_ref, ...), custom_call_target="tpu_custom_call" | custom-call | tf_op jit(solution)/shard_map/pallas_call | solution.py:316
  75.7 2.3 %collective-permute-start.5 = (bf16[2,256,512]{2,1,0:T(8,128)(2,1)S(1)}, bf16[2,256,512]{2,1,0:T(8,128)(2,1)S(1)}, u32[]{:S(2)}, u32[]{:S(2)}) collective-permute-start(bf16[2,256,512]{2,1,0:T(8,128)(2,1)S(1)} %get-tuple-element.81), channel_id=1, source_target_pairs={{0,4},{4,0},{8,12},{12,8},{16,20},{20,16},{24,28},{28,24},{32,36},... | collective-permute-start | bytes 1572872 | tf_op jit(solution)/shard_map/ppermute | solution.py:275
  77.9 1.5 %collective-permute-done.5.take_ref = bf16[2,256,512]{2,1,0:T(8,128)(2,1)S(1)} collective-permute-done((bf16[2,256,512]{2,1,0:T(8,128)(2,1)S(1)}, bf16[2,256,512]{2,1,0:T(8,128)(2,1)S(1)}, u32[]{:S(2)}, u32[]{:S(2)}) %collective-permute-start.5) | collective-permute-done | bytes 524320 | tf_op jit(solution)/shard_map/ppermute | solution.py:275
  79.5 0.1 shard_map.160
  79.5 1.9 %collective-permute-start.6 = (bf16[2,136,1024]{2,1,0:T(8,128)(2,1)S(1)}, bf16[2,136,1024]{2,1,0:T(8,128)(2,1)S(1)}, u32[]{:S(2)}, u32[]{:S(2)}) collective-permute-start(bf16[2,136,1024]{2,1,0:T(8,128)(2,1)S(1)} %get-tuple-element.87), channel_id=1, source_target_pairs={{0,504},{4,12},{8,0},{12,20},{16,8},{20,28},{24,16},{28,36},{32,24... | collective-permute-start | bytes 1671176 | tf_op jit(solution)/shard_map/ppermute | solution.py:272
  81.5 1.9 %collective-permute-start.7 = (bf16[2,72,1024]{2,1,0:T(8,128)(2,1)S(1)}, bf16[2,72,1024]{2,1,0:T(8,128)(2,1)S(1)}, u32[]{:S(2)}, u32[]{:S(2)}) collective-permute-start(bf16[2,72,1024]{2,1,0:T(8,128)(2,1)S(1)} %get-tuple-element.88), channel_id=1, source_target_pairs={{0,496},{4,20},{8,504},{12,28},{16,0},{20,36},{24,8},{28,44},{32,1... | collective-permute-start | bytes 884744 | tf_op jit(solution)/shard_map/ppermute | solution.py:272
  83.4 0.0 copy-start.10
  83.4 14.1 %all_to_all.11 = bf16[8,32,512]{2,1,0:T(8,128)(2,1)S(1)} all-to-all(bf16[8,32,512]{2,1,0:T(8,128)(2,1)S(1)} %bitcast.18), channel_id=1, replica_groups={{0,1,2,3,4,5,6,7},{8,9,10,11,12,13,14,15},{16,17,18,19,20,21,22,23},{24..., dimensions={0} | all-to-all | bytes 524288 | tf_op jit(solution)/shard_map/all_to_all | solution.py:332
  97.5 1.6 %collective-permute-done.7.two_ref = bf16[2,72,1024]{2,1,0:T(8,128)(2,1)S(1)} collective-permute-done((bf16[2,72,1024]{2,1,0:T(8,128)(2,1)S(1)}, bf16[2,72,1024]{2,1,0:T(8,128)(2,1)S(1)}, u32[]{:S(2)}, u32[]{:S(2)}) %collective-permute-start.7) | collective-permute-done | bytes 294944 | tf_op jit(solution)/shard_map/ppermute | solution.py:272
  99.2 0.0 collective-permute-done.6.one_ref
  99.2 0.0 copy-done.10
  99.2 0.2 shard_map.161
  99.4 1.9 %collective-permute-start.10 = (bf16[128,512]{1,0:T(8,128)(2,1)}, bf16[128,512]{1,0:T(8,128)(2,1)S(1)}, u32[]{:S(2)}, u32[]{:S(2)}) collective-permute-start(bf16[128,512]{1,0:T(8,128)(2,1)} %get-tuple-element.101), channel_id=1, source_target_pairs={{0,4},{4,0},{8,12},{12,8},{16,20},{20,16},{24,28},{28,24},{32,36},... | collective-permute-start | bytes 393224 | tf_op jit(solution)/shard_map/ppermute | solution.py:275
  101.3 0.3 copy.20
  101.6 0.9 reshape.35
  102.5 1.9 %collective-permute-start.8 = (bf16[2,32,1024]{2,1,0:T(8,128)(2,1)S(1)}, bf16[2,32,1024]{2,1,0:T(8,128)(2,1)S(1)}, u32[]{:S(2)}, u32[]{:S(2)}) collective-permute-start(bf16[2,32,1024]{2,1,0:T(8,128)(2,1)S(1)} %get-tuple-element.97), channel_id=1, source_target_pairs={{0,488},{4,28},{8,496},{12,36},{16,504},{20,44},{24,0},{28,52},{32... | collective-permute-start | bytes 393224 | tf_op jit(solution)/shard_map/ppermute | solution.py:272
  104.4 3.1 %collective-permute-start.9 = (bf16[2,16,1024]{2,1,0:T(8,128)(2,1)S(1)}, bf16[2,16,1024]{2,1,0:T(8,128)(2,1)S(1)}, u32[]{:S(2)}, u32[]{:S(2)}) collective-permute-start(bf16[2,16,1024]{2,1,0:T(8,128)(2,1)S(1)} %get-tuple-element.98), channel_id=1, source_target_pairs={{0,464},{4,52},{8,472},{12,60},{16,480},{20,68},{24,488},{28,76},{... | collective-permute-start | bytes 196616 | tf_op jit(solution)/shard_map/ppermute | solution.py:272
  107.5 0.0 collective-permute-done.10
  107.5 0.0 copy-start.4
  107.5 0.7 pad_maximum_fusion
  108.2 11.5 %collective-permute-done.9.six_ref = bf16[2,16,1024]{2,1,0:T(8,128)(2,1)S(1)} collective-permute-done((bf16[2,16,1024]{2,1,0:T(8,128)(2,1)S(1)}, bf16[2,16,1024]{2,1,0:T(8,128)(2,1)S(1)}, u32[]{:S(2)}, u32[]{:S(2)}) %collective-permute-start.9) | collective-permute-done | bytes 65568 | tf_op jit(solution)/shard_map/ppermute | solution.py:272
  119.7 0.0 collective-permute-done.8.three_ref
  119.7 0.0 copy-done.4
  119.7 0.5 shard_map.162
  120.2 3.4 %collective-permute-start.11 = (bf16[2,128,1024]{2,1,0:T(8,128)(2,1)S(1)}, bf16[2,128,1024]{2,1,0:T(8,128)(2,1)S(1)}, u32[]{:S(2)}, u32[]{:S(2)}) collective-permute-start(bf16[2,128,1024]{2,1,0:T(8,128)(2,1)S(1)} %get-tuple-element.109), channel_id=1, source_target_pairs={{0,4},{4,0},{8,12},{12,8},{16,20},{20,16},{24,28},{28,24},{32,36},... | collective-permute-start | bytes 1572872 | tf_op jit(solution)/shard_map/ppermute | solution.py:275
  123.7 1.5 %collective-permute-done.11.take_ref = bf16[2,128,1024]{2,1,0:T(8,128)(2,1)S(1)} collective-permute-done((bf16[2,128,1024]{2,1,0:T(8,128)(2,1)S(1)}, bf16[2,128,1024]{2,1,0:T(8,128)(2,1)S(1)}, u32[]{:S(2)}, u32[]{:S(2)}) %collective-permute-start.11) | collective-permute-done | bytes 524320 | tf_op jit(solution)/shard_map/ppermute | solution.py:275
  125.2 0.9 shard_map.163
  (10 shorter events, 0.0 us)
Async XLA Ops:
  0.6 2.8 %copy-start.11 = (bf16[128,1024]{1,0:T(8,128)(2,1)S(1)}, bf16[128,1024]{1,0:T(8,128)(2,1)}, u32[]{:S(2)}) copy-start(bf16[128,1024]{1,0:T(8,128)(2,1)} %param.15) | copy-start | bytes 786436
  3.5 2.3 %copy-start.6 = (bf16[240,256]{1,0:T(8,128)(2,1)S(1)}, bf16[240,256]{1,0:T(8,128)(2,1)}, u32[]{:S(2)}) copy-start(bf16[240,256]{1,0:T(8,128)(2,1)} %constant.39.clone.own_ref) | copy-start | bytes 368644
  5.8 20.2 %copy-start.12 = (bf16[128,1024]{1,0:T(8,128)(2,1)S(1)}, bf16[128,1024]{1,0:T(8,128)(2,1)}, u32[]{:S(2)}) copy-start(bf16[128,1024]{1,0:T(8,128)(2,1)} %param.13) | copy-start | bytes 786436
  6.3 21.9 %copy-start.2 = (bf16[2,128,512]{2,1,0:T(8,128)(2,1)}, bf16[2,128,512]{2,1,0:T(8,128)(2,1)S(1)}, u32[]{:S(2)}) copy-start(bf16[2,128,512]{2,1,0:T(8,128)(2,1)S(1)} %get-tuple-element.75.ones_ref) | copy-start | bytes 786436
  6.3 24.6 %collective-permute-start = (bf16[2,32,1024]{2,1,0:T(8,128)(2,1)S(1)}, bf16[2,32,1024]{2,1,0:T(8,128)(2,1)S(1)}, u32[]{:S(2)}, u32[]{:S(2)}) collective-permute-start(bf16[2,32,1024]{2,1,0:T(8,128)(2,1)S(1)} %get-tuple-element.60), channel_id=1, source_target_pairs={{0,24},{4,492},{8,32},{12,500},{16,40},{20,508},{24,48},{28,4},{32... | collective-permute-start | bytes 393224 | tf_op jit(solution)/shard_map/ppermute | solution.py:272
  19.9 11.0 %collective-permute-start.1 = (bf16[2,16,1024]{2,1,0:T(8,128)(2,1)S(1)}, bf16[2,16,1024]{2,1,0:T(8,128)(2,1)S(1)}, u32[]{:S(2)}, u32[]{:S(2)}) collective-permute-start(bf16[2,16,1024]{2,1,0:T(8,128)(2,1)S(1)} %get-tuple-element.61), channel_id=1, source_target_pairs={{0,48},{4,468},{8,56},{12,476},{16,64},{20,484},{24,72},{28,492},{... | collective-permute-start | bytes 196616 | tf_op jit(solution)/shard_map/ppermute | solution.py:272
  26.0 4.9 %copy-start.9 = (bf16[64,48]{1,0:T(8,128)(2,1)S(1)}, bf16[64,48]{1,0:T(8,128)(2,1)}, u32[]{:S(2)}) copy-start(bf16[64,48]{1,0:T(8,128)(2,1)} %constant.40.clone.w_ref) | copy-start | bytes 18436
  31.8 24.0 %collective-permute-start.2 = (bf16[2,136,1024]{2,1,0:T(8,128)(2,1)S(1)}, bf16[2,136,1024]{2,1,0:T(8,128)(2,1)S(1)}, u32[]{:S(2)}, u32[]{:S(2)}) collective-permute-start(bf16[2,136,1024]{2,1,0:T(8,128)(2,1)S(1)} %get-tuple-element.71), channel_id=1, source_target_pairs={{0,8},{4,508},{8,16},{12,4},{16,24},{20,12},{24,32},{28,20},{32,40... | collective-permute-start | bytes 1671176 | tf_op jit(solution)/shard_map/ppermute | solution.py:272
  35.2 20.6 %collective-permute-start.3 = (bf16[2,72,1024]{2,1,0:T(8,128)(2,1)}, bf16[2,72,1024]{2,1,0:T(8,128)(2,1)S(1)}, u32[]{:S(2)}, u32[]{:S(2)}) collective-permute-start(bf16[2,72,1024]{2,1,0:T(8,128)(2,1)} %get-tuple-element.72), channel_id=1, source_target_pairs={{0,16},{4,500},{8,24},{12,508},{16,32},{20,4},{24,40},{28,12},{32,... | collective-permute-start | bytes 884744 | tf_op jit(solution)/shard_map/ppermute | solution.py:272
  55.8 3.3 %copy-start.14 = (f32[2,640]{1,0:T(2,128)S(1)}, f32[2,640]{1,0:T(2,128)}, u32[]{:S(2)}) copy-start(f32[2,640]{1,0:T(2,128)} %constant.42.clone) | copy-start | bytes 15364
  56.7 2.4 %copy-start.13 = (s32[2,640]{1,0:T(2,128)S(1)}, s32[2,640]{1,0:T(2,128)}, u32[]{:S(2)}) copy-start(s32[2,640]{1,0:T(2,128)} %constant.41.clone) | copy-start | bytes 15364
  56.7 4.1 %collective-permute-start.4 = (bf16[2,256,512]{2,1,0:T(8,128)(2,1)}, bf16[2,256,512]{2,1,0:T(8,128)(2,1)S(1)}, u32[]{:S(2)}, u32[]{:S(2)}) collective-permute-start(bf16[2,256,512]{2,1,0:T(8,128)(2,1)} %get-tuple-element.79), channel_id=1, source_target_pairs={{0,4},{4,0},{8,12},{12,8},{16,20},{20,16},{24,28},{28,24},{32,36},... | collective-permute-start | bytes 1572872 | tf_op jit(solution)/shard_map/ppermute | solution.py:275
  60.8 0.8 copy-start
  61.6 1.0 copy-start.1
  62.6 0.9 copy-start.3
  63.6 0.9 copy-start.5
  64.5 0.9 copy-start.7
  65.4 0.8 copy-start.8
  75.7 3.8 %collective-permute-start.5 = (bf16[2,256,512]{2,1,0:T(8,128)(2,1)S(1)}, bf16[2,256,512]{2,1,0:T(8,128)(2,1)S(1)}, u32[]{:S(2)}, u32[]{:S(2)}) collective-permute-start(bf16[2,256,512]{2,1,0:T(8,128)(2,1)S(1)} %get-tuple-element.81), channel_id=1, source_target_pairs={{0,4},{4,0},{8,12},{12,8},{16,20},{20,16},{24,28},{28,24},{32,36},... | collective-permute-start | bytes 1572872 | tf_op jit(solution)/shard_map/ppermute | solution.py:275
  79.5 19.6 %collective-permute-start.6 = (bf16[2,136,1024]{2,1,0:T(8,128)(2,1)S(1)}, bf16[2,136,1024]{2,1,0:T(8,128)(2,1)S(1)}, u32[]{:S(2)}, u32[]{:S(2)}) collective-permute-start(bf16[2,136,1024]{2,1,0:T(8,128)(2,1)S(1)} %get-tuple-element.87), channel_id=1, source_target_pairs={{0,504},{4,12},{8,0},{12,20},{16,8},{20,28},{24,16},{28,36},{32,24... | collective-permute-start | bytes 1671176 | tf_op jit(solution)/shard_map/ppermute | solution.py:272
  81.5 17.7 %collective-permute-start.7 = (bf16[2,72,1024]{2,1,0:T(8,128)(2,1)S(1)}, bf16[2,72,1024]{2,1,0:T(8,128)(2,1)S(1)}, u32[]{:S(2)}, u32[]{:S(2)}) collective-permute-start(bf16[2,72,1024]{2,1,0:T(8,128)(2,1)S(1)} %get-tuple-element.88), channel_id=1, source_target_pairs={{0,496},{4,20},{8,504},{12,28},{16,0},{20,36},{24,8},{28,44},{32,1... | collective-permute-start | bytes 884744 | tf_op jit(solution)/shard_map/ppermute | solution.py:272
  83.4 15.8 %copy-start.10 = (bf16[48,64]{1,0:T(8,128)(2,1)S(1)}, bf16[48,64]{1,0:T(8,128)(2,1)}, u32[]{:S(2)}) copy-start(bf16[48,64]{1,0:T(8,128)(2,1)} %constant.46.clone.w_ref) | copy-start | bytes 18436
  99.4 8.1 %collective-permute-start.10 = (bf16[128,512]{1,0:T(8,128)(2,1)}, bf16[128,512]{1,0:T(8,128)(2,1)S(1)}, u32[]{:S(2)}, u32[]{:S(2)}) collective-permute-start(bf16[128,512]{1,0:T(8,128)(2,1)} %get-tuple-element.101), channel_id=1, source_target_pairs={{0,4},{4,0},{8,12},{12,8},{16,20},{20,16},{24,28},{28,24},{32,36},... | collective-permute-start | bytes 393224 | tf_op jit(solution)/shard_map/ppermute | solution.py:275
  102.5 17.2 %collective-permute-start.8 = (bf16[2,32,1024]{2,1,0:T(8,128)(2,1)S(1)}, bf16[2,32,1024]{2,1,0:T(8,128)(2,1)S(1)}, u32[]{:S(2)}, u32[]{:S(2)}) collective-permute-start(bf16[2,32,1024]{2,1,0:T(8,128)(2,1)S(1)} %get-tuple-element.97), channel_id=1, source_target_pairs={{0,488},{4,28},{8,496},{12,36},{16,504},{20,44},{24,0},{28,52},{32... | collective-permute-start | bytes 393224 | tf_op jit(solution)/shard_map/ppermute | solution.py:272
  104.4 15.3 %collective-permute-start.9 = (bf16[2,16,1024]{2,1,0:T(8,128)(2,1)S(1)}, bf16[2,16,1024]{2,1,0:T(8,128)(2,1)S(1)}, u32[]{:S(2)}, u32[]{:S(2)}) collective-permute-start(bf16[2,16,1024]{2,1,0:T(8,128)(2,1)S(1)} %get-tuple-element.98), channel_id=1, source_target_pairs={{0,464},{4,52},{8,472},{12,60},{16,480},{20,68},{24,488},{28,76},{... | collective-permute-start | bytes 196616 | tf_op jit(solution)/shard_map/ppermute | solution.py:272
  107.5 12.2 %copy-start.4 = (bf16[256,256]{1,0:T(8,128)(2,1)S(1)}, bf16[256,256]{1,0:T(8,128)(2,1)}, u32[]{:S(2)}) copy-start(bf16[256,256]{1,0:T(8,128)(2,1)} %constant.47.clone.w_ref) | copy-start | bytes 393220
  120.2 5.0 %collective-permute-start.11 = (bf16[2,128,1024]{2,1,0:T(8,128)(2,1)S(1)}, bf16[2,128,1024]{2,1,0:T(8,128)(2,1)S(1)}, u32[]{:S(2)}, u32[]{:S(2)}) collective-permute-start(bf16[2,128,1024]{2,1,0:T(8,128)(2,1)S(1)} %get-tuple-element.109), channel_id=1, source_target_pairs={{0,4},{4,0},{8,12},{12,8},{16,20},{20,16},{24,28},{28,24},{32,36},... | collective-permute-start | bytes 1572872 | tf_op jit(solution)/shard_map/ppermute | solution.py:275

commit v3 on v2

--- a/solution.py
+++ b/solution.py
@@ -14,7 +14,8 @@
 LOG_TWO = math.log(2.0)
 MASKED = -1e30
 SCALE = 1.0 / math.sqrt(HEAD_DIM)
-VMEM = 10 * 1024 * 1024
+VMEM = 4 * 1024 * 1024
+WIDE_VMEM = 52 * 1024 * 1024
 HALF = 512
 
 SIDE_LEVELS = [0] + [1] + [2] * 2 + [3] * 4 + [4] * 8
@@ -155,35 +156,38 @@
         two_ref[part] = _wide(two_own_ref[part], on[40:64]).astype(jnp.bfloat16)
 
 
-def join_view(core_ref, one_ref, two_ref, three_ref, six_ref, mine_ref, give_ref):
+def join_view(core_ref, one_ref, two_ref, three_ref, six_ref, q_ref, mine_ref, give_ref):
     core = core_ref[0]
     for out, lanes in ((mine_ref, _half(core)), (give_ref, _half(1 - core))):
         for part in range(2):
             near = _wide(one_ref[part, :, lanes], two_ref[part, :, lanes]).astype(jnp.bfloat16)
-            out[part, 0:208] = near
-            out[part, 208:240] = three_ref[part, :, lanes]
-            out[part, 240:256] = six_ref[part, :, lanes]
+            out[2 * part] = near[0:128]
+            out[2 * part + 1, 0:80] = near[128:208]
+            out[2 * part + 1, 80:112] = three_ref[part, :, lanes]
+            out[2 * part + 1, 112:128] = six_ref[part, :, lanes]
+        out[4] = q_ref[:, lanes]
 
 
 def attend(
-    core_ref, q_ref, k_ref, v_ref, do_ref, ones_ref, x_ref, y_ref, derive_ref, derive_t_ref, spread_ref, bias_ref,
-    o_ref, dqp_ref, dqo_ref, gp_ref, go_ref, gx_ref, gy_ref,
+    core_ref, k_ref, v_ref, do_ref, ones_ref, x_ref, y_ref, derive_ref, derive_t_ref, spread_ref, bias_ref,
+    o_ref, dq_ref, gp_ref, go_ref, gx_ref, gy_ref,
 ):
     core = core_ref[0]
     lanes = pl.ds(pl.multiple_of(pl.program_id(0) * HEAD_DIM, HEAD_DIM), HEAD_DIM)
     sets_p, sets_o = [], []
     for part, ref in enumerate((k_ref, v_ref)):
-        x, y = x_ref[part, :, lanes], y_ref[part, :, lanes]
+        x = jnp.concatenate([x_ref[2 * part], x_ref[2 * part + 1]], axis=0)
+        y = jnp.concatenate([y_ref[2 * part], y_ref[2 * part + 1]], axis=0)
         x_derived = _dot(derive_ref[...], x).astype(jnp.bfloat16)
         y_derived = _dot(derive_ref[...], y).astype(jnp.bfloat16)
-        sets_p.append(jnp.concatenate([ref[core], ones_ref[part, 64:128, lanes], x, y_derived], axis=0))
-        sets_o.append(jnp.concatenate([ref[1 - core], ones_ref[part, 0:64, lanes], y, x_derived], axis=0))
+        sets_p.append(jnp.concatenate([ref[core], ones_ref[part, 64:128], x, y_derived], axis=0))
+        sets_o.append(jnp.concatenate([ref[1 - core], ones_ref[part, 0:64], y, x_derived], axis=0))
     grads = []
     for block, (keys, values) in enumerate((sets_p, sets_o)):
         place = core if block == 0 else 1 - core
         here = pl.ds(pl.multiple_of(place * BLOCK, BLOCK), BLOCK)
-        q = q_ref[place]
-        do = do_ref[here, lanes]
+        q = (x_ref, y_ref)[block][4]
+        do = do_ref[here]
         scores = _outer(q, keys) * SCALE + bias_ref[block : block + 1]
         highest = jnp.max(scores, axis=1, keepdims=True)
         raised = jnp.exp(scores - highest)
@@ -193,15 +197,19 @@
         weight_grad = _outer(do, values)
         row_term = jnp.sum(weights * weight_grad, axis=1, keepdims=True)
         score_grad = (weights * ((weight_grad - row_term) * SCALE)).astype(jnp.bfloat16)
-        dq_ref = dqp_ref if block == 0 else dqo_ref
-        dq_ref[:, lanes] = _dot(score_grad, keys).astype(jnp.bfloat16)
+        dq = _dot(score_grad, keys).astype(jnp.bfloat16)
+        if block == 0:
+            dq_ref[:, lanes] = dq
+        else:
+            gy_ref[4, :, lanes] = dq
         grads.append((_pull(score_grad, q), _pull(low, do)))
     for part in range(2):
         gp, go = grads[0][part], grads[1][part]
         gx = gp[192:448] + _dot(derive_t_ref[...], go[448:640].astype(jnp.bfloat16))
         gy = go[192:448] + _dot(derive_t_ref[...], gp[448:640].astype(jnp.bfloat16))
-        gx_ref[part, :, lanes] = gx.astype(jnp.bfloat16)
-        gy_ref[part, :, lanes] = gy.astype(jnp.bfloat16)
+        for g, ref in ((gx, gx_ref), (gy, gy_ref)):
+            ref[2 * part, :, lanes] = g[0:128].astype(jnp.bfloat16)
+            ref[2 * part + 1, :, lanes] = g[128:256].astype(jnp.bfloat16)
         gp_ref[part, :, lanes] = gp[0:128] + _dot(spread_ref[...], go[128:192].astype(jnp.bfloat16))
         go_ref[part, :, lanes] = go[0:128] + _dot(spread_ref[...], gp[128:192].astype(jnp.bfloat16))
 
@@ -210,10 +218,10 @@
     core = core_ref[0]
     for src, lanes in ((mine_ref, _half(core)), (take_ref, _half(1 - core))):
         for part in range(2):
-            near = src[part, 0:208].astype(jnp.float32)
+            near = _wide(src[2 * part], src[2 * part + 1, 0:80])
             one_ref[part, :, lanes] = near[0:136].astype(jnp.bfloat16)
             two_ref[part, :, lanes] = near[136:208].astype(jnp.bfloat16)
-            far_ref[part, :, lanes] = src[part, 208:256]
+            far_ref[part, :, lanes] = src[2 * part + 1, 80:128]
 
 
 def fold_on(far_ref, one_ref, two_ref, w_ref, three_ref, six_ref):
@@ -269,7 +277,8 @@
     chip_groups = [[g * 2 * n_head + m for m in range(2 * n_head)] for g in range(size // 2)]
 
     def hop(x, chips):
-        return lax.ppermute(x, "seq", [(i, (i + (2 - 4 * (i % 2)) * chips) % size) for i in range(size)])
+        pairs = [(i, i + (2 - 4 * (i % 2)) * chips) for i in range(size)]
+        return lax.ppermute(x, "seq", [(i, j) for i, j in pairs if 0 <= j < size])
 
     def swap(x):
         return lax.ppermute(x, "seq", [(i, i ^ 1) for i in range(size)])
@@ -279,6 +288,8 @@
 
     def full(n, dtype=bf16):
         return ((2, n, width), dtype)
+
+    view = ((5, BLOCK, half), bf16)
 
     def part(n, dtype=bf16):
         return ((2, n, half), dtype)
@@ -290,10 +301,8 @@
         pack_own, [full(32), full(16), full(96), full(48), part(128)],
         core_arg, keys, values, _bf(_own_matrix()), scalars=1,
     )
-    t3, t6, late_queries = tie((t3, t6, queries))
     r3, r6 = hop(t3, 3), hop(t6, 6)
-    quest = both_cores(late_queries)
-    r3, r6, quest, late_cotangent = tie((r3, r6, quest, cotangent))
+    r3, r6, late_cotangent = tie((r3, r6, cotangent))
 
     t1, t2 = _whole(pack_on, [full(136), full(72)], r3, r6, own1, own2, _bf(_pass_matrix()))
     t1, t2, late_cotangent = tie((t1, t2, late_cotangent))
@@ -302,7 +311,7 @@
     do = lax.all_to_all(split, ("seq", "head"), 0, 0, axis_index_groups=chip_groups, tiled=True)
     do = do.reshape(2 * BLOCK, half)
     r1, r2, do = tie((r1, r2, do))
-    mine, give = _whole(join_view, [part(256)] * 2, core_arg, r1, r2, r3, r6, scalars=1)
+    mine, give = _whole(join_view, [view] * 2, core_arg, r1, r2, r3, r6, queries, scalars=1)
     other = swap(give)
 
     offsets, raise_by = _bias_tables()
@@ -310,41 +319,43 @@
     bias = jnp.where((target >= 0) & (target < size), jnp.asarray(raise_by, f32), MASKED).astype(f32)
 
     pick = pl.BlockSpec((2, BLOCK, HEAD_DIM), lambda h, c: (0, 0, c[0] * heads + h))
+    cut = lambda n: pl.BlockSpec((n, BLOCK, HEAD_DIM), lambda h, c: (0, 0, h))
+    const = lambda *dims: pl.BlockSpec(dims, lambda h, c: (0, 0))
     derive = _derive_matrix()
     spread = _own_matrix()[0:64, 0:BLOCK].T.copy()
-    outs = [((2 * BLOCK, half), bf16)] + [((BLOCK, half), bf16)] * 2 + [part(BLOCK, f32)] * 2 + [part(256)] * 2
-    attended, dq_mine, dq_give, gp, go, gx, gy = pl.pallas_call(
+    outs = [((2 * BLOCK, half), bf16), ((BLOCK, half), bf16)] + [part(BLOCK, f32)] * 2 + [((4, BLOCK, half), bf16), view]
+    attended, dq_mine, gp, go, gx, gy = pl.pallas_call(
         attend,
         out_shape=[jax.ShapeDtypeStruct(s, d) for s, d in outs],
         grid_spec=pltpu.PrefetchScalarGridSpec(
             num_scalar_prefetch=1,
             grid=(heads,),
-            in_specs=[pick] * 3 + [VMEM_SPEC] * 8,
+            in_specs=[pick] * 2
+            + [pl.BlockSpec((2 * BLOCK, HEAD_DIM), lambda h, c: (0, h)), cut(2), cut(5), cut(5)]
+            + [const(192, 256), const(256, 192), const(128, 64), const(2, 640)],
             out_specs=[VMEM_SPEC] * len(outs),
         ),
-        compiler_params=pltpu.CompilerParams(vmem_limit_bytes=VMEM),
-    )(core_arg, quest, keys, values, do, ones, mine, other, _bf(derive), _bf(derive.T.copy()), _bf(spread), bias)
-
-    u1, u2, far = _whole(split_view, [full(136), full(72), full(48)], core_arg, gx, swap(gy), scalars=1)
-    u1, u2, attended, dq_give = tie((u1, u2, attended, dq_give))
+        compiler_params=pltpu.CompilerParams(vmem_limit_bytes=WIDE_VMEM),
+    )(core_arg, keys, values, do, ones, mine, other, _bf(derive), _bf(derive.T.copy()), _bf(spread), bias)
+
+    take = swap(gy)
+    u1, u2, far = _whole(split_view, [full(136), full(72), full(48)], core_arg, gx, take, scalars=1)
+    u1, u2, attended = tie((u1, u2, attended))
     v2, v1 = hop(u2, -2), hop(u1, -1)
-
     out = lax.all_to_all(
         attended.reshape(2 * n_head, -1, half), ("seq", "head"), 0, 0, axis_index_groups=chip_groups, tiled=True
     )
-    v1, v2, out, dq_give = tie((v1, v2, out, dq_give))
+    v1, v2, out = tie((v1, v2, out))
 
     u3, u6 = _whole(fold_on, [full(32), full(16)], far, v1, v2, _bf(_pass_matrix().T.copy()))
-    u3, u6, out, dq_give = tie((u3, u6, out, dq_give))
     v3, v6 = hop(u3, -3), hop(u6, -6)
+    keep, back = _whole(
+        fold_own, [full(BLOCK, f32), full(BLOCK)], core_arg, v1, v2, v3, v6, gp, go, _bf(_final_matrix()), scalars=1
+    )
+    back, out, dq_mine, dq_take = tie((back, out, dq_mine, take[4]))
     out = out.reshape(2, n_head, -1, half).transpose(2, 1, 0, 3).reshape(-1, n_head * width)
-    dq_take = swap(dq_give)
     query_gradient = jnp.concatenate(
         [jnp.where(core == 0, dq_mine, dq_take), jnp.where(core == 0, dq_take, dq_mine)], axis=1
-    )
-    v3, v6, out, query_gradient = tie((v3, v6, out, query_gradient))
-    keep, back = _whole(
-        fold_own, [full(BLOCK, f32), full(BLOCK)], core_arg, v1, v2, v3, v6, gp, go, _bf(_final_matrix()), scalars=1
     )
     key_gradient, value_gradient = pl.pallas_call(
         finish,

time: 127 us -> 120 us (0.945)
  the two profiles are of different devices: /device:TPU:33 before, /device:TPU:49 now
where the time goes in v3:
time: 120 us; the launch traced here: 119 us
  starting transfers between devices  54 us (45%)
  blocking collectives  28.1 us (23%)
  waiting for transfers between devices  16.9 us (14%)
  Pallas kernels  13.7 us (11%)
  local copies, waits for them, and re-layouts  4.52 us (4%)
    ppermute x8, starting transfers between devices, hop(): return lax.ppermute(x, 'seq', [(i, j) for i, j in pairs if 0 <= j < size])  42.6 us
    ppermute x8, waiting for transfers between devices, hop(): return lax.ppermute(x, 'seq', [(i, j) for i, j in pairs if 0 <= j < size])  13.3 us
    all_to_all x1, blocking collectives, local(): lax.all_to_all(attended.reshape(2 * n_head, -1, half), ('seq', 'head'), 0...  11.7 us
    ppermute x3, starting transfers between devices, swap(): return lax.ppermute(x, 'seq', [(i, i ^ 1) for i in range(size)])  11.4 us
    pallas_call x1, Pallas kernels, local(): pl.pallas_call(attend, out_shape=[jax.ShapeDtypeStruct(s, d) for s, d in...  11.3 us
    all_to_all x1, blocking collectives, local(): lax.all_to_all(split, ('seq', 'head'), 0, 0, axis_index_groups=chip_group...  11.2 us
    all_gather x2, blocking collectives, both_cores(): return lax.all_gather(x, 'seq', axis=0, axis_index_groups=chip_cores)  5.14 us
    ppermute x3, waiting for transfers between devices, swap(): return lax.ppermute(x, 'seq', [(i, i ^ 1) for i in range(size)])  3.6 us
  transfers between devices with their start and end apart: 11, of which 4 were waited for; matrix products, arithmetic and copies ran while one was open for 2% of the time, Pallas kernels for 0%

profile of v3, /device:TPU:49, one launch (start us, length us, event | category | flops | bytes accessed | tf_op | source)
XLA Modules:
  0.0 119.0 jit_solution(10137317556813016146)
XLA Ops:
  0.6 0.0 copy-start.14
  0.6 2.8 %all-gather = bf16[256,1024]{1,0:T(8,128)(2,1)S(1)} all-gather(bf16[128,1024]{1,0:T(8,128)(2,1)} %param.14), channel_id=2, replica_groups={{0,4},{8,12},{16,20},{24,28},{32,36},{40,44},{48,52},{56,60},{64,68},{7..., dimensions={0}, use_global_device_ids=true | all-gather | bytes 786432 | tf_op jit(solution)/shard_map/all_gather | solution.py:287
  3.5 0.0 copy-done.14
  3.5 2.3 %all-gather.1 = bf16[256,1024]{1,0:T(8,128)(2,1)S(1)} all-gather(bf16[128,1024]{1,0:T(8,128)(2,1)S(1)} %copy-done.14), channel_id=3, replica_groups={{0,4},{8,12},{16,20},{24,28},{32,36},{40,44},{48,52},{56,60},{64,68},{7..., dimensions={0}, use_global_device_ids=true | all-gather | bytes 786432 | tf_op jit(solution)/shard_map/all_gather | solution.py:287
  5.8 0.0 copy-done.8
  5.8 0.5 shard_map.156
  6.3 0.0 copy-done
  6.3 0.3 copy-done.1
  6.6 11.0 %collective-permute-start = (bf16[2,32,1024]{2,1,0:T(8,128)(2,1)S(1)}, bf16[2,32,1024]{2,1,0:T(8,128)(2,1)S(1)}, u32[]{:S(2)}, u32[]{:S(2)}) collective-permute-start(bf16[2,32,1024]{2,1,0:T(8,128)(2,1)S(1)} %get-tuple-element.47), channel_id=1, source_target_pairs={{0,24},{8,32},{16,40},{24,48},{28,4},{32,56},{36,12},{40,64},{44,2... | collective-permute-start | bytes 393224 | tf_op jit(solution)/shard_map/ppermute | solution.py:281
  17.6 6.1 %collective-permute-start.1 = (bf16[2,16,1024]{2,1,0:T(8,128)(2,1)S(1)}, bf16[2,16,1024]{2,1,0:T(8,128)(2,1)S(1)}, u32[]{:S(2)}, u32[]{:S(2)}) collective-permute-start(bf16[2,16,1024]{2,1,0:T(8,128)(2,1)S(1)} %get-tuple-element.48), channel_id=1, source_target_pairs={{0,48},{8,56},{16,64},{24,72},{32,80},{40,88},{48,96},{52,4},{56,1... | collective-permute-start | bytes 196616 | tf_op jit(solution)/shard_map/ppermute | solution.py:281
  23.7 6.7 %collective-permute-done.1.six_ref = bf16[2,16,1024]{2,1,0:T(8,128)(2,1)S(1)} collective-permute-done((bf16[2,16,1024]{2,1,0:T(8,128)(2,1)S(1)}, bf16[2,16,1024]{2,1,0:T(8,128)(2,1)S(1)}, u32[]{:S(2)}, u32[]{:S(2)}) %collective-permute-start.1) | collective-permute-done | bytes 65568 | tf_op jit(solution)/shard_map/ppermute | solution.py:281
  30.4 0.0 collective-permute-done.three_ref
  30.4 0.0 copy-done.11
  30.4 0.2 shard_map.157
  30.6 3.3 %collective-permute-start.2 = (bf16[2,136,1024]{2,1,0:T(8,128)(2,1)S(1)}, bf16[2,136,1024]{2,1,0:T(8,128)(2,1)S(1)}, u32[]{:S(2)}, u32[]{:S(2)}) collective-permute-start(bf16[2,136,1024]{2,1,0:T(8,128)(2,1)S(1)} %get-tuple-element.56), channel_id=1, source_target_pairs={{0,8},{8,16},{12,4},{16,24},{20,12},{24,32},{28,20},{32,40},{36,28... | collective-permute-start | bytes 1671176 | tf_op jit(solution)/shard_map/ppermute | solution.py:281
  33.9 6.3 %collective-permute-start.3 = (bf16[2,72,1024]{2,1,0:T(8,128)(2,1)S(1)}, bf16[2,72,1024]{2,1,0:T(8,128)(2,1)S(1)}, u32[]{:S(2)}, u32[]{:S(2)}) collective-permute-start(bf16[2,72,1024]{2,1,0:T(8,128)(2,1)S(1)} %get-tuple-element.57), channel_id=1, source_target_pairs={{0,16},{8,24},{16,32},{20,4},{24,40},{28,12},{32,48},{36,20},{40,5... | collective-permute-start | bytes 884744 | tf_op jit(solution)/shard_map/ppermute | solution.py:281
  40.2 0.0 copy-done.15
  40.2 0.2 reshape.30
  40.4 0.1 copy.17
  40.5 0.0 copy-start.5
  40.5 11.2 %all_to_all.10 = bf16[8,32,512]{2,1,0:T(8,128)(2,1)S(1)} all-to-all(bf16[8,32,512]{2,1,0:T(8,128)(2,1)S(1)} %bitcast.20), channel_id=1, replica_groups={{0,1,2,3,4,5,6,7},{8,9,10,11,12,13,14,15},{16,17,18,19,20,21,22,23},{24..., dimensions={0} | all-to-all | bytes 524288 | tf_op jit(solution)/shard_map/all_to_all | solution.py:311
  51.7 0.0 collective-permute-done.3.two_ref
  51.7 0.0 collective-permute-done.2.one_ref
  51.7 0.0 copy-done.5
  51.7 0.0 copy-start.17
  51.8 0.0 copy-start.7
  51.8 0.0 copy-start.9
  51.8 0.0 copy-start.10
  51.8 0.1 shard_map.158
  51.9 0.0 copy-start.2
  51.9 0.8 copy-done.2
  52.8 2.4 %collective-permute-start.4 = (bf16[5,128,512]{2,1,0:T(8,128)(2,1)S(1)}, bf16[5,128,512]{2,1,0:T(8,128)(2,1)S(1)}, u32[]{:S(2)}, u32[]{:S(2)}) collective-permute-start(bf16[5,128,512]{2,1,0:T(8,128)(2,1)S(1)} %get-tuple-element.64), channel_id=1, source_target_pairs={{0,4},{4,0},{8,12},{12,8},{16,20},{20,16},{24,28},{28,24},{32,36},... | collective-permute-start | bytes 1966088 | tf_op jit(solution)/shard_map/ppermute | solution.py:284
  55.2 0.0 copy-done.17
  55.2 0.0 copy-done.16
  55.2 1.7 %collective-permute-done.4.y_ref = bf16[5,128,512]{2,1,0:T(8,128)(2,1)S(1)} collective-permute-done((bf16[5,128,512]{2,1,0:T(8,128)(2,1)S(1)}, bf16[5,128,512]{2,1,0:T(8,128)(2,1)S(1)}, u32[]{:S(2)}, u32[]{:S(2)}) %collective-permute-start.4) | collective-permute-done | bytes 655392 | tf_op jit(solution)/shard_map/ppermute | solution.py:284
  56.9 0.9 copy-done.13
  57.7 0.0 copy-done.7
  57.7 0.0 copy-done.9
  57.7 0.0 copy-done.10
  57.7 11.3 %shard_map.159 = (bf16[256,512]{1,0:T(8,128)(2,1)S(1)}, bf16[128,512]{1,0:T(8,128)(2,1)S(1)}, f32[2,128,512]{2,1,0:T(8,128)S(1)}, f32[2,128,512]{2,1,0:T(8,128)}...) custom-call(s32[1]{0:T(128)} %bitcast.core_ref, bf16[2,128,1024]{2,1,0:T(8,128)(2,1)} %bitcast.14, ...), custom_call_target="tpu_custom_call" | custom-call | tf_op jit(solution)/shard_map/pallas_call | solution.py:327
  69.0 2.3 %collective-permute-start.5 = (bf16[5,128,512]{2,1,0:T(8,128)(2,1)}, bf16[5,128,512]{2,1,0:T(8,128)(2,1)S(1)}, u32[]{:S(2)}, u32[]{:S(2)}) collective-permute-start(bf16[5,128,512]{2,1,0:T(8,128)(2,1)} %get-tuple-element.66), channel_id=1, source_target_pairs={{0,4},{4,0},{8,12},{12,8},{16,20},{20,16},{24,28},{28,24},{32,36},... | collective-permute-start | bytes 1966088 | tf_op jit(solution)/shard_map/ppermute | solution.py:284
  71.3 1.9 %collective-permute-done.5.take_ref = bf16[5,128,512]{2,1,0:T(8,128)(2,1)S(1)} collective-permute-done((bf16[5,128,512]{2,1,0:T(8,128)(2,1)}, bf16[5,128,512]{2,1,0:T(8,128)(2,1)S(1)}, u32[]{:S(2)}, u32[]{:S(2)}) %collective-permute-start.5) | collective-permute-done | bytes 655392 | tf_op jit(solution)/shard_map/ppermute | solution.py:284
  73.2 1.0 copy-done.4
  74.2 0.1 shard_map.160
  74.3 3.6 %collective-permute-start.6 = (bf16[2,136,1024]{2,1,0:T(8,128)(2,1)S(1)}, bf16[2,136,1024]{2,1,0:T(8,128)(2,1)S(1)}, u32[]{:S(2)}, u32[]{:S(2)}) collective-permute-start(bf16[2,136,1024]{2,1,0:T(8,128)(2,1)S(1)} %get-tuple-element.70), channel_id=1, source_target_pairs={{4,12},{8,0},{12,20},{16,8},{20,28},{24,16},{28,36},{32,24},{36,44... | collective-permute-start | bytes 1671176 | tf_op jit(solution)/shard_map/ppermute | solution.py:281
  77.9 2.9 %collective-permute-start.7 = (bf16[2,72,1024]{2,1,0:T(8,128)(2,1)S(1)}, bf16[2,72,1024]{2,1,0:T(8,128)(2,1)S(1)}, u32[]{:S(2)}, u32[]{:S(2)}) collective-permute-start(bf16[2,72,1024]{2,1,0:T(8,128)(2,1)S(1)} %get-tuple-element.71), channel_id=1, source_target_pairs={{4,20},{12,28},{16,0},{20,36},{24,8},{28,44},{32,16},{36,52},{40,2... | collective-permute-start | bytes 884744 | tf_op jit(solution)/shard_map/ppermute | solution.py:281
  80.8 0.0 copy-start.12
  80.9 11.7 %all_to_all.11 = bf16[8,32,512]{2,1,0:T(8,128)(2,1)S(1)} all-to-all(bf16[8,32,512]{2,1,0:T(8,128)(2,1)S(1)} %bitcast.18), channel_id=1, replica_groups={{0,1,2,3,4,5,6,7},{8,9,10,11,12,13,14,15},{16,17,18,19,20,21,22,23},{24..., dimensions={0} | all-to-all | bytes 524288 | tf_op jit(solution)/shard_map/all_to_all | solution.py:345
  92.6 0.0 collective-permute-done.7.two_ref
  92.6 0.0 collective-permute-done.6.one_ref
  92.6 0.0 copy-start.3
  92.6 0.2 shard_map.161
  92.8 2.9 %collective-permute-start.8 = (bf16[2,32,1024]{2,1,0:T(8,128)(2,1)S(1)}, bf16[2,32,1024]{2,1,0:T(8,128)(2,1)S(1)}, u32[]{:S(2)}, u32[]{:S(2)}) collective-permute-start(bf16[2,32,1024]{2,1,0:T(8,128)(2,1)S(1)} %get-tuple-element.76), channel_id=1, source_target_pairs={{4,28},{12,36},{20,44},{24,0},{28,52},{32,8},{36,60},{40,16},{44,6... | collective-permute-start | bytes 393224 | tf_op jit(solution)/shard_map/ppermute | solution.py:281
  95.7 0.0 copy-start.6
  95.7 6.5 %collective-permute-start.9 = (bf16[2,16,1024]{2,1,0:T(8,128)(2,1)S(1)}, bf16[2,16,1024]{2,1,0:T(8,128)(2,1)S(1)}, u32[]{:S(2)}, u32[]{:S(2)}) collective-permute-start(bf16[2,16,1024]{2,1,0:T(8,128)(2,1)S(1)} %get-tuple-element.77), channel_id=1, source_target_pairs={{4,52},{12,60},{20,68},{28,76},{36,84},{44,92},{48,0},{52,100},{56... | collective-permute-start | bytes 196616 | tf_op jit(solution)/shard_map/ppermute | solution.py:281
  102.3 6.6 %collective-permute-done.9.six_ref = bf16[2,16,1024]{2,1,0:T(8,128)(2,1)S(1)} collective-permute-done((bf16[2,16,1024]{2,1,0:T(8,128)(2,1)S(1)}, bf16[2,16,1024]{2,1,0:T(8,128)(2,1)S(1)}, u32[]{:S(2)}, u32[]{:S(2)}) %collective-permute-start.9) | collective-permute-done | bytes 65568 | tf_op jit(solution)/shard_map/ppermute | solution.py:281
  108.9 0.0 collective-permute-done.8.three_ref
  108.9 0.5 shard_map.162
  109.4 6.8 %collective-permute-start.10 = (bf16[2,128,1024]{2,1,0:T(8,128)(2,1)S(1)}, bf16[2,128,1024]{2,1,0:T(8,128)(2,1)S(1)}, u32[]{:S(2)}, u32[]{:S(2)}) collective-permute-start(bf16[2,128,1024]{2,1,0:T(8,128)(2,1)S(1)} %get-tuple-element.87), channel_id=1, source_target_pairs={{0,4},{4,0},{8,12},{12,8},{16,20},{20,16},{24,28},{28,24},{32,36},... | collective-permute-start | bytes 1572872 | tf_op jit(solution)/shard_map/ppermute | solution.py:284
  116.2 0.3 copy.20
  116.5 0.9 reshape.35
  117.4 0.7 pad_maximum_fusion
  118.1 0.0 collective-permute-done.10.take_ref
  118.1 0.9 shard_map.163
  (14 shorter events, 0.1 us)
Async XLA Ops:
  0.6 2.8 %copy-start.14 = (bf16[128,1024]{1,0:T(8,128)(2,1)S(1)}, bf16[128,1024]{1,0:T(8,128)(2,1)}, u32[]{:S(2)}) copy-start(bf16[128,1024]{1,0:T(8,128)(2,1)} %param.15) | copy-start | bytes 786436
  3.5 2.8 %copy-start = (bf16[256,1024]{1,0:T(8,128)(2,1)}, bf16[256,1024]{1,0:T(8,128)(2,1)S(1)}, u32[]{:S(2)}) copy-start(bf16[256,1024]{1,0:T(8,128)(2,1)S(1)} %all-gather) | copy-start | bytes 1572868
  3.5 2.3 %copy-start.8 = (bf16[240,256]{1,0:T(8,128)(2,1)S(1)}, bf16[240,256]{1,0:T(8,128)(2,1)}, u32[]{:S(2)}) copy-start(bf16[240,256]{1,0:T(8,128)(2,1)} %constant.39.clone.own_ref) | copy-start | bytes 368644
  5.8 0.8 copy-start.1
  5.8 24.6 %copy-start.11 = (bf16[64,48]{1,0:T(8,128)(2,1)S(1)}, bf16[64,48]{1,0:T(8,128)(2,1)}, u32[]{:S(2)}) copy-start(bf16[64,48]{1,0:T(8,128)(2,1)} %constant.40.clone.w_ref) | copy-start | bytes 18436
  6.6 23.8 %collective-permute-start = (bf16[2,32,1024]{2,1,0:T(8,128)(2,1)S(1)}, bf16[2,32,1024]{2,1,0:T(8,128)(2,1)S(1)}, u32[]{:S(2)}, u32[]{:S(2)}) collective-permute-start(bf16[2,32,1024]{2,1,0:T(8,128)(2,1)S(1)} %get-tuple-element.47), channel_id=1, source_target_pairs={{0,24},{8,32},{16,40},{24,48},{28,4},{32,56},{36,12},{40,64},{44,2... | collective-permute-start | bytes 393224 | tf_op jit(solution)/shard_map/ppermute | solution.py:281
  17.6 12.8 %collective-permute-start.1 = (bf16[2,16,1024]{2,1,0:T(8,128)(2,1)S(1)}, bf16[2,16,1024]{2,1,0:T(8,128)(2,1)S(1)}, u32[]{:S(2)}, u32[]{:S(2)}) collective-permute-start(bf16[2,16,1024]{2,1,0:T(8,128)(2,1)S(1)} %get-tuple-element.48), channel_id=1, source_target_pairs={{0,48},{8,56},{16,64},{24,72},{32,80},{40,88},{48,96},{52,4},{56,1... | collective-permute-start | bytes 196616 | tf_op jit(solution)/shard_map/ppermute | solution.py:281
  30.4 9.8 %copy-start.15 = (bf16[32,4096]{1,0:T(8,128)(2,1)S(1)}, bf16[32,4096]{1,0:T(8,128)(2,1)}, u32[]{:S(2)}) copy-start(bf16[32,4096]{1,0:T(8,128)(2,1)} %param.16) | copy-start | bytes 786436
  30.6 21.2 %collective-permute-start.2 = (bf16[2,136,1024]{2,1,0:T(8,128)(2,1)S(1)}, bf16[2,136,1024]{2,1,0:T(8,128)(2,1)S(1)}, u32[]{:S(2)}, u32[]{:S(2)}) collective-permute-start(bf16[2,136,1024]{2,1,0:T(8,128)(2,1)S(1)} %get-tuple-element.56), channel_id=1, source_target_pairs={{0,8},{8,16},{12,4},{16,24},{20,12},{24,32},{28,20},{32,40},{36,28... | collective-permute-start | bytes 1671176 | tf_op jit(solution)/shard_map/ppermute | solution.py:281
  33.9 17.9 %collective-permute-start.3 = (bf16[2,72,1024]{2,1,0:T(8,128)(2,1)S(1)}, bf16[2,72,1024]{2,1,0:T(8,128)(2,1)S(1)}, u32[]{:S(2)}, u32[]{:S(2)}) collective-permute-start(bf16[2,72,1024]{2,1,0:T(8,128)(2,1)S(1)} %get-tuple-element.57), channel_id=1, source_target_pairs={{0,16},{8,24},{16,32},{20,4},{24,40},{28,12},{32,48},{36,20},{40,5... | collective-permute-start | bytes 884744 | tf_op jit(solution)/shard_map/ppermute | solution.py:281
  40.5 11.3 %copy-start.5 = (bf16[128,1024]{1,0:T(8,128)(2,1)S(1)}, bf16[128,1024]{1,0:T(8,128)(2,1)}, u32[]{:S(2)}) copy-start(bf16[128,1024]{1,0:T(8,128)(2,1)} %q_ref.1) | copy-start | bytes 786436
  51.7 3.4 %copy-start.17 = (f32[2,640]{1,0:T(2,128)S(1)}, f32[2,640]{1,0:T(2,128)}, u32[]{:S(2)}) copy-start(f32[2,640]{1,0:T(2,128)} %constant.42.clone) | copy-start | bytes 15364
  51.8 6.0 %copy-start.7 = (bf16[256,192]{1,0:T(8,128)(2,1)S(1)}, bf16[256,192]{1,0:T(8,128)(2,1)}, u32[]{:S(2)}) copy-start(bf16[256,192]{1,0:T(8,128)(2,1)} %constant.44.clone.derive_t_ref) | copy-start | bytes 294916
  51.8 6.0 %copy-start.9 = (bf16[192,256]{1,0:T(8,128)(2,1)S(1)}, bf16[192,256]{1,0:T(8,128)(2,1)}, u32[]{:S(2)}) copy-start(bf16[192,256]{1,0:T(8,128)(2,1)} %constant.43.clone.derive_ref) | copy-start | bytes 294916
  51.8 5.9 %copy-start.10 = (bf16[128,64]{1,0:T(8,128)(2,1)S(1)}, bf16[128,64]{1,0:T(8,128)(2,1)}, u32[]{:S(2)}) copy-start(bf16[128,64]{1,0:T(8,128)(2,1)} %constant.45.clone.spread_ref) | copy-start | bytes 49156
  51.9 0.8 copy-start.2
  52.7 2.4 %copy-start.16 = (s32[2,640]{1,0:T(2,128)S(1)}, s32[2,640]{1,0:T(2,128)}, u32[]{:S(2)}) copy-start(s32[2,640]{1,0:T(2,128)} %constant.41.clone) | copy-start | bytes 15364
  52.8 4.1 %collective-permute-start.4 = (bf16[5,128,512]{2,1,0:T(8,128)(2,1)S(1)}, bf16[5,128,512]{2,1,0:T(8,128)(2,1)S(1)}, u32[]{:S(2)}, u32[]{:S(2)}) collective-permute-start(bf16[5,128,512]{2,1,0:T(8,128)(2,1)S(1)} %get-tuple-element.64), channel_id=1, source_target_pairs={{0,4},{4,0},{8,12},{12,8},{16,20},{20,16},{24,28},{28,24},{32,36},... | collective-permute-start | bytes 1966088 | tf_op jit(solution)/shard_map/ppermute | solution.py:284
  56.9 0.9 copy-start.13
  69.0 4.2 %collective-permute-start.5 = (bf16[5,128,512]{2,1,0:T(8,128)(2,1)}, bf16[5,128,512]{2,1,0:T(8,128)(2,1)S(1)}, u32[]{:S(2)}, u32[]{:S(2)}) collective-permute-start(bf16[5,128,512]{2,1,0:T(8,128)(2,1)} %get-tuple-element.66), channel_id=1, source_target_pairs={{0,4},{4,0},{8,12},{12,8},{16,20},{20,16},{24,28},{28,24},{32,36},... | collective-permute-start | bytes 1966088 | tf_op jit(solution)/shard_map/ppermute | solution.py:284
  73.2 1.0 copy-start.4
  74.3 18.3 %collective-permute-start.6 = (bf16[2,136,1024]{2,1,0:T(8,128)(2,1)S(1)}, bf16[2,136,1024]{2,1,0:T(8,128)(2,1)S(1)}, u32[]{:S(2)}, u32[]{:S(2)}) collective-permute-start(bf16[2,136,1024]{2,1,0:T(8,128)(2,1)S(1)} %get-tuple-element.70), channel_id=1, source_target_pairs={{4,12},{8,0},{12,20},{16,8},{20,28},{24,16},{28,36},{32,24},{36,44... | collective-permute-start | bytes 1671176 | tf_op jit(solution)/shard_map/ppermute | solution.py:281
  77.9 14.7 %collective-permute-start.7 = (bf16[2,72,1024]{2,1,0:T(8,128)(2,1)S(1)}, bf16[2,72,1024]{2,1,0:T(8,128)(2,1)S(1)}, u32[]{:S(2)}, u32[]{:S(2)}) collective-permute-start(bf16[2,72,1024]{2,1,0:T(8,128)(2,1)S(1)} %get-tuple-element.71), channel_id=1, source_target_pairs={{4,20},{12,28},{16,0},{20,36},{24,8},{28,44},{32,16},{36,52},{40,2... | collective-permute-start | bytes 884744 | tf_op jit(solution)/shard_map/ppermute | solution.py:281
  80.8 11.8 %copy-start.12 = (bf16[48,64]{1,0:T(8,128)(2,1)S(1)}, bf16[48,64]{1,0:T(8,128)(2,1)}, u32[]{:S(2)}) copy-start(bf16[48,64]{1,0:T(8,128)(2,1)} %constant.46.clone.w_ref) | copy-start | bytes 18436
  92.6 16.3 %copy-start.3 = (f32[2,128,512]{2,1,0:T(8,128)S(1)}, f32[2,128,512]{2,1,0:T(8,128)}, u32[]{:S(2)}) copy-start(f32[2,128,512]{2,1,0:T(8,128)} %get-tuple-element.79.go_ref) | copy-start | bytes 1572868
  92.8 16.1 %collective-permute-start.8 = (bf16[2,32,1024]{2,1,0:T(8,128)(2,1)S(1)}, bf16[2,32,1024]{2,1,0:T(8,128)(2,1)S(1)}, u32[]{:S(2)}, u32[]{:S(2)}) collective-permute-start(bf16[2,32,1024]{2,1,0:T(8,128)(2,1)S(1)} %get-tuple-element.76), channel_id=1, source_target_pairs={{4,28},{12,36},{20,44},{24,0},{28,52},{32,8},{36,60},{40,16},{44,6... | collective-permute-start | bytes 393224 | tf_op jit(solution)/shard_map/ppermute | solution.py:281
  95.7 13.2 %copy-start.6 = (bf16[256,256]{1,0:T(8,128)(2,1)S(1)}, bf16[256,256]{1,0:T(8,128)(2,1)}, u32[]{:S(2)}) copy-start(bf16[256,256]{1,0:T(8,128)(2,1)} %constant.47.clone.w_ref) | copy-start | bytes 393220
  95.7 13.2 %collective-permute-start.9 = (bf16[2,16,1024]{2,1,0:T(8,128)(2,1)S(1)}, bf16[2,16,1024]{2,1,0:T(8,128)(2,1)S(1)}, u32[]{:S(2)}, u32[]{:S(2)}) collective-permute-start(bf16[2,16,1024]{2,1,0:T(8,128)(2,1)S(1)} %get-tuple-element.77), channel_id=1, source_target_pairs={{4,52},{12,60},{20,68},{28,76},{36,84},{44,92},{48,0},{52,100},{56... | collective-permute-start | bytes 196616 | tf_op jit(solution)/shard_map/ppermute | solution.py:281
  109.4 8.7 %collective-permute-start.10 = (bf16[2,128,1024]{2,1,0:T(8,128)(2,1)S(1)}, bf16[2,128,1024]{2,1,0:T(8,128)(2,1)S(1)}, u32[]{:S(2)}, u32[]{:S(2)}) collective-permute-start(bf16[2,128,1024]{2,1,0:T(8,128)(2,1)S(1)} %get-tuple-element.87), channel_id=1, source_target_pairs={{0,4},{4,0},{8,12},{12,8},{16,20},{20,16},{24,28},{28,24},{32,36},... | collective-permute-start | bytes 1572872 | tf_op jit(solution)/shard_map/ppermute | solution.py:284

commit v4 on v3

--- a/solution.py
+++ b/solution.py
@@ -15,8 +15,10 @@
 MASKED = -1e30
 SCALE = 1.0 / math.sqrt(HEAD_DIM)
 VMEM = 4 * 1024 * 1024
-WIDE_VMEM = 52 * 1024 * 1024
+WIDE_VMEM = 40 * 1024 * 1024
+FULL_VMEM = 56 * 1024 * 1024
 HALF = 512
+PER_STEP = 2
 
 SIDE_LEVELS = [0] + [1] + [2] * 2 + [3] * 4 + [4] * 8
 VIEW = {1: [1, 2, 7, 8, 13, 14], 2: [3, 4, 9, 10, 15], 3: [5, 6], 6: [11, 12]}
@@ -138,11 +140,30 @@
     return pl.ds(pl.multiple_of(core * HALF, HALF), HALF)
 
 
-def pack_own(core_ref, k_ref, v_ref, own_ref, three_ref, six_ref, one_own_ref, two_own_ref, ones_ref):
+def pack_coarse(k_ref, v_ref, out_ref):
+    row = lax.broadcasted_iota(jnp.int32, (32, BLOCK), 0)
+    col = lax.broadcasted_iota(jnp.int32, (32, BLOCK), 1)
+    three = jnp.where(row == (col >> 3), 0.125, 0.0)
+    pool = jnp.where(row - 16 == (col >> 4), 0.0625, three).astype(jnp.bfloat16)
+    for part, ref in enumerate((k_ref, v_ref)):
+        out_ref[part] = _dot(pool, ref[...]).astype(jnp.bfloat16)
+
+
+def pack_far(core_ref, both_ref, three_ref, six_ref):
+    core = core_ref[0]
+    for part in range(2):
+        mine, other = both_ref[core, part], both_ref[1 - core, part]
+        three_ref[part, 0:16] = other[0:16]
+        three_ref[part, 16:32] = mine[0:16]
+        fours = [rows[16:32].astype(jnp.float32)[0:8] for rows in (other, mine)]
+        six_ref[part] = jnp.concatenate(fours, axis=0).astype(jnp.bfloat16)
+
+
+def pack_own(core_ref, k_ref, v_ref, own_ref, one_own_ref, two_own_ref, ones_ref):
     core = core_ref[0]
     for part, ref in enumerate((k_ref, v_ref)):
         levels = _dot(own_ref[...], jnp.concatenate([ref[core], ref[1 - core]], axis=0))
-        for out, distance in ((three_ref, 3), (six_ref, 6), (one_own_ref, 1), (two_own_ref, 2)):
+        for out, distance in ((one_own_ref, 1), (two_own_ref, 2)):
             spans = [_own_rows(level, block) for level, block in _own_sent(distance)]
             out[part] = jnp.concatenate([levels[a:b] for a, b in spans], axis=0).astype(jnp.bfloat16)
         one_own = jnp.concatenate([ref[core, :, _half(core)], ref[1 - core, :, _half(core)]], axis=0)
@@ -173,7 +194,8 @@
     o_ref, dq_ref, gp_ref, go_ref, gx_ref, gy_ref,
 ):
     core = core_ref[0]
-    lanes = pl.ds(pl.multiple_of(pl.program_id(0) * HEAD_DIM, HEAD_DIM), HEAD_DIM)
+    width = PER_STEP * HEAD_DIM
+    lanes = pl.ds(pl.multiple_of(pl.program_id(0) * width, width), width)
     sets_p, sets_o = [], []
     for part, ref in enumerate((k_ref, v_ref)):
         x = jnp.concatenate([x_ref[2 * part], x_ref[2 * part + 1]], axis=0)
@@ -182,29 +204,39 @@
         y_derived = _dot(derive_ref[...], y).astype(jnp.bfloat16)
         sets_p.append(jnp.concatenate([ref[core], ones_ref[part, 64:128], x, y_derived], axis=0))
         sets_o.append(jnp.concatenate([ref[1 - core], ones_ref[part, 0:64], y, x_derived], axis=0))
-    grads = []
-    for block, (keys, values) in enumerate((sets_p, sets_o)):
-        place = core if block == 0 else 1 - core
-        here = pl.ds(pl.multiple_of(place * BLOCK, BLOCK), BLOCK)
-        q = (x_ref, y_ref)[block][4]
-        do = do_ref[here]
-        scores = _outer(q, keys) * SCALE + bias_ref[block : block + 1]
-        highest = jnp.max(scores, axis=1, keepdims=True)
-        raised = jnp.exp(scores - highest)
+    here = [pl.ds(pl.multiple_of(place * BLOCK, BLOCK), BLOCK) for place in (core, 1 - core)]
+    items = []
+    for head in range(PER_STEP):
+        cols = slice(head * HEAD_DIM, (head + 1) * HEAD_DIM)
+        for block, (keys, values) in enumerate((sets_p, sets_o)):
+            q = (x_ref, y_ref)[block][4, :, cols]
+            items.append((block, keys[:, cols], values[:, cols], q, do_ref[here[block], cols]))
+    scores = [_outer(q, keys) for _, keys, _, q, _ in items]
+    weight_grads = [_outer(do, values) for _, _, values, _, do in items]
+    lows, score_grads = [], []
+    for (block, *_), raw, weight_grad in zip(items, scores, weight_grads, strict=True):
+        biased = raw * SCALE + bias_ref[block : block + 1]
+        raised = jnp.exp(biased - jnp.max(biased, axis=1, keepdims=True))
         weights = raised * (1.0 / jnp.sum(raised, axis=1, keepdims=True))
-        low = weights.astype(jnp.bfloat16)
-        o_ref[here, lanes] = _dot(low, values).astype(jnp.bfloat16)
-        weight_grad = _outer(do, values)
         row_term = jnp.sum(weights * weight_grad, axis=1, keepdims=True)
-        score_grad = (weights * ((weight_grad - row_term) * SCALE)).astype(jnp.bfloat16)
-        dq = _dot(score_grad, keys).astype(jnp.bfloat16)
-        if block == 0:
-            dq_ref[:, lanes] = dq
-        else:
-            gy_ref[4, :, lanes] = dq
-        grads.append((_pull(score_grad, q), _pull(low, do)))
-    for part in range(2):
-        gp, go = grads[0][part], grads[1][part]
+        lows.append(weights.astype(jnp.bfloat16))
+        score_grads.append((weights * ((weight_grad - row_term) * SCALE)).astype(jnp.bfloat16))
+    outs, dqs, dks, dvs = [], [], [], []
+    for (_, keys, values, q, do), low, score_grad in zip(items, lows, score_grads, strict=True):
+        outs.append(_dot(low, values))
+        dqs.append(_dot(score_grad, keys))
+        dks.append(_pull(score_grad, q))
+        dvs.append(_pull(low, do))
+
+    def heads_of(results, block):
+        return jnp.concatenate(results[block::2], axis=1)
+
+    for block in range(2):
+        o_ref[here[block], lanes] = heads_of(outs, block).astype(jnp.bfloat16)
+    dq_ref[:, lanes] = heads_of(dqs, 0).astype(jnp.bfloat16)
+    gy_ref[4, :, lanes] = heads_of(dqs, 1).astype(jnp.bfloat16)
+    for part, results in enumerate((dks, dvs)):
+        gp, go = heads_of(results, 0), heads_of(results, 1)
         gx = gp[192:448] + _dot(derive_t_ref[...], go[448:640].astype(jnp.bfloat16))
         gy = go[192:448] + _dot(derive_t_ref[...], gp[448:640].astype(jnp.bfloat16))
         for g, ref in ((gx, gx_ref), (gy, gy_ref)):
@@ -271,7 +303,6 @@
     core = lax.rem(seq, 2)
     width = queries.shape[1]
     half = width // 2
-    heads = half // HEAD_DIM
     n_head = lax.axis_size("head")
     chip_cores = [[2 * i, 2 * i + 1] for i in range(size // 2)]
     chip_groups = [[g * 2 * n_head + m for m in range(2 * n_head)] for g in range(size // 2)]
@@ -294,14 +325,24 @@
     def part(n, dtype=bf16):
         return ((2, n, half), dtype)
 
-    keys, values = both_cores(key_states), both_cores(value_states)
     core_arg = core.reshape(1).astype(jnp.int32)
-
-    t3, t6, own1, own2, ones = _whole(
-        pack_own, [full(32), full(16), full(96), full(48), part(128)],
-        core_arg, keys, values, _bf(_own_matrix()), scalars=1,
+    whole_block = pl.BlockSpec((BLOCK, width), lambda i: (0, 0))
+    mine = pl.pallas_call(
+        pack_coarse,
+        out_shape=jax.ShapeDtypeStruct(*full(32)),
+        grid=(1,),
+        in_specs=[whole_block] * 2,
+        out_specs=VMEM_SPEC,
+        compiler_params=pltpu.CompilerParams(vmem_limit_bytes=FULL_VMEM),
+    )(key_states, value_states)
+    t3, t6 = _whole(pack_far, [full(32), full(16)], core_arg, both_cores(mine), scalars=1)
+    t3, t6, late_keys, late_values = tie((t3, t6, key_states, value_states))
+    r3, r6 = hop(t3, 3), hop(t6, 6)
+
+    keys, values = both_cores(late_keys), both_cores(late_values)
+    own1, own2, ones = _whole(
+        pack_own, [full(96), full(48), part(128)], core_arg, keys, values, _bf(_own_matrix()), scalars=1
     )
-    r3, r6 = hop(t3, 3), hop(t6, 6)
     r3, r6, late_cotangent = tie((r3, r6, cotangent))
 
     t1, t2 = _whole(pack_on, [full(136), full(72)], r3, r6, own1, own2, _bf(_pass_matrix()))
@@ -318,8 +359,10 @@
     target = seq + (2 * core - 1) * jnp.asarray(offsets)
     bias = jnp.where((target >= 0) & (target < size), jnp.asarray(raise_by, f32), MASKED).astype(f32)
 
-    pick = pl.BlockSpec((2, BLOCK, HEAD_DIM), lambda h, c: (0, 0, c[0] * heads + h))
-    cut = lambda n: pl.BlockSpec((n, BLOCK, HEAD_DIM), lambda h, c: (0, 0, h))
+    step = PER_STEP * HEAD_DIM
+    steps = half // step
+    pick = pl.BlockSpec((2, BLOCK, step), lambda h, c: (0, 0, c[0] * steps + h))
+    cut = lambda n: pl.BlockSpec((n, BLOCK, step), lambda h, c: (0, 0, h))
     const = lambda *dims: pl.BlockSpec(dims, lambda h, c: (0, 0))
     derive = _derive_matrix()
     spread = _own_matrix()[0:64, 0:BLOCK].T.copy()
@@ -329,9 +372,9 @@
         out_shape=[jax.ShapeDtypeStruct(s, d) for s, d in outs],
         grid_spec=pltpu.PrefetchScalarGridSpec(
             num_scalar_prefetch=1,
-            grid=(heads,),
+            grid=(steps,),
             in_specs=[pick] * 2
-            + [pl.BlockSpec((2 * BLOCK, HEAD_DIM), lambda h, c: (0, h)), cut(2), cut(5), cut(5)]
+            + [pl.BlockSpec((2 * BLOCK, step), lambda h, c: (0, h)), cut(2), cut(5), cut(5)]
             + [const(192, 256), const(256, 192), const(128, 64), const(2, 640)],
             out_specs=[VMEM_SPEC] * len(outs),
         ),

time: 120 us -> 111 us (0.925)
  waiting for transfers between devices: 16.9 us -> 11.3 us
  local copies, waits for them, and re-layouts: 4.52 us -> 1.5 us
  Pallas kernels: 13.7 us -> 10.8 us
  blocking collectives: 28.1 us -> 31 us
    pallas_call x1, Pallas kernels: 11.3 us -> 4.83 us  [local(): pl.pallas_call(attend, out_shape=[jax.ShapeDtypeStruct(s, d) for s, d in...]
    ppermute x8, waiting for transfers between devices: 13.3 us -> 7.66 us  [hop(): return lax.ppermute(x, 'seq', [(i, j) for i, j in pairs if 0 <= j < size])]
    unnamed x36 -> x26, local copies, waits for them, and re-layouts: 3.09 us -> 0.07 us
    all_gather x2 -> x3, blocking collectives: 5.14 us -> 7.79 us  [both_cores(): return lax.all_gather(x, 'seq', axis=0, axis_index_groups=chip_cores)]
    pallas_call x0 -> x1, Pallas kernels: none -> 1.89 us  [local(): pl.pallas_call(pack_coarse, out_shape=jax.ShapeDtypeStruct(*full(32)), gr...]
    pallas_call x6 -> x7, Pallas kernels: 1.57 us -> 3.22 us  [_whole(): pl.pallas_call(body, out_shape=[jax.ShapeDtypeStruct(s, d) for s, d in ou...]
where the time goes in v4:
time: 111 us; the launch traced here: 110 us
  starting transfers between devices  53.9 us (49%)
  blocking collectives  31 us (28%)
  waiting for transfers between devices  11.3 us (10%)
  Pallas kernels  10.8 us (10%)
  local copies, waits for them, and re-layouts  1.5 us (1%)
    ppermute x8, starting transfers between devices, hop(): return lax.ppermute(x, 'seq', [(i, j) for i, j in pairs if 0 <= j < size])  42.7 us
    all_to_all x1, blocking collectives, local(): lax.all_to_all(attended.reshape(2 * n_head, -1, half), ('seq', 'head'), 0...  12 us
    all_to_all x1, blocking collectives, local(): lax.all_to_all(split, ('seq', 'head'), 0, 0, axis_index_groups=chip_group...  11.2 us
    ppermute x3, starting transfers between devices, swap(): return lax.ppermute(x, 'seq', [(i, i ^ 1) for i in range(size)])  11.2 us
    all_gather x3, blocking collectives, both_cores(): return lax.all_gather(x, 'seq', axis=0, axis_index_groups=chip_cores)  7.79 us
    ppermute x8, waiting for transfers between devices, hop(): return lax.ppermute(x, 'seq', [(i, j) for i, j in pairs if 0 <= j < size])  7.66 us
    pallas_call x1, Pallas kernels, local(): pl.pallas_call(attend, out_shape=[jax.ShapeDtypeStruct(s, d) for s, d in...  4.83 us
    ppermute x3, waiting for transfers between devices, swap(): return lax.ppermute(x, 'seq', [(i, i ^ 1) for i in range(size)])  3.61 us
  transfers between devices with their start and end apart: 11, of which 4 were waited for; matrix products, arithmetic and copies ran while one was open for 2% of the time, Pallas kernels for 0%

profile of v4, /device:TPU:49, one launch (start us, length us, event | category | flops | bytes accessed | tf_op | source)
XLA Modules:
  0.0 110.2 jit_solution(17229267999175770504)
XLA Ops:
  0.6 1.9 %shard_map.156 = bf16[2,32,1024]{2,1,0:T(8,128)(2,1)} custom-call(bf16[128,1024]{1,0:T(8,128)(2,1)} %k_ref.1, bf16[128,1024]{1,0:T(8,128)(2,1)} %v_ref.1), custom_call_target="tpu_custom_call" | custom-call | tf_op jit(solution)/shard_map/pallas_call | solution.py:330
  2.5 0.0 copy-start.8
  2.5 2.6 %all-gather = bf16[4,32,1024]{2,1,0:T(8,128)(2,1)S(1)} all-gather(bf16[2,32,1024]{2,1,0:T(8,128)(2,1)} %shard_map.156), channel_id=2, replica_groups={{0,4},{8,12},{16,20},{24,28},{32,36},{40,44},{48,52},{56,60},{64,68},{7..., dimensions={0}, use_global_device_ids=true | all-gather | bytes 393216 | tf_op jit(solution)/shard_map/all_gather | solution.py:318
  5.2 0.0 copy-start.9
  5.2 11.1 %collective-permute-start = (bf16[2,32,1024]{2,1,0:T(8,128)(2,1)S(1)}, bf16[2,32,1024]{2,1,0:T(8,128)(2,1)S(1)}, u32[]{:S(2)}, u32[]{:S(2)}) collective-permute-start(bf16[2,32,1024]{2,1,0:T(8,128)(2,1)S(1)} %get-tuple-element.55), channel_id=1, source_target_pairs={{0,24},{8,32},{16,40},{24,48},{28,4},{32,56},{36,12},{40,64},{44,2... | collective-permute-start | bytes 393224 | tf_op jit(solution)/shard_map/ppermute | solution.py:312
  16.3 6.1 %collective-permute-start.1 = (bf16[2,16,1024]{2,1,0:T(8,128)(2,1)S(1)}, bf16[2,16,1024]{2,1,0:T(8,128)(2,1)S(1)}, u32[]{:S(2)}, u32[]{:S(2)}) collective-permute-start(bf16[2,16,1024]{2,1,0:T(8,128)(2,1)S(1)} %get-tuple-element.56), channel_id=1, source_target_pairs={{0,48},{8,56},{16,64},{24,72},{32,80},{40,88},{48,96},{52,4},{56,1... | collective-permute-start | bytes 196616 | tf_op jit(solution)/shard_map/ppermute | solution.py:312
  22.4 0.0 copy-done.8
  22.4 2.9 %all-gather.1 = bf16[256,1024]{1,0:T(8,128)(2,1)S(1)} all-gather(bf16[128,1024]{1,0:T(8,128)(2,1)S(1)} %copy-done.8), channel_id=3, replica_groups={{0,4},{8,12},{16,20},{24,28},{32,36},{40,44},{48,52},{56,60},{64,68},{7..., dimensions={0}, use_global_device_ids=true | all-gather | bytes 786432 | tf_op jit(solution)/shard_map/all_gather | solution.py:318
  25.3 0.0 copy-done.9
  25.3 0.0 copy-start.3
  25.3 2.3 %all-gather.2 = bf16[256,1024]{1,0:T(8,128)(2,1)S(1)} all-gather(bf16[128,1024]{1,0:T(8,128)(2,1)S(1)} %copy-done.9), channel_id=4, replica_groups={{0,4},{8,12},{16,20},{24,28},{32,36},{40,44},{48,52},{56,60},{64,68},{7..., dimensions={0}, use_global_device_ids=true | all-gather | bytes 786432 | tf_op jit(solution)/shard_map/all_gather | solution.py:318
  27.6 0.0 copy-done.3
  27.6 0.5 shard_map.158
  28.1 1.0 collective-permute-done.1.six_ref
  29.1 0.0 collective-permute-done.three_ref
  29.1 0.0 copy-done.6
  29.1 1.0 shard_map.159
  30.1 3.2 %collective-permute-start.2 = (bf16[2,136,1024]{2,1,0:T(8,128)(2,1)}, bf16[2,136,1024]{2,1,0:T(8,128)(2,1)S(1)}, u32[]{:S(2)}, u32[]{:S(2)}) collective-permute-start(bf16[2,136,1024]{2,1,0:T(8,128)(2,1)} %get-tuple-element.64), channel_id=1, source_target_pairs={{0,8},{8,16},{12,4},{16,24},{20,12},{24,32},{28,20},{32,40},{36,28... | collective-permute-start | bytes 1671176 | tf_op jit(solution)/shard_map/ppermute | solution.py:312
  33.4 6.3 %collective-permute-start.3 = (bf16[2,72,1024]{2,1,0:T(8,128)(2,1)S(1)}, bf16[2,72,1024]{2,1,0:T(8,128)(2,1)S(1)}, u32[]{:S(2)}, u32[]{:S(2)}) collective-permute-start(bf16[2,72,1024]{2,1,0:T(8,128)(2,1)S(1)} %get-tuple-element.65), channel_id=1, source_target_pairs={{0,16},{8,24},{16,32},{20,4},{24,40},{28,12},{32,48},{36,20},{40,5... | collective-permute-start | bytes 884744 | tf_op jit(solution)/shard_map/ppermute | solution.py:312
  39.7 0.0 copy-done.10
  39.8 0.2 reshape.30
  39.9 0.1 copy.19
  40.0 0.0 copy-start
  40.0 11.2 %all_to_all.10 = bf16[8,32,512]{2,1,0:T(8,128)(2,1)S(1)} all-to-all(bf16[8,32,512]{2,1,0:T(8,128)(2,1)S(1)} %bitcast.22), channel_id=1, replica_groups={{0,1,2,3,4,5,6,7},{8,9,10,11,12,13,14,15},{16,17,18,19,20,21,22,23},{24..., dimensions={0} | all-to-all | bytes 524288 | tf_op jit(solution)/shard_map/all_to_all | solution.py:352
  51.3 0.0 collective-permute-done.3.two_ref
  51.3 0.0 collective-permute-done.2.one_ref
  51.3 0.0 copy-done
  51.3 0.0 copy-start.12
  51.3 0.0 copy-start.2
  51.3 0.0 copy-start.4
  51.3 0.0 copy-start.5
  51.3 0.9 shard_map.160
  52.3 2.4 %collective-permute-start.4 = (bf16[5,128,512]{2,1,0:T(8,128)(2,1)}, bf16[5,128,512]{2,1,0:T(8,128)(2,1)S(1)}, u32[]{:S(2)}, u32[]{:S(2)}) collective-permute-start(bf16[5,128,512]{2,1,0:T(8,128)(2,1)} %get-tuple-element.72), channel_id=1, source_target_pairs={{0,4},{4,0},{8,12},{12,8},{16,20},{20,16},{24,28},{28,24},{32,36},... | collective-permute-start | bytes 1966088 | tf_op jit(solution)/shard_map/ppermute | solution.py:315
  54.7 0.0 copy-done.12
  54.7 0.0 copy-done.11
  54.7 1.9 %collective-permute-done.4.y_ref = bf16[5,128,512]{2,1,0:T(8,128)(2,1)S(1)} collective-permute-done((bf16[5,128,512]{2,1,0:T(8,128)(2,1)}, bf16[5,128,512]{2,1,0:T(8,128)(2,1)S(1)}, u32[]{:S(2)}, u32[]{:S(2)}) %collective-permute-start.4) | collective-permute-done | bytes 655392 | tf_op jit(solution)/shard_map/ppermute | solution.py:315
  56.6 0.0 copy-done.2
  56.6 0.0 copy-done.4
  56.6 0.0 copy-done.5
  56.6 4.8 %shard_map.161 = (bf16[256,512]{1,0:T(8,128)(2,1)S(1)}, bf16[128,512]{1,0:T(8,128)(2,1)S(1)}, f32[2,128,512]{2,1,0:T(8,128)S(1)}, f32[2,128,512]{2,1,0:T(8,128)S...) custom-call(s32[1]{0:T(128)} %bitcast.core_ref, bf16[2,128,1024]{2,1,0:T(8,128)(2,1)S(1)} %bitcast.15, ...), custom_call_target="tpu_custom_call" | custom-call | tf_op jit(solution)/shard_map/pallas_call | solution.py:370
  61.4 2.3 %collective-permute-start.5 = (bf16[5,128,512]{2,1,0:T(8,128)(2,1)S(1)}, bf16[5,128,512]{2,1,0:T(8,128)(2,1)S(1)}, u32[]{:S(2)}, u32[]{:S(2)}) collective-permute-start(bf16[5,128,512]{2,1,0:T(8,128)(2,1)S(1)} %get-tuple-element.74), channel_id=1, source_target_pairs={{0,4},{4,0},{8,12},{12,8},{16,20},{20,16},{24,28},{28,24},{32,36},... | collective-permute-start | bytes 1966088 | tf_op jit(solution)/shard_map/ppermute | solution.py:315
  63.7 1.7 %collective-permute-done.5.take_ref = bf16[5,128,512]{2,1,0:T(8,128)(2,1)S(1)} collective-permute-done((bf16[5,128,512]{2,1,0:T(8,128)(2,1)S(1)}, bf16[5,128,512]{2,1,0:T(8,128)(2,1)S(1)}, u32[]{:S(2)}, u32[]{:S(2)}) %collective-permute-start.5) | collective-permute-done | bytes 655392 | tf_op jit(solution)/shard_map/ppermute | solution.py:315
  65.4 0.1 shard_map.162
  65.5 3.6 %collective-permute-start.6 = (bf16[2,136,1024]{2,1,0:T(8,128)(2,1)S(1)}, bf16[2,136,1024]{2,1,0:T(8,128)(2,1)S(1)}, u32[]{:S(2)}, u32[]{:S(2)}) collective-permute-start(bf16[2,136,1024]{2,1,0:T(8,128)(2,1)S(1)} %get-tuple-element.78), channel_id=1, source_target_pairs={{4,12},{8,0},{12,20},{16,8},{20,28},{24,16},{28,36},{32,24},{36,44... | collective-permute-start | bytes 1671176 | tf_op jit(solution)/shard_map/ppermute | solution.py:312
  69.1 2.9 %collective-permute-start.7 = (bf16[2,72,1024]{2,1,0:T(8,128)(2,1)S(1)}, bf16[2,72,1024]{2,1,0:T(8,128)(2,1)S(1)}, u32[]{:S(2)}, u32[]{:S(2)}) collective-permute-start(bf16[2,72,1024]{2,1,0:T(8,128)(2,1)S(1)} %get-tuple-element.79), channel_id=1, source_target_pairs={{4,20},{12,28},{16,0},{20,36},{24,8},{28,44},{32,16},{36,52},{40,2... | collective-permute-start | bytes 884744 | tf_op jit(solution)/shard_map/ppermute | solution.py:312
  72.0 0.0 copy-start.7
  72.0 12.0 %all_to_all.11 = bf16[8,32,512]{2,1,0:T(8,128)(2,1)S(1)} all-to-all(bf16[8,32,512]{2,1,0:T(8,128)(2,1)S(1)} %bitcast.20), channel_id=1, replica_groups={{0,1,2,3,4,5,6,7},{8,9,10,11,12,13,14,15},{16,17,18,19,20,21,22,23},{24..., dimensions={0} | all-to-all | bytes 524288 | tf_op jit(solution)/shard_map/all_to_all | solution.py:388
  84.0 0.0 collective-permute-done.7.two_ref
  84.0 0.0 collective-permute-done.6.one_ref
  84.0 0.0 copy-done.7
  84.0 0.2 shard_map.163
  84.2 2.9 %collective-permute-start.8 = (bf16[2,32,1024]{2,1,0:T(8,128)(2,1)S(1)}, bf16[2,32,1024]{2,1,0:T(8,128)(2,1)S(1)}, u32[]{:S(2)}, u32[]{:S(2)}) collective-permute-start(bf16[2,32,1024]{2,1,0:T(8,128)(2,1)S(1)} %get-tuple-element.84), channel_id=1, source_target_pairs={{4,28},{12,36},{20,44},{24,0},{28,52},{32,8},{36,60},{40,16},{44,6... | collective-permute-start | bytes 393224 | tf_op jit(solution)/shard_map/ppermute | solution.py:312
  87.1 0.0 copy-start.1
  87.1 6.5 %collective-permute-start.9 = (bf16[2,16,1024]{2,1,0:T(8,128)(2,1)S(1)}, bf16[2,16,1024]{2,1,0:T(8,128)(2,1)S(1)}, u32[]{:S(2)}, u32[]{:S(2)}) collective-permute-start(bf16[2,16,1024]{2,1,0:T(8,128)(2,1)S(1)} %get-tuple-element.85), channel_id=1, source_target_pairs={{4,52},{12,60},{20,68},{28,76},{36,84},{44,92},{48,0},{52,100},{56... | collective-permute-start | bytes 196616 | tf_op jit(solution)/shard_map/ppermute | solution.py:312
  93.7 6.6 %collective-permute-done.9.six_ref = bf16[2,16,1024]{2,1,0:T(8,128)(2,1)S(1)} collective-permute-done((bf16[2,16,1024]{2,1,0:T(8,128)(2,1)S(1)}, bf16[2,16,1024]{2,1,0:T(8,128)(2,1)S(1)}, u32[]{:S(2)}, u32[]{:S(2)}) %collective-permute-start.9) | collective-permute-done | bytes 65568 | tf_op jit(solution)/shard_map/ppermute | solution.py:312
  100.3 0.0 collective-permute-done.8.three_ref
  100.3 0.0 copy-done.1
  100.3 0.5 shard_map.164
  100.8 6.6 %collective-permute-start.10 = (bf16[2,128,1024]{2,1,0:T(8,128)(2,1)S(1)}, bf16[2,128,1024]{2,1,0:T(8,128)(2,1)S(1)}, u32[]{:S(2)}, u32[]{:S(2)}) collective-permute-start(bf16[2,128,1024]{2,1,0:T(8,128)(2,1)S(1)} %get-tuple-element.95), channel_id=1, source_target_pairs={{0,4},{4,0},{8,12},{12,8},{16,20},{20,16},{24,28},{28,24},{32,36},... | collective-permute-start | bytes 1572872 | tf_op jit(solution)/shard_map/ppermute | solution.py:315
  107.4 0.3 copy.22
  107.7 0.9 reshape.35
  108.6 0.7 pad_maximum_fusion
  109.3 0.0 collective-permute-done.10.take_ref
  109.3 0.9 shard_map.165
  (7 shorter events, 0.1 us)
Async XLA Ops:
  2.5 19.9 %copy-start.8 = (bf16[128,1024]{1,0:T(8,128)(2,1)S(1)}, bf16[128,1024]{1,0:T(8,128)(2,1)}, u32[]{:S(2)}) copy-start(bf16[128,1024]{1,0:T(8,128)(2,1)} %k_ref.1) | copy-start | bytes 786436
  5.2 20.1 %copy-start.9 = (bf16[128,1024]{1,0:T(8,128)(2,1)S(1)}, bf16[128,1024]{1,0:T(8,128)(2,1)}, u32[]{:S(2)}) copy-start(bf16[128,1024]{1,0:T(8,128)(2,1)} %v_ref.1) | copy-start | bytes 786436
  5.2 23.9 %collective-permute-start = (bf16[2,32,1024]{2,1,0:T(8,128)(2,1)S(1)}, bf16[2,32,1024]{2,1,0:T(8,128)(2,1)S(1)}, u32[]{:S(2)}, u32[]{:S(2)}) collective-permute-start(bf16[2,32,1024]{2,1,0:T(8,128)(2,1)S(1)} %get-tuple-element.55), channel_id=1, source_target_pairs={{0,24},{8,32},{16,40},{24,48},{28,4},{32,56},{36,12},{40,64},{44,2... | collective-permute-start | bytes 393224 | tf_op jit(solution)/shard_map/ppermute | solution.py:312
  16.3 12.8 %collective-permute-start.1 = (bf16[2,16,1024]{2,1,0:T(8,128)(2,1)S(1)}, bf16[2,16,1024]{2,1,0:T(8,128)(2,1)S(1)}, u32[]{:S(2)}, u32[]{:S(2)}) collective-permute-start(bf16[2,16,1024]{2,1,0:T(8,128)(2,1)S(1)} %get-tuple-element.56), channel_id=1, source_target_pairs={{0,48},{8,56},{16,64},{24,72},{32,80},{40,88},{48,96},{52,4},{56,1... | collective-permute-start | bytes 196616 | tf_op jit(solution)/shard_map/ppermute | solution.py:312
  25.3 2.3 %copy-start.3 = (bf16[240,256]{1,0:T(8,128)(2,1)S(1)}, bf16[240,256]{1,0:T(8,128)(2,1)}, u32[]{:S(2)}) copy-start(bf16[240,256]{1,0:T(8,128)(2,1)} %constant.39.clone.own_ref) | copy-start | bytes 368644
  27.6 1.5 %copy-start.6 = (bf16[64,48]{1,0:T(8,128)(2,1)S(1)}, bf16[64,48]{1,0:T(8,128)(2,1)}, u32[]{:S(2)}) copy-start(bf16[64,48]{1,0:T(8,128)(2,1)} %constant.40.clone.w_ref) | copy-start | bytes 18436
  29.1 10.6 %copy-start.10 = (bf16[32,4096]{1,0:T(8,128)(2,1)S(1)}, bf16[32,4096]{1,0:T(8,128)(2,1)}, u32[]{:S(2)}) copy-start(bf16[32,4096]{1,0:T(8,128)(2,1)} %param.16) | copy-start | bytes 786436
  30.1 21.1 %collective-permute-start.2 = (bf16[2,136,1024]{2,1,0:T(8,128)(2,1)}, bf16[2,136,1024]{2,1,0:T(8,128)(2,1)S(1)}, u32[]{:S(2)}, u32[]{:S(2)}) collective-permute-start(bf16[2,136,1024]{2,1,0:T(8,128)(2,1)} %get-tuple-element.64), channel_id=1, source_target_pairs={{0,8},{8,16},{12,4},{16,24},{20,12},{24,32},{28,20},{32,40},{36,28... | collective-permute-start | bytes 1671176 | tf_op jit(solution)/shard_map/ppermute | solution.py:312
  33.4 17.9 %collective-permute-start.3 = (bf16[2,72,1024]{2,1,0:T(8,128)(2,1)S(1)}, bf16[2,72,1024]{2,1,0:T(8,128)(2,1)S(1)}, u32[]{:S(2)}, u32[]{:S(2)}) collective-permute-start(bf16[2,72,1024]{2,1,0:T(8,128)(2,1)S(1)} %get-tuple-element.65), channel_id=1, source_target_pairs={{0,16},{8,24},{16,32},{20,4},{24,40},{28,12},{32,48},{36,20},{40,5... | collective-permute-start | bytes 884744 | tf_op jit(solution)/shard_map/ppermute | solution.py:312
  40.0 11.2 %copy-start = (bf16[128,1024]{1,0:T(8,128)(2,1)S(1)}, bf16[128,1024]{1,0:T(8,128)(2,1)}, u32[]{:S(2)}) copy-start(bf16[128,1024]{1,0:T(8,128)(2,1)} %q_ref.1) | copy-start | bytes 786436
  51.3 3.4 %copy-start.12 = (f32[2,640]{1,0:T(2,128)S(1)}, f32[2,640]{1,0:T(2,128)}, u32[]{:S(2)}) copy-start(f32[2,640]{1,0:T(2,128)} %constant.42.clone) | copy-start | bytes 15364
  51.3 5.3 %copy-start.2 = (bf16[256,192]{1,0:T(8,128)(2,1)S(1)}, bf16[256,192]{1,0:T(8,128)(2,1)}, u32[]{:S(2)}) copy-start(bf16[256,192]{1,0:T(8,128)(2,1)} %constant.44.clone.derive_t_ref) | copy-start | bytes 294916
  51.3 5.3 %copy-start.4 = (bf16[192,256]{1,0:T(8,128)(2,1)S(1)}, bf16[192,256]{1,0:T(8,128)(2,1)}, u32[]{:S(2)}) copy-start(bf16[192,256]{1,0:T(8,128)(2,1)} %constant.43.clone.derive_ref) | copy-start | bytes 294916
  51.3 5.3 %copy-start.5 = (bf16[128,64]{1,0:T(8,128)(2,1)S(1)}, bf16[128,64]{1,0:T(8,128)(2,1)}, u32[]{:S(2)}) copy-start(bf16[128,64]{1,0:T(8,128)(2,1)} %constant.45.clone.spread_ref) | copy-start | bytes 49156
  52.3 2.4 %copy-start.11 = (s32[2,640]{1,0:T(2,128)S(1)}, s32[2,640]{1,0:T(2,128)}, u32[]{:S(2)}) copy-start(s32[2,640]{1,0:T(2,128)} %constant.41.clone) | copy-start | bytes 15364
  52.3 4.3 %collective-permute-start.4 = (bf16[5,128,512]{2,1,0:T(8,128)(2,1)}, bf16[5,128,512]{2,1,0:T(8,128)(2,1)S(1)}, u32[]{:S(2)}, u32[]{:S(2)}) collective-permute-start(bf16[5,128,512]{2,1,0:T(8,128)(2,1)} %get-tuple-element.72), channel_id=1, source_target_pairs={{0,4},{4,0},{8,12},{12,8},{16,20},{20,16},{24,28},{28,24},{32,36},... | collective-permute-start | bytes 1966088 | tf_op jit(solution)/shard_map/ppermute | solution.py:315
  61.4 4.0 %collective-permute-start.5 = (bf16[5,128,512]{2,1,0:T(8,128)(2,1)S(1)}, bf16[5,128,512]{2,1,0:T(8,128)(2,1)S(1)}, u32[]{:S(2)}, u32[]{:S(2)}) collective-permute-start(bf16[5,128,512]{2,1,0:T(8,128)(2,1)S(1)} %get-tuple-element.74), channel_id=1, source_target_pairs={{0,4},{4,0},{8,12},{12,8},{16,20},{20,16},{24,28},{28,24},{32,36},... | collective-permute-start | bytes 1966088 | tf_op jit(solution)/shard_map/ppermute | solution.py:315
  65.5 18.5 %collective-permute-start.6 = (bf16[2,136,1024]{2,1,0:T(8,128)(2,1)S(1)}, bf16[2,136,1024]{2,1,0:T(8,128)(2,1)S(1)}, u32[]{:S(2)}, u32[]{:S(2)}) collective-permute-start(bf16[2,136,1024]{2,1,0:T(8,128)(2,1)S(1)} %get-tuple-element.78), channel_id=1, source_target_pairs={{4,12},{8,0},{12,20},{16,8},{20,28},{24,16},{28,36},{32,24},{36,44... | collective-permute-start | bytes 1671176 | tf_op jit(solution)/shard_map/ppermute | solution.py:312
  69.1 14.9 %collective-permute-start.7 = (bf16[2,72,1024]{2,1,0:T(8,128)(2,1)S(1)}, bf16[2,72,1024]{2,1,0:T(8,128)(2,1)S(1)}, u32[]{:S(2)}, u32[]{:S(2)}) collective-permute-start(bf16[2,72,1024]{2,1,0:T(8,128)(2,1)S(1)} %get-tuple-element.79), channel_id=1, source_target_pairs={{4,20},{12,28},{16,0},{20,36},{24,8},{28,44},{32,16},{36,52},{40,2... | collective-permute-start | bytes 884744 | tf_op jit(solution)/shard_map/ppermute | solution.py:312
  72.0 12.0 %copy-start.7 = (bf16[48,64]{1,0:T(8,128)(2,1)S(1)}, bf16[48,64]{1,0:T(8,128)(2,1)}, u32[]{:S(2)}) copy-start(bf16[48,64]{1,0:T(8,128)(2,1)} %constant.46.clone.w_ref) | copy-start | bytes 18436
  84.2 16.1 %collective-permute-start.8 = (bf16[2,32,1024]{2,1,0:T(8,128)(2,1)S(1)}, bf16[2,32,1024]{2,1,0:T(8,128)(2,1)S(1)}, u32[]{:S(2)}, u32[]{:S(2)}) collective-permute-start(bf16[2,32,1024]{2,1,0:T(8,128)(2,1)S(1)} %get-tuple-element.84), channel_id=1, source_target_pairs={{4,28},{12,36},{20,44},{24,0},{28,52},{32,8},{36,60},{40,16},{44,6... | collective-permute-start | bytes 393224 | tf_op jit(solution)/shard_map/ppermute | solution.py:312
  87.1 13.2 %copy-start.1 = (bf16[256,256]{1,0:T(8,128)(2,1)S(1)}, bf16[256,256]{1,0:T(8,128)(2,1)}, u32[]{:S(2)}) copy-start(bf16[256,256]{1,0:T(8,128)(2,1)} %constant.47.clone.w_ref) | copy-start | bytes 393220
  87.1 13.2 %collective-permute-start.9 = (bf16[2,16,1024]{2,1,0:T(8,128)(2,1)S(1)}, bf16[2,16,1024]{2,1,0:T(8,128)(2,1)S(1)}, u32[]{:S(2)}, u32[]{:S(2)}) collective-permute-start(bf16[2,16,1024]{2,1,0:T(8,128)(2,1)S(1)} %get-tuple-element.85), channel_id=1, source_target_pairs={{4,52},{12,60},{20,68},{28,76},{36,84},{44,92},{48,0},{52,100},{56... | collective-permute-start | bytes 196616 | tf_op jit(solution)/shard_map/ppermute | solution.py:312
  100.8 8.5 %collective-permute-start.10 = (bf16[2,128,1024]{2,1,0:T(8,128)(2,1)S(1)}, bf16[2,128,1024]{2,1,0:T(8,128)(2,1)S(1)}, u32[]{:S(2)}, u32[]{:S(2)}) collective-permute-start(bf16[2,128,1024]{2,1,0:T(8,128)(2,1)S(1)} %get-tuple-element.95), channel_id=1, source_target_pairs={{0,4},{4,0},{8,12},{12,8},{16,20},{20,16},{24,28},{28,24},{32,36},... | collective-permute-start | bytes 1572872 | tf_op jit(solution)/shard_map/ppermute | solution.py:315

commit v5 on v4

--- a/solution.py
+++ b/solution.py
@@ -15,10 +15,11 @@
 MASKED = -1e30
 SCALE = 1.0 / math.sqrt(HEAD_DIM)
 VMEM = 4 * 1024 * 1024
-WIDE_VMEM = 40 * 1024 * 1024
+WIDE_VMEM = 28 * 1024 * 1024
 FULL_VMEM = 56 * 1024 * 1024
 HALF = 512
 PER_STEP = 2
+SPANS = 4
 
 SIDE_LEVELS = [0] + [1] + [2] * 2 + [3] * 4 + [4] * 8
 VIEW = {1: [1, 2, 7, 8, 13, 14], 2: [3, 4, 9, 10, 15], 3: [5, 6], 6: [11, 12]}
@@ -204,13 +205,17 @@
         y_derived = _dot(derive_ref[...], y).astype(jnp.bfloat16)
         sets_p.append(jnp.concatenate([ref[core], ones_ref[part, 64:128], x, y_derived], axis=0))
         sets_o.append(jnp.concatenate([ref[1 - core], ones_ref[part, 0:64], y, x_derived], axis=0))
-    here = [pl.ds(pl.multiple_of(place * BLOCK, BLOCK), BLOCK) for place in (core, 1 - core)]
+    span = BLOCK // SPANS
+    here = [
+        [pl.ds(pl.multiple_of((2 * i + place) * span, span), span) for i in range(SPANS)] for place in (core, 1 - core)
+    ]
     items = []
     for head in range(PER_STEP):
         cols = slice(head * HEAD_DIM, (head + 1) * HEAD_DIM)
         for block, (keys, values) in enumerate((sets_p, sets_o)):
             q = (x_ref, y_ref)[block][4, :, cols]
-            items.append((block, keys[:, cols], values[:, cols], q, do_ref[here[block], cols]))
+            do = jnp.concatenate([do_ref[rows, cols] for rows in here[block]], axis=0)
+            items.append((block, keys[:, cols], values[:, cols], q, do))
     scores = [_outer(q, keys) for _, keys, _, q, _ in items]
     weight_grads = [_outer(do, values) for _, _, values, _, do in items]
     lows, score_grads = [], []
@@ -232,7 +237,9 @@
         return jnp.concatenate(results[block::2], axis=1)
 
     for block in range(2):
-        o_ref[here[block], lanes] = heads_of(outs, block).astype(jnp.bfloat16)
+        out = heads_of(outs, block).astype(jnp.bfloat16)
+        for i, rows in enumerate(here[block]):
+            o_ref[rows, lanes] = out[i * span : (i + 1) * span]
     dq_ref[:, lanes] = heads_of(dqs, 0).astype(jnp.bfloat16)
     gy_ref[4, :, lanes] = heads_of(dqs, 1).astype(jnp.bfloat16)
     for part, results in enumerate((dks, dvs)):
@@ -305,7 +312,9 @@
     half = width // 2
     n_head = lax.axis_size("head")
     chip_cores = [[2 * i, 2 * i + 1] for i in range(size // 2)]
-    chip_groups = [[g * 2 * n_head + m for m in range(2 * n_head)] for g in range(size // 2)]
+    chip_groups = [
+        [(2 * g + c) * n_head + h for h in range(n_head) for c in range(2)] for g in range(size // 2)
+    ]
 
     def hop(x, chips):
         pairs = [(i, i + (2 - 4 * (i % 2)) * chips) for i in range(size)]
@@ -348,7 +357,7 @@
     t1, t2 = _whole(pack_on, [full(136), full(72)], r3, r6, own1, own2, _bf(_pass_matrix()))
     t1, t2, late_cotangent = tie((t1, t2, late_cotangent))
     r2, r1 = hop(t2, 2), hop(t1, 1)
-    split = late_cotangent.reshape(-1, n_head, 2, half).transpose(2, 1, 0, 3).reshape(2 * n_head, -1, half)
+    split = late_cotangent.reshape(-1, 2 * n_head, half).transpose(1, 0, 2)
     do = lax.all_to_all(split, ("seq", "head"), 0, 0, axis_index_groups=chip_groups, tiled=True)
     do = do.reshape(2 * BLOCK, half)
     r1, r2, do = tie((r1, r2, do))
@@ -396,7 +405,7 @@
         fold_own, [full(BLOCK, f32), full(BLOCK)], core_arg, v1, v2, v3, v6, gp, go, _bf(_final_matrix()), scalars=1
     )
     back, out, dq_mine, dq_take = tie((back, out, dq_mine, take[4]))
-    out = out.reshape(2, n_head, -1, half).transpose(2, 1, 0, 3).reshape(-1, n_head * width)
+    out = out.transpose(1, 0, 2).reshape(-1, n_head * width)
     query_gradient = jnp.concatenate(
         [jnp.where(core == 0, dq_mine, dq_take), jnp.where(core == 0, dq_take, dq_mine)], axis=1
     )

time: 111 us -> 110 us (level)
  starting transfers between devices: 53.9 us -> 55.2 us
    ppermute x3, starting transfers between devices: 11.2 us -> 12.7 us  [swap(): return lax.ppermute(x, 'seq', [(i, i ^ 1) for i in range(size)])]
  transfers between devices with their start and end apart: 11 -> 11, of which waited for: 4 -> 5; matrix products, arithmetic and copies ran while one was open for 2% -> 1% of each run, Pallas kernels for 0% -> 0%
where the time goes in v5:
time: 110 us; the launch traced here: 109 us
  starting transfers between devices  55.2 us (50%)
  blocking collectives  30.3 us (28%)
  waiting for transfers between devices  11.1 us (10%)
  Pallas kernels  9.96 us (9%)
    ppermute x8, starting transfers between devices, hop(): return lax.ppermute(x, 'seq', [(i, j) for i, j in pairs if 0 <= j < size])  42.5 us
    ppermute x3, starting transfers between devices, swap(): return lax.ppermute(x, 'seq', [(i, i ^ 1) for i in range(size)])  12.7 us
    all_to_all x1, blocking collectives, local(): lax.all_to_all(attended.reshape(2 * n_head, -1, half), ('seq', 'head'), 0...  11.3 us
    all_to_all x1, blocking collectives, local(): lax.all_to_all(split, ('seq', 'head'), 0, 0, axis_index_groups=chip_group...  11.2 us
    all_gather x3, blocking collectives, both_cores(): return lax.all_gather(x, 'seq', axis=0, axis_index_groups=chip_cores)  7.79 us
    ppermute x8, waiting for transfers between devices, hop(): return lax.ppermute(x, 'seq', [(i, j) for i, j in pairs if 0 <= j < size])  7.54 us
    pallas_call x1, Pallas kernels, local(): pl.pallas_call(attend, out_shape=[jax.ShapeDtypeStruct(s, d) for s, d in...  4.81 us
    ppermute x3, waiting for transfers between devices, swap(): return lax.ppermute(x, 'seq', [(i, i ^ 1) for i in range(size)])  3.6 us
  transfers between devices with their start and end apart: 11, of which 5 were waited for; matrix products, arithmetic and copies ran while one was open for 1% of the time, Pallas kernels for 0%

profile of v5, /device:TPU:49, one launch (start us, length us, event | category | flops | bytes accessed | tf_op | source)
XLA Modules:
  0.0 109.1 jit_solution(13480823097318114253)
XLA Ops:
  0.6 1.9 %shard_map.156 = bf16[2,32,1024]{2,1,0:T(8,128)(2,1)} custom-call(bf16[128,1024]{1,0:T(8,128)(2,1)} %k_ref.1, bf16[128,1024]{1,0:T(8,128)(2,1)} %v_ref.1), custom_call_target="tpu_custom_call" | custom-call | tf_op jit(solution)/shard_map/pallas_call | solution.py:339
  2.5 0.0 copy-start.8
  2.5 2.6 %all-gather = bf16[4,32,1024]{2,1,0:T(8,128)(2,1)S(1)} all-gather(bf16[2,32,1024]{2,1,0:T(8,128)(2,1)} %shard_map.156), channel_id=2, replica_groups={{0,4},{8,12},{16,20},{24,28},{32,36},{40,44},{48,52},{56,60},{64,68},{7..., dimensions={0}, use_global_device_ids=true | all-gather | bytes 393216 | tf_op jit(solution)/shard_map/all_gather | solution.py:327
  5.2 0.0 copy-start.9
  5.2 11.1 %collective-permute-start = (bf16[2,32,1024]{2,1,0:T(8,128)(2,1)S(1)}, bf16[2,32,1024]{2,1,0:T(8,128)(2,1)S(1)}, u32[]{:S(2)}, u32[]{:S(2)}) collective-permute-start(bf16[2,32,1024]{2,1,0:T(8,128)(2,1)S(1)} %get-tuple-element.55), channel_id=1, source_target_pairs={{0,24},{8,32},{16,40},{24,48},{28,4},{32,56},{36,12},{40,64},{44,2... | collective-permute-start | bytes 393224 | tf_op jit(solution)/shard_map/ppermute | solution.py:321
  16.3 6.1 %collective-permute-start.1 = (bf16[2,16,1024]{2,1,0:T(8,128)(2,1)S(1)}, bf16[2,16,1024]{2,1,0:T(8,128)(2,1)S(1)}, u32[]{:S(2)}, u32[]{:S(2)}) collective-permute-start(bf16[2,16,1024]{2,1,0:T(8,128)(2,1)S(1)} %get-tuple-element.56), channel_id=1, source_target_pairs={{0,48},{8,56},{16,64},{24,72},{32,80},{40,88},{48,96},{52,4},{56,1... | collective-permute-start | bytes 196616 | tf_op jit(solution)/shard_map/ppermute | solution.py:321
  22.4 0.0 copy-done.8
  22.4 2.9 %all-gather.1 = bf16[256,1024]{1,0:T(8,128)(2,1)S(1)} all-gather(bf16[128,1024]{1,0:T(8,128)(2,1)S(1)} %copy-done.8), channel_id=3, replica_groups={{0,4},{8,12},{16,20},{24,28},{32,36},{40,44},{48,52},{56,60},{64,68},{7..., dimensions={0}, use_global_device_ids=true | all-gather | bytes 786432 | tf_op jit(solution)/shard_map/all_gather | solution.py:327
  25.3 0.0 copy-done.9
  25.3 0.0 copy-start.3
  25.3 2.3 %all-gather.2 = bf16[256,1024]{1,0:T(8,128)(2,1)S(1)} all-gather(bf16[128,1024]{1,0:T(8,128)(2,1)S(1)} %copy-done.9), channel_id=4, replica_groups={{0,4},{8,12},{16,20},{24,28},{32,36},{40,44},{48,52},{56,60},{64,68},{7..., dimensions={0}, use_global_device_ids=true | all-gather | bytes 786432 | tf_op jit(solution)/shard_map/all_gather | solution.py:327
  27.6 0.0 copy-done.3
  27.6 0.0 copy-start.6
  27.6 0.5 shard_map.158
  28.1 1.0 collective-permute-done.1.six_ref
  29.1 0.0 collective-permute-done.three_ref
  29.1 0.0 copy-done.6
  29.1 0.0 copy-start.10
  29.1 0.2 shard_map.159
  29.3 3.3 %collective-permute-start.2 = (bf16[2,136,1024]{2,1,0:T(8,128)(2,1)S(1)}, bf16[2,136,1024]{2,1,0:T(8,128)(2,1)S(1)}, u32[]{:S(2)}, u32[]{:S(2)}) collective-permute-start(bf16[2,136,1024]{2,1,0:T(8,128)(2,1)S(1)} %get-tuple-element.64), channel_id=1, source_target_pairs={{0,8},{8,16},{12,4},{16,24},{20,12},{24,32},{28,20},{32,40},{36,28... | collective-permute-start | bytes 1671176 | tf_op jit(solution)/shard_map/ppermute | solution.py:321
  32.6 6.3 %collective-permute-start.3 = (bf16[2,72,1024]{2,1,0:T(8,128)(2,1)S(1)}, bf16[2,72,1024]{2,1,0:T(8,128)(2,1)S(1)}, u32[]{:S(2)}, u32[]{:S(2)}) collective-permute-start(bf16[2,72,1024]{2,1,0:T(8,128)(2,1)S(1)} %get-tuple-element.65), channel_id=1, source_target_pairs={{0,16},{8,24},{16,32},{20,4},{24,40},{28,12},{32,48},{36,20},{40,5... | collective-permute-start | bytes 884744 | tf_op jit(solution)/shard_map/ppermute | solution.py:321
  39.0 0.0 copy-done.10
  39.0 0.0 copy-start
  39.0 11.2 %all_to_all.10 = bf16[8,32,512]{2,1,0:T(8,128)(2,1)S(1)} all-to-all(bf16[8,32,512]{2,1,0:T(8,128)(2,1)S(1)} %bitcast.26), channel_id=1, replica_groups={{0,4,1,5,2,6,3,7},{8,12,9,13,10,14,11,15},{16,20,17,21,18,22,19,23},{24..., dimensions={0} | all-to-all | bytes 524288 | tf_op jit(solution)/shard_map/all_to_all | solution.py:361
  50.2 0.0 collective-permute-done.3.two_ref
  50.2 0.0 collective-permute-done.2.one_ref
  50.2 0.0 copy-done
  50.2 0.0 copy-start.12
  50.2 0.0 copy-start.2
  50.2 0.0 copy-start.4
  50.2 0.0 copy-start.5
  50.2 0.9 shard_map.160
  51.2 0.0 copy-start.11
  51.2 3.1 %collective-permute-start.4 = (bf16[5,128,512]{2,1,0:T(8,128)(2,1)}, bf16[5,128,512]{2,1,0:T(8,128)(2,1)S(1)}, u32[]{:S(2)}, u32[]{:S(2)}) collective-permute-start(bf16[5,128,512]{2,1,0:T(8,128)(2,1)} %get-tuple-element.72), channel_id=1, source_target_pairs={{0,4},{4,0},{8,12},{12,8},{16,20},{20,16},{24,28},{28,24},{32,36},... | collective-permute-start | bytes 1966088 | tf_op jit(solution)/shard_map/ppermute | solution.py:324
  54.2 0.0 copy-done.12
  54.3 0.0 copy-done.11
  54.3 1.9 %collective-permute-done.4.y_ref = bf16[5,128,512]{2,1,0:T(8,128)(2,1)S(1)} collective-permute-done((bf16[5,128,512]{2,1,0:T(8,128)(2,1)}, bf16[5,128,512]{2,1,0:T(8,128)(2,1)S(1)}, u32[]{:S(2)}, u32[]{:S(2)}) %collective-permute-start.4) | collective-permute-done | bytes 655392 | tf_op jit(solution)/shard_map/ppermute | solution.py:324
  56.2 0.0 copy-done.2
  56.2 0.0 copy-done.4
  56.2 0.0 copy-done.5
  56.2 4.8 %shard_map.161 = (bf16[256,512]{1,0:T(8,128)(2,1)S(1)}, bf16[128,512]{1,0:T(8,128)(2,1)S(1)}, f32[2,128,512]{2,1,0:T(8,128)S(1)}, f32[2,128,512]{2,1,0:T(8,128)S...) custom-call(s32[1]{0:T(128)} %bitcast.core_ref, bf16[2,128,1024]{2,1,0:T(8,128)(2,1)S(1)} %bitcast.19, ...), custom_call_target="tpu_custom_call" | custom-call | tf_op jit(solution)/shard_map/pallas_call | solution.py:379
  61.0 2.3 %collective-permute-start.5 = (bf16[5,128,512]{2,1,0:T(8,128)(2,1)S(1)}, bf16[5,128,512]{2,1,0:T(8,128)(2,1)S(1)}, u32[]{:S(2)}, u32[]{:S(2)}) collective-permute-start(bf16[5,128,512]{2,1,0:T(8,128)(2,1)S(1)} %get-tuple-element.74), channel_id=1, source_target_pairs={{0,4},{4,0},{8,12},{12,8},{16,20},{20,16},{24,28},{28,24},{32,36},... | collective-permute-start | bytes 1966088 | tf_op jit(solution)/shard_map/ppermute | solution.py:324
  63.3 1.7 %collective-permute-done.5.take_ref = bf16[5,128,512]{2,1,0:T(8,128)(2,1)S(1)} collective-permute-done((bf16[5,128,512]{2,1,0:T(8,128)(2,1)S(1)}, bf16[5,128,512]{2,1,0:T(8,128)(2,1)S(1)}, u32[]{:S(2)}, u32[]{:S(2)}) %collective-permute-start.5) | collective-permute-done | bytes 655392 | tf_op jit(solution)/shard_map/ppermute | solution.py:324
  65.0 0.1 shard_map.162
  65.1 3.6 %collective-permute-start.6 = (bf16[2,136,1024]{2,1,0:T(8,128)(2,1)S(1)}, bf16[2,136,1024]{2,1,0:T(8,128)(2,1)S(1)}, u32[]{:S(2)}, u32[]{:S(2)}) collective-permute-start(bf16[2,136,1024]{2,1,0:T(8,128)(2,1)S(1)} %get-tuple-element.78), channel_id=1, source_target_pairs={{4,12},{8,0},{12,20},{16,8},{20,28},{24,16},{28,36},{32,24},{36,44... | collective-permute-start | bytes 1671176 | tf_op jit(solution)/shard_map/ppermute | solution.py:321
  68.7 2.9 %collective-permute-start.7 = (bf16[2,72,1024]{2,1,0:T(8,128)(2,1)S(1)}, bf16[2,72,1024]{2,1,0:T(8,128)(2,1)S(1)}, u32[]{:S(2)}, u32[]{:S(2)}) collective-permute-start(bf16[2,72,1024]{2,1,0:T(8,128)(2,1)S(1)} %get-tuple-element.79), channel_id=1, source_target_pairs={{4,20},{12,28},{16,0},{20,36},{24,8},{28,44},{32,16},{36,52},{40,2... | collective-permute-start | bytes 884744 | tf_op jit(solution)/shard_map/ppermute | solution.py:321
  71.6 0.0 copy-start.7
  71.7 11.3 %all_to_all.11 = bf16[8,32,512]{2,1,0:T(8,128)(2,1)S(1)} all-to-all(bf16[8,32,512]{2,1,0:T(8,128)(2,1)S(1)} %bitcast.24), channel_id=1, replica_groups={{0,4,1,5,2,6,3,7},{8,12,9,13,10,14,11,15},{16,20,17,21,18,22,19,23},{24..., dimensions={0} | all-to-all | bytes 524288 | tf_op jit(solution)/shard_map/all_to_all | solution.py:397
  83.0 0.2 collective-permute-done.7.two_ref
  83.2 0.0 collective-permute-done.6.one_ref
  83.2 0.0 copy-done.7
  83.2 0.2 shard_map.163
  83.4 2.5 %collective-permute-start.8 = (bf16[2,32,1024]{2,1,0:T(8,128)(2,1)S(1)}, bf16[2,32,1024]{2,1,0:T(8,128)(2,1)S(1)}, u32[]{:S(2)}, u32[]{:S(2)}) collective-permute-start(bf16[2,32,1024]{2,1,0:T(8,128)(2,1)S(1)} %get-tuple-element.84), channel_id=1, source_target_pairs={{4,28},{12,36},{20,44},{24,0},{28,52},{32,8},{36,60},{40,16},{44,6... | collective-permute-start | bytes 393224 | tf_op jit(solution)/shard_map/ppermute | solution.py:321
  85.9 0.0 copy-start.1
  85.9 6.7 %collective-permute-start.9 = (bf16[2,16,1024]{2,1,0:T(8,128)(2,1)S(1)}, bf16[2,16,1024]{2,1,0:T(8,128)(2,1)S(1)}, u32[]{:S(2)}, u32[]{:S(2)}) collective-permute-start(bf16[2,16,1024]{2,1,0:T(8,128)(2,1)S(1)} %get-tuple-element.85), channel_id=1, source_target_pairs={{4,52},{12,60},{20,68},{28,76},{36,84},{44,92},{48,0},{52,100},{56... | collective-permute-start | bytes 196616 | tf_op jit(solution)/shard_map/ppermute | solution.py:321
  92.6 6.3 %collective-permute-done.9.six_ref = bf16[2,16,1024]{2,1,0:T(8,128)(2,1)S(1)} collective-permute-done((bf16[2,16,1024]{2,1,0:T(8,128)(2,1)S(1)}, bf16[2,16,1024]{2,1,0:T(8,128)(2,1)S(1)}, u32[]{:S(2)}, u32[]{:S(2)}) %collective-permute-start.9) | collective-permute-done | bytes 65568 | tf_op jit(solution)/shard_map/ppermute | solution.py:321
  98.9 0.0 collective-permute-done.8.three_ref
  98.9 0.0 copy-done.1
  98.9 0.5 shard_map.164
  99.4 7.3 %collective-permute-start.10 = (bf16[2,128,1024]{2,1,0:T(8,128)(2,1)S(1)}, bf16[2,128,1024]{2,1,0:T(8,128)(2,1)S(1)}, u32[]{:S(2)}, u32[]{:S(2)}) collective-permute-start(bf16[2,128,1024]{2,1,0:T(8,128)(2,1)S(1)} %get-tuple-element.95), channel_id=1, source_target_pairs={{0,4},{4,0},{8,12},{12,8},{16,20},{20,16},{24,28},{28,24},{32,36},... | collective-permute-start | bytes 1572872 | tf_op jit(solution)/shard_map/ppermute | solution.py:324
  106.8 0.7 copy.22
  107.5 0.7 pad_maximum_fusion
  108.3 0.0 collective-permute-done.10.take_ref
  108.3 0.9 shard_map.165
  (5 shorter events, 0.1 us)
Async XLA Ops:
  2.5 19.9 %copy-start.8 = (bf16[128,1024]{1,0:T(8,128)(2,1)S(1)}, bf16[128,1024]{1,0:T(8,128)(2,1)}, u32[]{:S(2)}) copy-start(bf16[128,1024]{1,0:T(8,128)(2,1)} %k_ref.1) | copy-start | bytes 786436
  5.2 20.1 %copy-start.9 = (bf16[128,1024]{1,0:T(8,128)(2,1)S(1)}, bf16[128,1024]{1,0:T(8,128)(2,1)}, u32[]{:S(2)}) copy-start(bf16[128,1024]{1,0:T(8,128)(2,1)} %v_ref.1) | copy-start | bytes 786436
  5.2 23.9 %collective-permute-start = (bf16[2,32,1024]{2,1,0:T(8,128)(2,1)S(1)}, bf16[2,32,1024]{2,1,0:T(8,128)(2,1)S(1)}, u32[]{:S(2)}, u32[]{:S(2)}) collective-permute-start(bf16[2,32,1024]{2,1,0:T(8,128)(2,1)S(1)} %get-tuple-element.55), channel_id=1, source_target_pairs={{0,24},{8,32},{16,40},{24,48},{28,4},{32,56},{36,12},{40,64},{44,2... | collective-permute-start | bytes 393224 | tf_op jit(solution)/shard_map/ppermute | solution.py:321
  16.3 12.8 %collective-permute-start.1 = (bf16[2,16,1024]{2,1,0:T(8,128)(2,1)S(1)}, bf16[2,16,1024]{2,1,0:T(8,128)(2,1)S(1)}, u32[]{:S(2)}, u32[]{:S(2)}) collective-permute-start(bf16[2,16,1024]{2,1,0:T(8,128)(2,1)S(1)} %get-tuple-element.56), channel_id=1, source_target_pairs={{0,48},{8,56},{16,64},{24,72},{32,80},{40,88},{48,96},{52,4},{56,1... | collective-permute-start | bytes 196616 | tf_op jit(solution)/shard_map/ppermute | solution.py:321
  25.3 2.3 %copy-start.3 = (bf16[240,256]{1,0:T(8,128)(2,1)S(1)}, bf16[240,256]{1,0:T(8,128)(2,1)}, u32[]{:S(2)}) copy-start(bf16[240,256]{1,0:T(8,128)(2,1)} %constant.39.clone.own_ref) | copy-start | bytes 368644
  27.6 1.5 %copy-start.6 = (bf16[64,48]{1,0:T(8,128)(2,1)S(1)}, bf16[64,48]{1,0:T(8,128)(2,1)}, u32[]{:S(2)}) copy-start(bf16[64,48]{1,0:T(8,128)(2,1)} %constant.40.clone.w_ref) | copy-start | bytes 18436
  29.1 9.8 %copy-start.10 = (bf16[32,4096]{1,0:T(8,128)(2,1)S(1)}, bf16[32,4096]{1,0:T(8,128)(2,1)}, u32[]{:S(2)}) copy-start(bf16[32,4096]{1,0:T(8,128)(2,1)} %param.16) | copy-start | bytes 786436
  29.3 20.8 %collective-permute-start.2 = (bf16[2,136,1024]{2,1,0:T(8,128)(2,1)S(1)}, bf16[2,136,1024]{2,1,0:T(8,128)(2,1)S(1)}, u32[]{:S(2)}, u32[]{:S(2)}) collective-permute-start(bf16[2,136,1024]{2,1,0:T(8,128)(2,1)S(1)} %get-tuple-element.64), channel_id=1, source_target_pairs={{0,8},{8,16},{12,4},{16,24},{20,12},{24,32},{28,20},{32,40},{36,28... | collective-permute-start | bytes 1671176 | tf_op jit(solution)/shard_map/ppermute | solution.py:321
  32.6 17.6 %collective-permute-start.3 = (bf16[2,72,1024]{2,1,0:T(8,128)(2,1)S(1)}, bf16[2,72,1024]{2,1,0:T(8,128)(2,1)S(1)}, u32[]{:S(2)}, u32[]{:S(2)}) collective-permute-start(bf16[2,72,1024]{2,1,0:T(8,128)(2,1)S(1)} %get-tuple-element.65), channel_id=1, source_target_pairs={{0,16},{8,24},{16,32},{20,4},{24,40},{28,12},{32,48},{36,20},{40,5... | collective-permute-start | bytes 884744 | tf_op jit(solution)/shard_map/ppermute | solution.py:321
  39.0 11.2 %copy-start = (bf16[128,1024]{1,0:T(8,128)(2,1)S(1)}, bf16[128,1024]{1,0:T(8,128)(2,1)}, u32[]{:S(2)}) copy-start(bf16[128,1024]{1,0:T(8,128)(2,1)} %q_ref.1) | copy-start | bytes 786436
  50.2 4.1 %copy-start.12 = (f32[2,640]{1,0:T(2,128)S(1)}, f32[2,640]{1,0:T(2,128)}, u32[]{:S(2)}) copy-start(f32[2,640]{1,0:T(2,128)} %constant.42.clone) | copy-start | bytes 15364
  50.2 6.0 %copy-start.2 = (bf16[256,192]{1,0:T(8,128)(2,1)S(1)}, bf16[256,192]{1,0:T(8,128)(2,1)}, u32[]{:S(2)}) copy-start(bf16[256,192]{1,0:T(8,128)(2,1)} %constant.44.clone.derive_t_ref) | copy-start | bytes 294916
  50.2 5.9 %copy-start.4 = (bf16[192,256]{1,0:T(8,128)(2,1)S(1)}, bf16[192,256]{1,0:T(8,128)(2,1)}, u32[]{:S(2)}) copy-start(bf16[192,256]{1,0:T(8,128)(2,1)} %constant.43.clone.derive_ref) | copy-start | bytes 294916
  50.2 5.9 %copy-start.5 = (bf16[128,64]{1,0:T(8,128)(2,1)S(1)}, bf16[128,64]{1,0:T(8,128)(2,1)}, u32[]{:S(2)}) copy-start(bf16[128,64]{1,0:T(8,128)(2,1)} %constant.45.clone.spread_ref) | copy-start | bytes 49156
  51.2 3.1 %copy-start.11 = (s32[2,640]{1,0:T(2,128)S(1)}, s32[2,640]{1,0:T(2,128)}, u32[]{:S(2)}) copy-start(s32[2,640]{1,0:T(2,128)} %constant.41.clone) | copy-start | bytes 15364
  51.2 5.0 %collective-permute-start.4 = (bf16[5,128,512]{2,1,0:T(8,128)(2,1)}, bf16[5,128,512]{2,1,0:T(8,128)(2,1)S(1)}, u32[]{:S(2)}, u32[]{:S(2)}) collective-permute-start(bf16[5,128,512]{2,1,0:T(8,128)(2,1)} %get-tuple-element.72), channel_id=1, source_target_pairs={{0,4},{4,0},{8,12},{12,8},{16,20},{20,16},{24,28},{28,24},{32,36},... | collective-permute-start | bytes 1966088 | tf_op jit(solution)/shard_map/ppermute | solution.py:324
  61.0 4.0 %collective-permute-start.5 = (bf16[5,128,512]{2,1,0:T(8,128)(2,1)S(1)}, bf16[5,128,512]{2,1,0:T(8,128)(2,1)S(1)}, u32[]{:S(2)}, u32[]{:S(2)}) collective-permute-start(bf16[5,128,512]{2,1,0:T(8,128)(2,1)S(1)} %get-tuple-element.74), channel_id=1, source_target_pairs={{0,4},{4,0},{8,12},{12,8},{16,20},{20,16},{24,28},{28,24},{32,36},... | collective-permute-start | bytes 1966088 | tf_op jit(solution)/shard_map/ppermute | solution.py:324
  65.1 18.1 %collective-permute-start.6 = (bf16[2,136,1024]{2,1,0:T(8,128)(2,1)S(1)}, bf16[2,136,1024]{2,1,0:T(8,128)(2,1)S(1)}, u32[]{:S(2)}, u32[]{:S(2)}) collective-permute-start(bf16[2,136,1024]{2,1,0:T(8,128)(2,1)S(1)} %get-tuple-element.78), channel_id=1, source_target_pairs={{4,12},{8,0},{12,20},{16,8},{20,28},{24,16},{28,36},{32,24},{36,44... | collective-permute-start | bytes 1671176 | tf_op jit(solution)/shard_map/ppermute | solution.py:321
  68.7 14.5 %collective-permute-start.7 = (bf16[2,72,1024]{2,1,0:T(8,128)(2,1)S(1)}, bf16[2,72,1024]{2,1,0:T(8,128)(2,1)S(1)}, u32[]{:S(2)}, u32[]{:S(2)}) collective-permute-start(bf16[2,72,1024]{2,1,0:T(8,128)(2,1)S(1)} %get-tuple-element.79), channel_id=1, source_target_pairs={{4,20},{12,28},{16,0},{20,36},{24,8},{28,44},{32,16},{36,52},{40,2... | collective-permute-start | bytes 884744 | tf_op jit(solution)/shard_map/ppermute | solution.py:321
  71.6 11.6 %copy-start.7 = (bf16[48,64]{1,0:T(8,128)(2,1)S(1)}, bf16[48,64]{1,0:T(8,128)(2,1)}, u32[]{:S(2)}) copy-start(bf16[48,64]{1,0:T(8,128)(2,1)} %constant.46.clone.w_ref) | copy-start | bytes 18436
  83.4 15.5 %collective-permute-start.8 = (bf16[2,32,1024]{2,1,0:T(8,128)(2,1)S(1)}, bf16[2,32,1024]{2,1,0:T(8,128)(2,1)S(1)}, u32[]{:S(2)}, u32[]{:S(2)}) collective-permute-start(bf16[2,32,1024]{2,1,0:T(8,128)(2,1)S(1)} %get-tuple-element.84), channel_id=1, source_target_pairs={{4,28},{12,36},{20,44},{24,0},{28,52},{32,8},{36,60},{40,16},{44,6... | collective-permute-start | bytes 393224 | tf_op jit(solution)/shard_map/ppermute | solution.py:321
  85.9 13.0 %copy-start.1 = (bf16[256,256]{1,0:T(8,128)(2,1)S(1)}, bf16[256,256]{1,0:T(8,128)(2,1)}, u32[]{:S(2)}) copy-start(bf16[256,256]{1,0:T(8,128)(2,1)} %constant.47.clone.w_ref) | copy-start | bytes 393220
  85.9 13.0 %collective-permute-start.9 = (bf16[2,16,1024]{2,1,0:T(8,128)(2,1)S(1)}, bf16[2,16,1024]{2,1,0:T(8,128)(2,1)S(1)}, u32[]{:S(2)}, u32[]{:S(2)}) collective-permute-start(bf16[2,16,1024]{2,1,0:T(8,128)(2,1)S(1)} %get-tuple-element.85), channel_id=1, source_target_pairs={{4,52},{12,60},{20,68},{28,76},{36,84},{44,92},{48,0},{52,100},{56... | collective-permute-start | bytes 196616 | tf_op jit(solution)/shard_map/ppermute | solution.py:321
  99.4 8.9 %collective-permute-start.10 = (bf16[2,128,1024]{2,1,0:T(8,128)(2,1)S(1)}, bf16[2,128,1024]{2,1,0:T(8,128)(2,1)S(1)}, u32[]{:S(2)}, u32[]{:S(2)}) collective-permute-start(bf16[2,128,1024]{2,1,0:T(8,128)(2,1)S(1)} %get-tuple-element.95), channel_id=1, source_target_pairs={{0,4},{4,0},{8,12},{12,8},{16,20},{20,16},{24,28},{28,24},{32,36},... | collective-permute-start | bytes 1572872 | tf_op jit(solution)/shard_map/ppermute | solution.py:324

commit v6 on v5

--- a/solution.py
+++ b/solution.py
@@ -147,7 +147,7 @@
     three = jnp.where(row == (col >> 3), 0.125, 0.0)
     pool = jnp.where(row - 16 == (col >> 4), 0.0625, three).astype(jnp.bfloat16)
     for part, ref in enumerate((k_ref, v_ref)):
-        out_ref[part] = _dot(pool, ref[...]).astype(jnp.bfloat16)
+        out_ref[part, :, _half(pl.program_id(0))] = _dot(pool, ref[...]).astype(jnp.bfloat16)
 
 
 def pack_far(core_ref, both_ref, three_ref, six_ref):
@@ -335,12 +335,12 @@
         return ((2, n, half), dtype)
 
     core_arg = core.reshape(1).astype(jnp.int32)
-    whole_block = pl.BlockSpec((BLOCK, width), lambda i: (0, 0))
+    half_block = pl.BlockSpec((BLOCK, half), lambda i: (0, i))
     mine = pl.pallas_call(
         pack_coarse,
         out_shape=jax.ShapeDtypeStruct(*full(32)),
-        grid=(1,),
-        in_specs=[whole_block] * 2,
+        grid=(2,),
+        in_specs=[half_block] * 2,
         out_specs=VMEM_SPEC,
         compiler_params=pltpu.CompilerParams(vmem_limit_bytes=FULL_VMEM),
     )(key_states, value_states)

time: 110 us -> 110 us (level)
  no operation moved by 1% of the time
where the time goes in v6:
time: 110 us; the launch traced here: 109 us
  starting transfers between devices  55.2 us (50%)
  blocking collectives  30.3 us (28%)
  waiting for transfers between devices  11.2 us (10%)
  Pallas kernels  10 us (9%)
    ppermute x8, starting transfers between devices, hop(): return lax.ppermute(x, 'seq', [(i, j) for i, j in pairs if 0 <= j < size])  42.5 us
    ppermute x3, starting transfers between devices, swap(): return lax.ppermute(x, 'seq', [(i, i ^ 1) for i in range(size)])  12.7 us
    all_to_all x1, blocking collectives, local(): lax.all_to_all(attended.reshape(2 * n_head, -1, half), ('seq', 'head'), 0...  11.3 us
    all_to_all x1, blocking collectives, local(): lax.all_to_all(split, ('seq', 'head'), 0, 0, axis_index_groups=chip_group...  11.2 us
    all_gather x3, blocking collectives, both_cores(): return lax.all_gather(x, 'seq', axis=0, axis_index_groups=chip_cores)  7.79 us
    ppermute x8, waiting for transfers between devices, hop(): return lax.ppermute(x, 'seq', [(i, j) for i, j in pairs if 0 <= j < size])  7.56 us
    pallas_call x1, Pallas kernels, local(): pl.pallas_call(attend, out_shape=[jax.ShapeDtypeStruct(s, d) for s, d in...  4.81 us
    ppermute x3, waiting for transfers between devices, swap(): return lax.ppermute(x, 'seq', [(i, i ^ 1) for i in range(size)])  3.6 us
  transfers between devices with their start and end apart: 11, of which 5 were waited for; matrix products, arithmetic and copies ran while one was open for 1% of the time, Pallas kernels for 0%

profile of v6, /device:TPU:49, one launch (start us, length us, event | category | flops | bytes accessed | tf_op | source)
XLA Modules:
  0.0 109.2 jit_solution(13806088588774757318)
XLA Ops:
  0.6 2.0 %shard_map.156 = bf16[2,32,1024]{2,1,0:T(8,128)(2,1)} custom-call(bf16[128,1024]{1,0:T(8,128)(2,1)} %k_ref.1, bf16[128,1024]{1,0:T(8,128)(2,1)} %v_ref.1), custom_call_target="tpu_custom_call" | custom-call | tf_op jit(solution)/shard_map/pallas_call | solution.py:339
  2.6 0.0 copy-start.8
  2.6 2.6 %all-gather = bf16[4,32,1024]{2,1,0:T(8,128)(2,1)S(1)} all-gather(bf16[2,32,1024]{2,1,0:T(8,128)(2,1)} %shard_map.156), channel_id=2, replica_groups={{0,4},{8,12},{16,20},{24,28},{32,36},{40,44},{48,52},{56,60},{64,68},{7..., dimensions={0}, use_global_device_ids=true | all-gather | bytes 393216 | tf_op jit(solution)/shard_map/all_gather | solution.py:327
  5.3 0.0 copy-start.9
  5.3 11.1 %collective-permute-start = (bf16[2,32,1024]{2,1,0:T(8,128)(2,1)S(1)}, bf16[2,32,1024]{2,1,0:T(8,128)(2,1)S(1)}, u32[]{:S(2)}, u32[]{:S(2)}) collective-permute-start(bf16[2,32,1024]{2,1,0:T(8,128)(2,1)S(1)} %get-tuple-element.55), channel_id=1, source_target_pairs={{0,24},{8,32},{16,40},{24,48},{28,4},{32,56},{36,12},{40,64},{44,2... | collective-permute-start | bytes 393224 | tf_op jit(solution)/shard_map/ppermute | solution.py:321
  16.4 6.1 %collective-permute-start.1 = (bf16[2,16,1024]{2,1,0:T(8,128)(2,1)S(1)}, bf16[2,16,1024]{2,1,0:T(8,128)(2,1)S(1)}, u32[]{:S(2)}, u32[]{:S(2)}) collective-permute-start(bf16[2,16,1024]{2,1,0:T(8,128)(2,1)S(1)} %get-tuple-element.56), channel_id=1, source_target_pairs={{0,48},{8,56},{16,64},{24,72},{32,80},{40,88},{48,96},{52,4},{56,1... | collective-permute-start | bytes 196616 | tf_op jit(solution)/shard_map/ppermute | solution.py:321
  22.5 0.0 copy-done.8
  22.5 2.9 %all-gather.1 = bf16[256,1024]{1,0:T(8,128)(2,1)S(1)} all-gather(bf16[128,1024]{1,0:T(8,128)(2,1)S(1)} %copy-done.8), channel_id=3, replica_groups={{0,4},{8,12},{16,20},{24,28},{32,36},{40,44},{48,52},{56,60},{64,68},{7..., dimensions={0}, use_global_device_ids=true | all-gather | bytes 786432 | tf_op jit(solution)/shard_map/all_gather | solution.py:327
  25.4 0.0 copy-done.9
  25.4 0.0 copy-start.3
  25.4 2.3 %all-gather.2 = bf16[256,1024]{1,0:T(8,128)(2,1)S(1)} all-gather(bf16[128,1024]{1,0:T(8,128)(2,1)S(1)} %copy-done.9), channel_id=4, replica_groups={{0,4},{8,12},{16,20},{24,28},{32,36},{40,44},{48,52},{56,60},{64,68},{7..., dimensions={0}, use_global_device_ids=true | all-gather | bytes 786432 | tf_op jit(solution)/shard_map/all_gather | solution.py:327
  27.7 0.0 copy-done.3
  27.7 0.0 copy-start.6
  27.7 0.5 shard_map.158
  28.2 1.0 collective-permute-done.1.six_ref
  29.2 0.0 collective-permute-done.three_ref
  29.2 0.0 copy-done.6
  29.2 0.0 copy-start.10
  29.2 0.2 shard_map.159
  29.4 3.3 %collective-permute-start.2 = (bf16[2,136,1024]{2,1,0:T(8,128)(2,1)S(1)}, bf16[2,136,1024]{2,1,0:T(8,128)(2,1)S(1)}, u32[]{:S(2)}, u32[]{:S(2)}) collective-permute-start(bf16[2,136,1024]{2,1,0:T(8,128)(2,1)S(1)} %get-tuple-element.64), channel_id=1, source_target_pairs={{0,8},{8,16},{12,4},{16,24},{20,12},{24,32},{28,20},{32,40},{36,28... | collective-permute-start | bytes 1671176 | tf_op jit(solution)/shard_map/ppermute | solution.py:321
  32.7 6.3 %collective-permute-start.3 = (bf16[2,72,1024]{2,1,0:T(8,128)(2,1)S(1)}, bf16[2,72,1024]{2,1,0:T(8,128)(2,1)S(1)}, u32[]{:S(2)}, u32[]{:S(2)}) collective-permute-start(bf16[2,72,1024]{2,1,0:T(8,128)(2,1)S(1)} %get-tuple-element.65), channel_id=1, source_target_pairs={{0,16},{8,24},{16,32},{20,4},{24,40},{28,12},{32,48},{36,20},{40,5... | collective-permute-start | bytes 884744 | tf_op jit(solution)/shard_map/ppermute | solution.py:321
  39.0 0.0 copy-done.10
  39.1 0.0 copy-start
  39.1 11.2 %all_to_all.10 = bf16[8,32,512]{2,1,0:T(8,128)(2,1)S(1)} all-to-all(bf16[8,32,512]{2,1,0:T(8,128)(2,1)S(1)} %bitcast.26), channel_id=1, replica_groups={{0,4,1,5,2,6,3,7},{8,12,9,13,10,14,11,15},{16,20,17,21,18,22,19,23},{24..., dimensions={0} | all-to-all | bytes 524288 | tf_op jit(solution)/shard_map/all_to_all | solution.py:361
  50.2 0.0 collective-permute-done.3.two_ref
  50.3 0.0 collective-permute-done.2.one_ref
  50.3 0.0 copy-done
  50.3 0.0 copy-start.12
  50.3 0.0 copy-start.2
  50.3 0.0 copy-start.4
  50.3 0.0 copy-start.5
  50.3 0.9 shard_map.160
  51.2 0.0 copy-start.11
  51.2 3.1 %collective-permute-start.4 = (bf16[5,128,512]{2,1,0:T(8,128)(2,1)}, bf16[5,128,512]{2,1,0:T(8,128)(2,1)S(1)}, u32[]{:S(2)}, u32[]{:S(2)}) collective-permute-start(bf16[5,128,512]{2,1,0:T(8,128)(2,1)} %get-tuple-element.72), channel_id=1, source_target_pairs={{0,4},{4,0},{8,12},{12,8},{16,20},{20,16},{24,28},{28,24},{32,36},... | collective-permute-start | bytes 1966088 | tf_op jit(solution)/shard_map/ppermute | solution.py:324
  54.3 0.0 copy-done.12
  54.3 0.0 copy-done.11
  54.4 1.9 %collective-permute-done.4.y_ref = bf16[5,128,512]{2,1,0:T(8,128)(2,1)S(1)} collective-permute-done((bf16[5,128,512]{2,1,0:T(8,128)(2,1)}, bf16[5,128,512]{2,1,0:T(8,128)(2,1)S(1)}, u32[]{:S(2)}, u32[]{:S(2)}) %collective-permute-start.4) | collective-permute-done | bytes 655392 | tf_op jit(solution)/shard_map/ppermute | solution.py:324
  56.2 0.0 copy-done.2
  56.2 0.0 copy-done.4
  56.2 0.0 copy-done.5
  56.2 4.8 %shard_map.161 = (bf16[256,512]{1,0:T(8,128)(2,1)S(1)}, bf16[128,512]{1,0:T(8,128)(2,1)S(1)}, f32[2,128,512]{2,1,0:T(8,128)S(1)}, f32[2,128,512]{2,1,0:T(8,128)S...) custom-call(s32[1]{0:T(128)} %bitcast.core_ref, bf16[2,128,1024]{2,1,0:T(8,128)(2,1)S(1)} %bitcast.19, ...), custom_call_target="tpu_custom_call" | custom-call | tf_op jit(solution)/shard_map/pallas_call | solution.py:379
  61.1 2.3 %collective-permute-start.5 = (bf16[5,128,512]{2,1,0:T(8,128)(2,1)S(1)}, bf16[5,128,512]{2,1,0:T(8,128)(2,1)S(1)}, u32[]{:S(2)}, u32[]{:S(2)}) collective-permute-start(bf16[5,128,512]{2,1,0:T(8,128)(2,1)S(1)} %get-tuple-element.74), channel_id=1, source_target_pairs={{0,4},{4,0},{8,12},{12,8},{16,20},{20,16},{24,28},{28,24},{32,36},... | collective-permute-start | bytes 1966088 | tf_op jit(solution)/shard_map/ppermute | solution.py:324
  63.4 1.7 %collective-permute-done.5.take_ref = bf16[5,128,512]{2,1,0:T(8,128)(2,1)S(1)} collective-permute-done((bf16[5,128,512]{2,1,0:T(8,128)(2,1)S(1)}, bf16[5,128,512]{2,1,0:T(8,128)(2,1)S(1)}, u32[]{:S(2)}, u32[]{:S(2)}) %collective-permute-start.5) | collective-permute-done | bytes 655392 | tf_op jit(solution)/shard_map/ppermute | solution.py:324
  65.1 0.1 shard_map.162
  65.2 3.6 %collective-permute-start.6 = (bf16[2,136,1024]{2,1,0:T(8,128)(2,1)S(1)}, bf16[2,136,1024]{2,1,0:T(8,128)(2,1)S(1)}, u32[]{:S(2)}, u32[]{:S(2)}) collective-permute-start(bf16[2,136,1024]{2,1,0:T(8,128)(2,1)S(1)} %get-tuple-element.78), channel_id=1, source_target_pairs={{4,12},{8,0},{12,20},{16,8},{20,28},{24,16},{28,36},{32,24},{36,44... | collective-permute-start | bytes 1671176 | tf_op jit(solution)/shard_map/ppermute | solution.py:321
  68.8 2.9 %collective-permute-start.7 = (bf16[2,72,1024]{2,1,0:T(8,128)(2,1)S(1)}, bf16[2,72,1024]{2,1,0:T(8,128)(2,1)S(1)}, u32[]{:S(2)}, u32[]{:S(2)}) collective-permute-start(bf16[2,72,1024]{2,1,0:T(8,128)(2,1)S(1)} %get-tuple-element.79), channel_id=1, source_target_pairs={{4,20},{12,28},{16,0},{20,36},{24,8},{28,44},{32,16},{36,52},{40,2... | collective-permute-start | bytes 884744 | tf_op jit(solution)/shard_map/ppermute | solution.py:321
  71.7 0.0 copy-start.7
  71.7 11.3 %all_to_all.11 = bf16[8,32,512]{2,1,0:T(8,128)(2,1)S(1)} all-to-all(bf16[8,32,512]{2,1,0:T(8,128)(2,1)S(1)} %bitcast.24), channel_id=1, replica_groups={{0,4,1,5,2,6,3,7},{8,12,9,13,10,14,11,15},{16,20,17,21,18,22,19,23},{24..., dimensions={0} | all-to-all | bytes 524288 | tf_op jit(solution)/shard_map/all_to_all | solution.py:397
  83.1 0.2 collective-permute-done.7.two_ref
  83.3 0.0 collective-permute-done.6.one_ref
  83.3 0.0 copy-done.7
  83.3 0.2 shard_map.163
  83.5 2.5 %collective-permute-start.8 = (bf16[2,32,1024]{2,1,0:T(8,128)(2,1)S(1)}, bf16[2,32,1024]{2,1,0:T(8,128)(2,1)S(1)}, u32[]{:S(2)}, u32[]{:S(2)}) collective-permute-start(bf16[2,32,1024]{2,1,0:T(8,128)(2,1)S(1)} %get-tuple-element.84), channel_id=1, source_target_pairs={{4,28},{12,36},{20,44},{24,0},{28,52},{32,8},{36,60},{40,16},{44,6... | collective-permute-start | bytes 393224 | tf_op jit(solution)/shard_map/ppermute | solution.py:321
  86.0 0.0 copy-start.1
  86.0 6.7 %collective-permute-start.9 = (bf16[2,16,1024]{2,1,0:T(8,128)(2,1)S(1)}, bf16[2,16,1024]{2,1,0:T(8,128)(2,1)S(1)}, u32[]{:S(2)}, u32[]{:S(2)}) collective-permute-start(bf16[2,16,1024]{2,1,0:T(8,128)(2,1)S(1)} %get-tuple-element.85), channel_id=1, source_target_pairs={{4,52},{12,60},{20,68},{28,76},{36,84},{44,92},{48,0},{52,100},{56... | collective-permute-start | bytes 196616 | tf_op jit(solution)/shard_map/ppermute | solution.py:321
  92.7 6.3 %collective-permute-done.9.six_ref = bf16[2,16,1024]{2,1,0:T(8,128)(2,1)S(1)} collective-permute-done((bf16[2,16,1024]{2,1,0:T(8,128)(2,1)S(1)}, bf16[2,16,1024]{2,1,0:T(8,128)(2,1)S(1)}, u32[]{:S(2)}, u32[]{:S(2)}) %collective-permute-start.9) | collective-permute-done | bytes 65568 | tf_op jit(solution)/shard_map/ppermute | solution.py:321
  99.0 0.0 collective-permute-done.8.three_ref
  99.0 0.0 copy-done.1
  99.0 0.5 shard_map.164
  99.5 7.3 %collective-permute-start.10 = (bf16[2,128,1024]{2,1,0:T(8,128)(2,1)S(1)}, bf16[2,128,1024]{2,1,0:T(8,128)(2,1)S(1)}, u32[]{:S(2)}, u32[]{:S(2)}) collective-permute-start(bf16[2,128,1024]{2,1,0:T(8,128)(2,1)S(1)} %get-tuple-element.95), channel_id=1, source_target_pairs={{0,4},{4,0},{8,12},{12,8},{16,20},{20,16},{24,28},{28,24},{32,36},... | collective-permute-start | bytes 1572872 | tf_op jit(solution)/shard_map/ppermute | solution.py:324
  106.9 0.7 copy.22
  107.6 0.7 pad_maximum_fusion
  108.3 0.0 collective-permute-done.10.take_ref
  108.4 0.9 shard_map.165
  (5 shorter events, 0.1 us)
Async XLA Ops:
  2.6 19.9 %copy-start.8 = (bf16[128,1024]{1,0:T(8,128)(2,1)S(1)}, bf16[128,1024]{1,0:T(8,128)(2,1)}, u32[]{:S(2)}) copy-start(bf16[128,1024]{1,0:T(8,128)(2,1)} %k_ref.1) | copy-start | bytes 786436
  5.3 20.1 %copy-start.9 = (bf16[128,1024]{1,0:T(8,128)(2,1)S(1)}, bf16[128,1024]{1,0:T(8,128)(2,1)}, u32[]{:S(2)}) copy-start(bf16[128,1024]{1,0:T(8,128)(2,1)} %v_ref.1) | copy-start | bytes 786436
  5.3 23.9 %collective-permute-start = (bf16[2,32,1024]{2,1,0:T(8,128)(2,1)S(1)}, bf16[2,32,1024]{2,1,0:T(8,128)(2,1)S(1)}, u32[]{:S(2)}, u32[]{:S(2)}) collective-permute-start(bf16[2,32,1024]{2,1,0:T(8,128)(2,1)S(1)} %get-tuple-element.55), channel_id=1, source_target_pairs={{0,24},{8,32},{16,40},{24,48},{28,4},{32,56},{36,12},{40,64},{44,2... | collective-permute-start | bytes 393224 | tf_op jit(solution)/shard_map/ppermute | solution.py:321
  16.4 12.8 %collective-permute-start.1 = (bf16[2,16,1024]{2,1,0:T(8,128)(2,1)S(1)}, bf16[2,16,1024]{2,1,0:T(8,128)(2,1)S(1)}, u32[]{:S(2)}, u32[]{:S(2)}) collective-permute-start(bf16[2,16,1024]{2,1,0:T(8,128)(2,1)S(1)} %get-tuple-element.56), channel_id=1, source_target_pairs={{0,48},{8,56},{16,64},{24,72},{32,80},{40,88},{48,96},{52,4},{56,1... | collective-permute-start | bytes 196616 | tf_op jit(solution)/shard_map/ppermute | solution.py:321
  25.4 2.3 %copy-start.3 = (bf16[240,256]{1,0:T(8,128)(2,1)S(1)}, bf16[240,256]{1,0:T(8,128)(2,1)}, u32[]{:S(2)}) copy-start(bf16[240,256]{1,0:T(8,128)(2,1)} %constant.39.clone.own_ref) | copy-start | bytes 368644
  27.7 1.5 %copy-start.6 = (bf16[64,48]{1,0:T(8,128)(2,1)S(1)}, bf16[64,48]{1,0:T(8,128)(2,1)}, u32[]{:S(2)}) copy-start(bf16[64,48]{1,0:T(8,128)(2,1)} %constant.40.clone.w_ref) | copy-start | bytes 18436
  29.2 9.8 %copy-start.10 = (bf16[32,4096]{1,0:T(8,128)(2,1)S(1)}, bf16[32,4096]{1,0:T(8,128)(2,1)}, u32[]{:S(2)}) copy-start(bf16[32,4096]{1,0:T(8,128)(2,1)} %param.16) | copy-start | bytes 786436
  29.4 20.8 %collective-permute-start.2 = (bf16[2,136,1024]{2,1,0:T(8,128)(2,1)S(1)}, bf16[2,136,1024]{2,1,0:T(8,128)(2,1)S(1)}, u32[]{:S(2)}, u32[]{:S(2)}) collective-permute-start(bf16[2,136,1024]{2,1,0:T(8,128)(2,1)S(1)} %get-tuple-element.64), channel_id=1, source_target_pairs={{0,8},{8,16},{12,4},{16,24},{20,12},{24,32},{28,20},{32,40},{36,28... | collective-permute-start | bytes 1671176 | tf_op jit(solution)/shard_map/ppermute | solution.py:321
  32.7 17.6 %collective-permute-start.3 = (bf16[2,72,1024]{2,1,0:T(8,128)(2,1)S(1)}, bf16[2,72,1024]{2,1,0:T(8,128)(2,1)S(1)}, u32[]{:S(2)}, u32[]{:S(2)}) collective-permute-start(bf16[2,72,1024]{2,1,0:T(8,128)(2,1)S(1)} %get-tuple-element.65), channel_id=1, source_target_pairs={{0,16},{8,24},{16,32},{20,4},{24,40},{28,12},{32,48},{36,20},{40,5... | collective-permute-start | bytes 884744 | tf_op jit(solution)/shard_map/ppermute | solution.py:321
  39.1 11.2 %copy-start = (bf16[128,1024]{1,0:T(8,128)(2,1)S(1)}, bf16[128,1024]{1,0:T(8,128)(2,1)}, u32[]{:S(2)}) copy-start(bf16[128,1024]{1,0:T(8,128)(2,1)} %q_ref.1) | copy-start | bytes 786436
  50.3 4.1 %copy-start.12 = (f32[2,640]{1,0:T(2,128)S(1)}, f32[2,640]{1,0:T(2,128)}, u32[]{:S(2)}) copy-start(f32[2,640]{1,0:T(2,128)} %constant.42.clone) | copy-start | bytes 15364
  50.3 6.0 %copy-start.2 = (bf16[256,192]{1,0:T(8,128)(2,1)S(1)}, bf16[256,192]{1,0:T(8,128)(2,1)}, u32[]{:S(2)}) copy-start(bf16[256,192]{1,0:T(8,128)(2,1)} %constant.44.clone.derive_t_ref) | copy-start | bytes 294916
  50.3 5.9 %copy-start.4 = (bf16[192,256]{1,0:T(8,128)(2,1)S(1)}, bf16[192,256]{1,0:T(8,128)(2,1)}, u32[]{:S(2)}) copy-start(bf16[192,256]{1,0:T(8,128)(2,1)} %constant.43.clone.derive_ref) | copy-start | bytes 294916
  50.3 5.9 %copy-start.5 = (bf16[128,64]{1,0:T(8,128)(2,1)S(1)}, bf16[128,64]{1,0:T(8,128)(2,1)}, u32[]{:S(2)}) copy-start(bf16[128,64]{1,0:T(8,128)(2,1)} %constant.45.clone.spread_ref) | copy-start | bytes 49156
  51.2 3.1 %copy-start.11 = (s32[2,640]{1,0:T(2,128)S(1)}, s32[2,640]{1,0:T(2,128)}, u32[]{:S(2)}) copy-start(s32[2,640]{1,0:T(2,128)} %constant.41.clone) | copy-start | bytes 15364
  51.2 5.0 %collective-permute-start.4 = (bf16[5,128,512]{2,1,0:T(8,128)(2,1)}, bf16[5,128,512]{2,1,0:T(8,128)(2,1)S(1)}, u32[]{:S(2)}, u32[]{:S(2)}) collective-permute-start(bf16[5,128,512]{2,1,0:T(8,128)(2,1)} %get-tuple-element.72), channel_id=1, source_target_pairs={{0,4},{4,0},{8,12},{12,8},{16,20},{20,16},{24,28},{28,24},{32,36},... | collective-permute-start | bytes 1966088 | tf_op jit(solution)/shard_map/ppermute | solution.py:324
  61.1 4.0 %collective-permute-start.5 = (bf16[5,128,512]{2,1,0:T(8,128)(2,1)S(1)}, bf16[5,128,512]{2,1,0:T(8,128)(2,1)S(1)}, u32[]{:S(2)}, u32[]{:S(2)}) collective-permute-start(bf16[5,128,512]{2,1,0:T(8,128)(2,1)S(1)} %get-tuple-element.74), channel_id=1, source_target_pairs={{0,4},{4,0},{8,12},{12,8},{16,20},{20,16},{24,28},{28,24},{32,36},... | collective-permute-start | bytes 1966088 | tf_op jit(solution)/shard_map/ppermute | solution.py:324
  65.2 18.1 %collective-permute-start.6 = (bf16[2,136,1024]{2,1,0:T(8,128)(2,1)S(1)}, bf16[2,136,1024]{2,1,0:T(8,128)(2,1)S(1)}, u32[]{:S(2)}, u32[]{:S(2)}) collective-permute-start(bf16[2,136,1024]{2,1,0:T(8,128)(2,1)S(1)} %get-tuple-element.78), channel_id=1, source_target_pairs={{4,12},{8,0},{12,20},{16,8},{20,28},{24,16},{28,36},{32,24},{36,44... | collective-permute-start | bytes 1671176 | tf_op jit(solution)/shard_map/ppermute | solution.py:321
  68.8 14.5 %collective-permute-start.7 = (bf16[2,72,1024]{2,1,0:T(8,128)(2,1)S(1)}, bf16[2,72,1024]{2,1,0:T(8,128)(2,1)S(1)}, u32[]{:S(2)}, u32[]{:S(2)}) collective-permute-start(bf16[2,72,1024]{2,1,0:T(8,128)(2,1)S(1)} %get-tuple-element.79), channel_id=1, source_target_pairs={{4,20},{12,28},{16,0},{20,36},{24,8},{28,44},{32,16},{36,52},{40,2... | collective-permute-start | bytes 884744 | tf_op jit(solution)/shard_map/ppermute | solution.py:321
  71.7 11.6 %copy-start.7 = (bf16[48,64]{1,0:T(8,128)(2,1)S(1)}, bf16[48,64]{1,0:T(8,128)(2,1)}, u32[]{:S(2)}) copy-start(bf16[48,64]{1,0:T(8,128)(2,1)} %constant.46.clone.w_ref) | copy-start | bytes 18436
  83.5 15.5 %collective-permute-start.8 = (bf16[2,32,1024]{2,1,0:T(8,128)(2,1)S(1)}, bf16[2,32,1024]{2,1,0:T(8,128)(2,1)S(1)}, u32[]{:S(2)}, u32[]{:S(2)}) collective-permute-start(bf16[2,32,1024]{2,1,0:T(8,128)(2,1)S(1)} %get-tuple-element.84), channel_id=1, source_target_pairs={{4,28},{12,36},{20,44},{24,0},{28,52},{32,8},{36,60},{40,16},{44,6... | collective-permute-start | bytes 393224 | tf_op jit(solution)/shard_map/ppermute | solution.py:321
  86.0 13.0 %copy-start.1 = (bf16[256,256]{1,0:T(8,128)(2,1)S(1)}, bf16[256,256]{1,0:T(8,128)(2,1)}, u32[]{:S(2)}) copy-start(bf16[256,256]{1,0:T(8,128)(2,1)} %constant.47.clone.w_ref) | copy-start | bytes 393220
  86.0 13.0 %collective-permute-start.9 = (bf16[2,16,1024]{2,1,0:T(8,128)(2,1)S(1)}, bf16[2,16,1024]{2,1,0:T(8,128)(2,1)S(1)}, u32[]{:S(2)}, u32[]{:S(2)}) collective-permute-start(bf16[2,16,1024]{2,1,0:T(8,128)(2,1)S(1)} %get-tuple-element.85), channel_id=1, source_target_pairs={{4,52},{12,60},{20,68},{28,76},{36,84},{44,92},{48,0},{52,100},{56... | collective-permute-start | bytes 196616 | tf_op jit(solution)/shard_map/ppermute | solution.py:321
  99.5 8.9 %collective-permute-start.10 = (bf16[2,128,1024]{2,1,0:T(8,128)(2,1)S(1)}, bf16[2,128,1024]{2,1,0:T(8,128)(2,1)S(1)}, u32[]{:S(2)}, u32[]{:S(2)}) collective-permute-start(bf16[2,128,1024]{2,1,0:T(8,128)(2,1)S(1)} %get-tuple-element.95), channel_id=1, source_target_pairs={{0,4},{4,0},{8,12},{12,8},{16,20},{20,16},{24,28},{28,24},{32,36},... | collective-permute-start | bytes 1572872 | tf_op jit(solution)/shard_map/ppermute | solution.py:324
